TPU v7x, 32 devices: a whole 2x2x4 slice. The times are simulated.
32 devices in a mesh: expert: 8 (over y, x, core), wshard: 4 (over z).
Axes of the slice: x: 2, y: 2, z: 4, core: 2. Of those that a mesh axis runs over, the one named last changes fastest.
Arguments:
- tokens: bfloat16 [4096, 2048], P(('expert', 'wshard')), may hold values from -6 to 6
- attention_norm: float32 [2048], P(('expert', 'wshard')), may hold values from 0.5 to 1.5
- query_weight: float32 [2048, 3072], P(('expert', 'wshard')), may hold values from -0.1875 to 0.1875
- latent_down: float32 [2048, 576], P(('expert', 'wshard')), may hold values from -0.125 to 0.125
- latent_norm: float32 [512], P(('expert', 'wshard')), may hold values from 0.5 to 1.5
- latent_up: float32 [512, 4096], P(('expert', 'wshard')), may hold values from -0.25 to 0.25
- output_weight: float32 [2048, 2048], P(('expert', 'wshard')), may hold values from -1 to 1
- post_norm: float32 [2048], P(('expert', 'wshard')), may hold values from 0.5 to 1.5
- shared_gate: float32 [2048, 2816], P(('expert', 'wshard')), may hold values from -0.125 to 0.125
- shared_up: float32 [2048, 2816], P(('expert', 'wshard')), may hold values from -0.125 to 0.125
- shared_down: float32 [2816, 2048], P(('expert', 'wshard')), may hold values from -0.109375 to 0.109375
- router_weight: float32 [2048, 16], P(('expert', 'wshard')), may hold values from -0.0625 to 0.0625
- expert_gate: bfloat16 [16, 2048, 1408], P('expert', None, 'wshard'), may hold values from -0.125 to 0.125
- expert_up: bfloat16 [16, 2048, 1408], P('expert', None, 'wshard'), may hold values from -0.125 to 0.125
- expert_down: bfloat16 [16, 1408, 2048], P('expert', 'wshard'), may hold values from -1 to 1
- image_piece_index: int32 [4096], P(('expert', 'wshard')), may hold values from 0 to 16, as said below
- routes: int32 [4096, 6], P(('expert', 'wshard')), may hold values from 0 to 15, all different within a row
- cotangent: bfloat16 [4096, 2048], P(('expert', 'wshard')), may hold values from -6 to 6
Outputs:
- layer_out: bfloat16 [4096, 2048], P(('expert', 'wshard'))
- tokens_grad: float32 [4096, 2048], P(('expert', 'wshard'))
- attention_norm_grad: float32 [2048], P(('expert', 'wshard'))
- query_weight_grad: float32 [2048, 3072], P(('expert', 'wshard'))
- latent_down_grad: float32 [2048, 576], P(('expert', 'wshard'))
- latent_norm_grad: float32 [512], P(('expert', 'wshard'))
- latent_up_grad: float32 [512, 4096], P(('expert', 'wshard'))
- output_weight_grad: float32 [2048, 2048], P(('expert', 'wshard'))
- post_norm_grad: float32 [2048], P(('expert', 'wshard'))
- shared_gate_grad: float32 [2048, 2816], P(('expert', 'wshard'))
- shared_up_grad: float32 [2048, 2816], P(('expert', 'wshard'))
- shared_down_grad: float32 [2816, 2048], P(('expert', 'wshard'))
- router_weight_grad: float32 [2048, 16], P(('expert', 'wshard'))
- expert_gate_grad: float32 [16, 2048, 1408], P('expert', None, 'wshard')
- expert_up_grad: float32 [16, 2048, 1408], P('expert', None, 'wshard')
- expert_down_grad: float32 [16, 1408, 2048], P('expert', 'wshard')
Inputs may be any that keep to these rules, and one draw needn't show every extreme that they name: `image_piece_index`: tokens come in aligned blocks of 256; all tokens of a block carry the same id, 0 for text or 1 + the block's index among all tokens for an image piece; the last block is an image piece. `routes`: each row names 6 different experts.
All inputs are finite; a program needn't handle non-finite values.
Results may differ from a plain program's by a relative error of at most 0.022.
Values may be sent and summed in bfloat16 or wider, within the bound.
No kernel may reach another device: no remote copies, remote signals or barrier semaphores. Data moves between devices by JAX's collectives and lax.ppermute only.
A program may use at most 576 MiB of HBM per device.

v0:
```python
import functools

import jax
import jax.numpy as jnp
from jax import lax
from jax.experimental import pallas as pl
from jax.experimental.pallas import tpu as pltpu
from jax.sharding import Mesh, PartitionSpec as P

D = 2048
H = 16
DN = 128
DR = 64
DV = 128
KVR = 512
TOPK = 6
PIECE = 256
EPSILON = 1e-06
ROPE_BASE = 10000.0
NEGATIVE = -1e30
BF = jnp.bfloat16
F32 = jnp.float32
EVERY = ("c", "k", "z")
COLUMN = ("k", "z")


def swap(block, axis, distance):
    n = lax.axis_size(axis)
    return lax.ppermute(block, axis, [(i, i ^ distance) for i in range(n)])


def lanes(n):
    return -(-n // 128) * 128


def widen(block, extra):
    room = lanes(extra.shape[1]) - extra.shape[1]
    return jnp.concatenate([block, jnp.pad(extra.astype(BF), ((0, 0), (0, room)))], axis=1)


def dot(a, b, dims):
    return lax.dot_general(a, b, (dims, ((), ())), preferred_element_type=F32)


def mm(a, b):
    return dot(a, b, ((1,), (0,)))


def mm_nt(a, b):
    return dot(a, b, ((1,), (1,)))


def mm_tn(a, b):
    return dot(a, b, ((0,), (0,)))


def gather_column(unit):
    z_size = lax.axis_size("z")
    mine = jnp.concatenate([unit] + [swap(unit, "z", d) for d in range(1, z_size)], axis=0)
    return mine


def gather_every(unit):
    mine = gather_column(unit)
    groups = [mine] + [swap(mine, "c", d) for d in range(1, lax.axis_size("c"))]
    return [(g, swap(g, "k", 1)) for g in groups]


def scatter_column(part, rows):
    z_size = lax.axis_size("z")
    half = z_size * rows
    summed = part[:half].astype(F32) + swap(part[half:].astype(BF), "k", 1).astype(F32)
    return scatter_z(summed, rows)


def scatter_z(summed, rows):
    total = summed[:rows]
    for d in range(1, lax.axis_size("z")):
        total = total + swap(summed[d * rows : (d + 1) * rows].astype(BF), "z", d).astype(F32)
    return total


def scatter_every(parts, rows):
    total = None
    half = lax.axis_size("z") * rows
    for d in reversed(range(len(parts))):
        part = parts[d]
        summed = part[:half].astype(F32) + swap(part[half:].astype(BF), "k", 1).astype(F32)
        if d:
            summed = swap(summed.astype(BF), "c", d).astype(F32)
        total = summed if total is None else total + summed
    return scatter_z(total, rows)


def pick(array, index):
    return lax.dynamic_index_in_dim(array, index, axis=0, keepdims=False)


def scatter_weight(part):
    c_size, k_size, z_size = (lax.axis_size(a) for a in EVERY)
    c, k, z = (lax.axis_index(a) for a in EVERY)
    rows = part.shape[0] // (c_size * k_size * z_size)
    n = part.shape[1]
    grid = part.reshape(c_size, k_size, z_size * rows, n)
    away = lax.dynamic_index_in_dim(grid, k ^ 1, axis=1, keepdims=False).astype(BF)
    kept = lax.dynamic_index_in_dim(grid, k, axis=1, keepdims=False).astype(F32)
    summed = kept + swap(away, "k", 1).astype(F32)
    total = pick(summed, c)
    for d in range(1, c_size):
        total = total + swap(pick(summed, c ^ d).astype(BF), "c", d).astype(F32)
    total = total.reshape(z_size, rows, n)
    out = pick(total, z)
    for d in range(1, z_size):
        out = out + swap(pick(total, z ^ d).astype(BF), "z", d).astype(F32)
    return out


def rms_parts(values):
    return lax.rsqrt(jnp.mean(values * values, axis=-1, keepdims=True) + EPSILON)


def rms_back(values, scale, gain, grad):
    weighted = grad * gain
    inner = jnp.mean(weighted * values, axis=-1, keepdims=True)
    return scale * (weighted - values * (scale * scale * inner)), grad * values * scale


def rotate(values, cosine, sine, sign):
    half = values.shape[-1] // 2
    a, b = values[..., :half], values[..., half:]
    return jnp.concatenate([a * cosine - sign * b * sine, b * cosine + sign * a * sine], axis=-1)


def expert_kernel(
    local_experts,
    capacity,
    rows,
    experts,
    first,
    place_ref,
    sec_a,
    sec_b,
    cot_a,
    cot_b,
    gate_hbm,
    up_hbm,
    down_hbm,
    sin_hbm,
    sdn_hbm,
    *rest,
):
    rest = rest if first else rest[5:]
    (x_out, c_out, aw_out, gg_out, ug_out, out_out, in_out, sg_out, sd_out) = rest[:9]
    (sec_v, cot_v, gate_v, up_v, down_v, sin_v, sdn_v, x_v, c_v, y_v, z_v, aw_v, gg_v, ug_v) = rest[9:23]
    (choose_v, prob_v, sact_v, slow_v, sgp_v, sdp_v, sem_in, sem_out) = rest[23:31]
    half = sec_a.shape[0]
    blocks = 2 * half // rows
    per = blocks * capacity
    wpad = sdn_v.shape[0]
    base = place_ref[1] * per

    def copy(src, dst, sem, i):
        made = pltpu.make_async_copy(src, dst, sem.at[i])
        made.start()
        return made

    in_sec = [
        copy(sec_a, sec_v.at[pl.ds(0, half)], sem_in, 0),
        copy(sec_b, sec_v.at[pl.ds(half, half)], sem_in, 1),
    ]
    in_cot = [
        copy(cot_a, cot_v.at[pl.ds(0, half)], sem_in, 2),
        copy(cot_b, cot_v.at[pl.ds(half, half)], sem_in, 3),
    ]
    in_gate = copy(gate_hbm, gate_v, sem_in, 4)
    in_up = copy(up_hbm, up_v, sem_in, 5)
    in_down = copy(down_hbm, down_v, sem_in, 6)
    in_sin = copy(sin_hbm, sin_v, sem_in, 7)
    in_sdn = copy(sdn_hbm, sdn_v, sem_in, 8)
    for one in in_cot:
        one.wait()

    first_expert = place_ref[0]
    tail = cot_v.shape[1] - D
    row_i = lax.broadcasted_iota(jnp.int32, (rows, rows), 0)
    col_i = lax.broadcasted_iota(jnp.int32, (rows, rows), 1)
    earlier = (col_i < row_i).astype(BF)
    lane = lax.broadcasted_iota(jnp.int32, (rows, tail), 1)
    slot = lax.broadcasted_iota(jnp.int32, (rows, local_experts * capacity), 1).astype(F32)
    for one in in_sec:
        one.wait()
    sec_tail = sec_v.shape[1] - D
    tail_lane = lax.broadcasted_iota(jnp.int32, (capacity, sec_tail), 1)

    def gather(b, carry):
        at = pl.ds(pl.multiple_of(b * rows, rows), rows)
        named = cot_v[at, D:]
        rank = mm(earlier, named)
        code = jnp.where((named.astype(F32) > 0) & (rank < capacity), rank, -1e6)
        chosen = jnp.zeros(slot.shape, F32)
        for e in range(local_experts):
            own = jnp.sum(jnp.where(lane == first_expert + e, code, 0.0), axis=1, keepdims=True)
            chosen = jnp.where(own + e * capacity == slot, 1.0, chosen)
        choose = chosen.astype(BF)
        choose_v[at, :] = choose
        picked = mm_tn(choose, sec_v[at, :])
        cots = mm_tn(choose, cot_v[at, :D])
        for e in range(local_experts):
            mine = slice(e * capacity, (e + 1) * capacity)
            to = pl.ds(pl.multiple_of(e * per + b * capacity, capacity), capacity)
            x_v[to, :] = picked[mine, :D].astype(BF)
            c_v[to, :] = cots[mine].astype(BF)
            which = first_expert + e
            hits = (tail_lane == which) | (tail_lane == which + experts)
            prob = jnp.sum(jnp.where(hits, picked[mine, D:], 0.0), axis=1, keepdims=True)
            prob_v[to, :] = jnp.broadcast_to(prob, (capacity, 128))
        return carry

    lax.fori_loop(0, blocks, gather, 0)
    outs = []
    for e in range(local_experts):
        mine = pl.ds(e * per, per)
        outs.append(copy(x_v.at[mine], x_out.at[e, pl.ds(base, per)], sem_out, 2 * e))
        outs.append(copy(c_v.at[mine], c_out.at[e, pl.ds(base, per)], sem_out, 2 * e + 1))
    used = 2 * local_experts

    in_sin.wait()
    in_sdn.wait()
    shared = mm(sec_v[:, :D], sin_v[...])
    s_gate, s_up = shared[:, :wpad], shared[:, wpad:]
    s_sigma = jax.nn.sigmoid(s_gate)
    s_silu = s_gate * s_sigma
    s_grad = mm_nt(cot_v[:, :D], sdn_v[...])
    sact_v[...] = (s_silu * s_up).astype(BF)
    slow_v[:, :wpad] = (s_grad * s_up * (s_sigma * (1.0 + s_gate * (1.0 - s_sigma)))).astype(BF)
    slow_v[:, wpad:] = (s_grad * s_silu).astype(BF)
    sgp_v[...] = mm_tn(slow_v[...], sec_v[:, :D])
    sdp_v[...] = mm_tn(sact_v[...], cot_v[:, :D])
    outs.append(copy(sgp_v, sg_out, sem_out, used))
    outs.append(copy(sdp_v, sd_out, sem_out, used + 1))
    used += 2

    in_gate.wait()
    in_up.wait()
    in_down.wait()
    in_tail = z_v.shape[2] - D
    pair_lane = lax.broadcasted_iota(jnp.int32, (per, in_tail), 1)
    for e in range(local_experts):
        mine = pl.ds(e * per, per)
        x_e, c_e = x_v[mine, :], c_v[mine, :]
        gate = mm(x_e, gate_v[e])
        up = mm(x_e, up_v[e])
        pull = mm_nt(c_e, down_v[e])
        prob = prob_v[mine, :1]
        sigma = jax.nn.sigmoid(gate)
        silu = gate * sigma
        act = silu * up
        pair = jnp.sum(pull * act, axis=1, keepdims=True)
        pull = pull * prob
        gg_v[e] = (pull * up * (sigma * (1.0 + gate * (1.0 - sigma)))).astype(BF)
        ug_v[e] = (pull * silu).astype(BF)
        aw_v[e] = (act * prob).astype(BF)
        outs.append(copy(aw_v.at[e], aw_out.at[e, pl.ds(base, per)], sem_out, used))
        outs.append(copy(gg_v.at[e], gg_out.at[e, pl.ds(base, per)], sem_out, used + 1))
        outs.append(copy(ug_v.at[e], ug_out.at[e, pl.ds(base, per)], sem_out, used + 2))
        used += 3
        y = mm(aw_v[e], down_v[e]).astype(BF)
        y_v[:, e * capacity : (e + 1) * capacity, :] = y.reshape(blocks, capacity, D)
        zed = (mm_nt(gg_v[e], gate_v[e]) + mm_nt(ug_v[e], up_v[e])).astype(BF)
        z_v[:, e * capacity : (e + 1) * capacity, :D] = zed.reshape(blocks, capacity, D)
        pairs = jnp.where(pair_lane == first_expert + e, pair, 0.0).astype(BF)
        z_v[:, e * capacity : (e + 1) * capacity, D:] = pairs.reshape(blocks, capacity, in_tail)

    def scatter(b, carry):
        at = pl.ds(pl.multiple_of(b * rows, rows), rows)
        choose = choose_v[at, :]
        cot_v[at, :D] = (mm(choose, y_v[b]) + mm(sact_v[at, :], sdn_v[...])).astype(BF)
        back = mm(choose, z_v[b])
        sec_v[at, :D] = (back[:, :D] + mm_nt(slow_v[at, :], sin_v[...])).astype(BF)
        sec_v[at, D:] = back[:, D:].astype(BF)
        return carry

    lax.fori_loop(0, blocks, scatter, 0)
    outs.append(copy(sec_v, in_out, sem_out, used))
    outs.append(copy(cot_v.at[:, pl.ds(0, D)], out_out, sem_out, used + 1))
    for one in outs:
        one.wait()


def expert_group(place, sec, cot, weights, kept, capacity, rows, experts, groups):
    gate, up, down, sin, sdn = weights
    local_experts, _, hidden = gate.shape
    half = sec[0].shape[0]
    tokens = 2 * half
    blocks = tokens // rows
    per = blocks * capacity
    slots = per * groups
    wpad = sdn.shape[0]
    in_width = D + lanes(experts)
    big = (local_experts, slots)
    shapes = [
        jax.ShapeDtypeStruct((*big, D), BF),
        jax.ShapeDtypeStruct((*big, D), BF),
        jax.ShapeDtypeStruct((*big, hidden), BF),
        jax.ShapeDtypeStruct((*big, hidden), BF),
        jax.ShapeDtypeStruct((*big, hidden), BF),
        jax.ShapeDtypeStruct((tokens, D), BF),
        jax.ShapeDtypeStruct((tokens, in_width), BF),
        jax.ShapeDtypeStruct((2 * wpad, D), F32),
        jax.ShapeDtypeStruct((wpad, D), F32),
    ]
    first = kept is None
    operands = [place, *sec, *cot, gate, up, down, sin, sdn] + ([] if first else list(kept))
    any_space = pl.BlockSpec(memory_space=pl.ANY)
    smem = pl.BlockSpec(memory_space=pltpu.SMEM)
    flops = 2 * tokens * D * (6 * wpad + 8 * local_experts * capacity) + 12 * local_experts * per * D * hidden
    return pl.pallas_call(
        functools.partial(expert_kernel, local_experts, capacity, rows, experts, first),
        out_shape=shapes,
        in_specs=[smem] + [any_space] * (len(operands) - 1),
        out_specs=[any_space] * len(shapes),
        scratch_shapes=[
            pltpu.VMEM((tokens, sec[0].shape[1]), BF),
            pltpu.VMEM((tokens, cot[0].shape[1]), BF),
            pltpu.VMEM(gate.shape, BF),
            pltpu.VMEM(up.shape, BF),
            pltpu.VMEM(down.shape, BF),
            pltpu.VMEM(sin.shape, BF),
            pltpu.VMEM(sdn.shape, BF),
            pltpu.VMEM((local_experts * per, D), BF),
            pltpu.VMEM((local_experts * per, D), BF),
            pltpu.VMEM((blocks, local_experts * capacity, D), BF),
            pltpu.VMEM((blocks, local_experts * capacity, in_width), BF),
            pltpu.VMEM((local_experts, per, hidden), BF),
            pltpu.VMEM((local_experts, per, hidden), BF),
            pltpu.VMEM((local_experts, per, hidden), BF),
            pltpu.VMEM((tokens, local_experts * capacity), BF),
            pltpu.VMEM((local_experts * per, 128), F32),
            pltpu.VMEM((tokens, wpad), BF),
            pltpu.VMEM((tokens, 2 * wpad), BF),
            pltpu.VMEM((2 * wpad, D), F32),
            pltpu.VMEM((wpad, D), F32),
            pltpu.SemaphoreType.DMA((9,)),
            pltpu.SemaphoreType.DMA((5 * local_experts + 4,)),
        ],
        input_output_aliases={} if first else {10 + i: i for i in range(5)},
        compiler_params=pltpu.CompilerParams(vmem_limit_bytes=63 * 1024 * 1024),
        cost_estimate=pl.CostEstimate(flops=flops, bytes_accessed=38 << 20, transcendentals=0),
    )(*operands)


def on_device(
    tokens,
    attention_norm,
    query_weight,
    latent_down,
    latent_norm,
    latent_up,
    output_weight,
    post_norm,
    shared_gate,
    shared_up,
    shared_down,
    router_weight,
    expert_gate,
    expert_up,
    expert_down,
    image_piece_index,
    routes,
    cotangent,
):
    rows = tokens.shape[0]
    c_size, k_size, z_size = (lax.axis_size(a) for a in EVERY)
    c, k, z = (lax.axis_index(a) for a in EVERY)
    column_size = k_size * z_size
    device_count = c_size * column_size
    local_experts = expert_gate.shape[0]
    experts = router_weight.shape[1]
    capacity = rows * TOPK * 4 // (3 * experts)
    length = column_size * rows
    heads = H // column_size
    width = shared_down.shape[0]
    score_scale = (DN + DR) ** (-0.5)
    weight_rows = query_weight.shape[0]
    up_rows = latent_up.shape[0]

    expert_ids = jnp.arange(experts, dtype=jnp.int32)
    named = jnp.any(routes[:, :, None] == expert_ids[None, None, :], axis=1)
    flag = (image_piece_index > 0).astype(BF)[:, None]
    mine = gather_column(widen(tokens, flag))
    sequence = jnp.concatenate([mine, swap(mine, "k", 1)], axis=0)
    cot_groups = gather_every(widen(cotangent, named))

    small = jnp.concatenate(
        [
            latent_down,
            router_weight,
            attention_norm[:, None],
            post_norm[:, None],
            jnp.pad(latent_norm, (0, weight_rows - latent_norm.shape[0]))[:, None],
        ],
        axis=1,
    ).astype(BF)
    small_width = small.shape[1]
    small = jnp.pad(small, ((0, 0), (0, lanes(small_width) - small_width)))
    full_small = lax.all_gather(small, EVERY, axis=0, tiled=True)
    down_width = KVR + DR
    full_down = full_small[:, :down_width]
    full_router = full_small[:, down_width : down_width + experts]
    attn_gain = full_small[:, down_width + experts].astype(F32)
    post_gain = full_small[:, down_width + experts + 1].astype(F32)
    latent_gain = (
        full_small[:, down_width + experts + 2]
        .reshape(device_count, weight_rows)[:, : latent_norm.shape[0]]
        .reshape(KVR)
        .astype(F32)
    )
    q_width = heads * (DN + DR)
    kv_width = heads * (DN + DV)
    q_out = query_weight.astype(BF).reshape(weight_rows, column_size, q_width).transpose(1, 0, 2)
    q_out = jnp.pad(q_out, ((0, 0), (0, 0), (0, kv_width - q_width)))
    up_out = latent_up.astype(BF).reshape(up_rows, column_size, kv_width).transpose(1, 0, 2)
    head_pack = jnp.concatenate([q_out, up_out], axis=1)
    head_pack = lax.all_to_all(head_pack, COLUMN, split_axis=0, concat_axis=0, tiled=True)
    head_pack = lax.all_gather(head_pack, "c", axis=0, tiled=False)
    head_query = head_pack[:, :, :weight_rows, :q_width].reshape(D, q_width)
    head_up = head_pack[:, :, weight_rows:].reshape(KVR, kv_width)
    full_out = lax.all_gather(output_weight.astype(BF), EVERY, axis=0, tiled=True)
    shared_pack = jnp.concatenate(
        [
            shared_gate.astype(BF).reshape(weight_rows, device_count, width),
            shared_up.astype(BF).reshape(weight_rows, device_count, width),
        ],
        axis=2,
    ).transpose(1, 0, 2)
    shared_in = lax.all_to_all(shared_pack, EVERY, split_axis=0, concat_axis=0, tiled=True)
    shared_in = shared_in.reshape(D, 2 * width)
    room = ((0, 0), (0, lanes(width) - width))
    shared_in = jnp.concatenate(
        [jnp.pad(shared_in[:, :width], room), jnp.pad(shared_in[:, width:], room)], axis=1
    )
    shared_low = shared_down.astype(BF)

    step = jnp.arange(rows, dtype=jnp.int32)
    places = jnp.concatenate(
        [
            ((k ^ dk) * z_size + (z ^ dz)) * rows + step
            for dk in range(k_size)
            for dz in range(z_size)
        ]
    )
    image = sequence[:, D] > 0
    allowed = (places[None, :] <= places[:, None]) | (
        (places[None, :] // PIECE == places[:, None] // PIECE) & image[:, None]
    )
    frequency = ROPE_BASE ** (-2.0 * jnp.arange(DR // 2, dtype=F32) / DR)
    angles = places.astype(F32)[:, None] * frequency[None, :]
    cosine, sine = jnp.cos(angles), jnp.sin(angles)

    values = sequence[:, :D].astype(F32)
    first_scale = rms_parts(values)
    first_low = (values * first_scale * attn_gain).astype(BF)
    query_raw = mm(first_low, head_query).reshape(length, heads, DN + DR)
    down_raw = mm(first_low, full_down)
    query_nope = query_raw[..., :DN].astype(BF)
    query_rope = rotate(query_raw[..., DN:], cosine[:, None], sine[:, None], 1.0).astype(BF)
    latent_raw = down_raw[:, :KVR]
    latent_scale = rms_parts(latent_raw)
    latent_low = (latent_raw * latent_scale * latent_gain).astype(BF)
    key_rope = rotate(down_raw[:, KVR:], cosine, sine, 1.0).astype(BF)
    expanded = mm(latent_low, head_up).astype(BF).reshape(length, heads, DN + DV)
    key_nope = expanded[..., :DN]
    value_rows = expanded[..., DN:]
    scores = jnp.einsum("thd,uhd->htu", query_nope, key_nope, preferred_element_type=F32)
    scores = scores + jnp.einsum("thd,ud->htu", query_rope, key_rope, preferred_element_type=F32)
    scores = jnp.where(allowed[None], scores * score_scale, NEGATIVE)
    weights_attn = jax.nn.softmax(scores, axis=-1)
    probs_low = weights_attn.astype(BF)
    heads_out = jnp.einsum("htu,uhd->thd", probs_low, value_rows, preferred_element_type=F32)
    heads_out = heads_out.astype(BF).reshape(length, heads * DV)

    def place_order(array):
        blocks = array.reshape(k_size, z_size, rows, array.shape[1])
        return jnp.concatenate(
            [
                lax.dynamic_slice(
                    blocks, (k ^ (j // z_size), z ^ (j % z_size), 0, 0), (1, 1, rows, array.shape[1])
                ).reshape(rows, array.shape[1])
                for j in range(column_size)
            ],
            axis=0,
        )

    def own_order(array):
        return place_order(array)

    def heads_to_tokens(array):
        moved = lax.all_to_all(
            place_order(array).reshape(column_size, rows, array.shape[1]),
            COLUMN,
            split_axis=0,
            concat_axis=0,
            tiled=True,
        )
        return moved.transpose(1, 0, 2).reshape(rows, column_size * array.shape[1])

    def tokens_to_heads(array):
        n = array.shape[1] // column_size
        moved = lax.all_to_all(
            array.reshape(rows, column_size, n).transpose(1, 0, 2),
            COLUMN,
            split_axis=0,
            concat_axis=0,
            tiled=True,
        )
        return own_order(moved.reshape(length, n))

    heads_low = heads_to_tokens(heads_out)
    residual = tokens.astype(F32) + mm(heads_low, full_out)
    second_scale = rms_parts(residual)
    second_low = (residual * second_scale * post_gain).astype(BF)
    router_probs = jax.nn.softmax(mm(second_low, full_router), axis=-1)

    probs_high = router_probs.astype(BF)
    probs_rest = (router_probs - probs_high.astype(F32)).astype(BF)
    second_groups = gather_every(
        widen(second_low, jnp.concatenate([probs_high, probs_rest], axis=1))
    )
    wpad = lanes(width)
    place = jnp.stack([(c * k_size + k) * local_experts, jnp.zeros((), jnp.int32)]).astype(jnp.int32)
    shared_rows = jnp.pad(shared_low, ((0, wpad - width), (0, 0)))
    weights = (expert_gate, expert_up, expert_down, shared_in, shared_rows)
    kept, out_parts, in_parts, sg_parts, sd_parts = None, [], [], [], []
    for d in range(c_size):
        results = expert_group(
            place.at[1].set(d), second_groups[d], cot_groups[d], weights, kept, capacity, rows, experts, c_size
        )
        kept = results[:5]
        out_parts.append(results[5])
        in_parts.append(results[6])
        sg_parts.append(results[7])
        sd_parts.append(results[8])
    expert_in, cot_in, act_weighted, gate_grad, up_grad = kept
    ein = lambda spec, a, b: jnp.einsum(spec, a, b, preferred_element_type=F32)
    expert_down_grad = ein("esf,esd->efd", act_weighted, cot_in)
    expert_gate_grad = ein("esd,esf->edf", expert_in, gate_grad)
    expert_up_grad = ein("esd,esf->edf", expert_in, up_grad)
    shared_in_grad = sum(sg_parts[1:], sg_parts[0])
    shared_in_grad = jnp.concatenate(
        [shared_in_grad[:width], shared_in_grad[wpad : wpad + width]], axis=0
    ).astype(BF)
    shared_down_grad = sum(sd_parts[1:], sd_parts[0])[:width]

    second_sum = scatter_every(in_parts, rows)
    out_sum = scatter_every(out_parts, rows)
    layer_out = (residual + out_sum).astype(BF)

    probs_grad = second_sum[:, D : D + experts]
    logits_grad = (
        router_probs * (probs_grad - jnp.sum(router_probs * probs_grad, axis=-1, keepdims=True))
    ).astype(BF)
    router_grad = mm_tn(second_low, logits_grad)
    second_grad = second_sum[:, :D] + mm_nt(logits_grad, full_router)
    norm_part, post_terms = rms_back(residual, second_scale, post_gain, second_grad)
    residual_grad = cotangent.astype(F32) + norm_part
    attn_grad_low = residual_grad.astype(BF)
    output_grad = mm_tn(heads_low, attn_grad_low)
    heads_grad = tokens_to_heads(mm_nt(attn_grad_low, full_out).astype(BF))
    heads_grad = heads_grad.reshape(length, heads, DV)

    value_grad = ein("htu,thd->uhd", probs_low, heads_grad)
    dprob = ein("thd,uhd->htu", heads_grad, value_rows)
    score_grad = (
        weights_attn * (dprob - jnp.sum(weights_attn * dprob, axis=-1, keepdims=True))
    ).astype(BF)
    query_nope_grad = ein("htu,uhd->thd", score_grad, key_nope) * score_scale
    query_rope_grad = ein("htu,ud->thd", score_grad, key_rope) * score_scale
    key_nope_grad = ein("htu,thd->uhd", score_grad, query_nope) * score_scale
    key_rope_grad = ein("htu,thd->ud", score_grad, query_rope) * score_scale
    expanded_grad = jnp.concatenate([key_nope_grad, value_grad], axis=-1)
    expanded_grad = expanded_grad.reshape(length, kv_width).astype(BF)
    head_up_grad = mm_tn(latent_low, expanded_grad)
    latent_part = mm_nt(expanded_grad, head_up)
    latent_part = jnp.concatenate(
        [latent_part, key_rope_grad, jnp.zeros((length, lanes(down_width) - down_width), F32)], axis=1
    )
    latent_sum = scatter_column(latent_part, rows)
    latent_raw_grad, latent_terms = rms_back(
        latent_raw[:rows], latent_scale[:rows], latent_gain, latent_sum[:, :KVR]
    )
    rope_raw_grad = rotate(latent_sum[:, KVR:down_width], cosine[:rows], sine[:rows], -1.0)
    down_grad_low = jnp.concatenate([latent_raw_grad, rope_raw_grad], axis=-1).astype(BF)
    query_rope_raw = rotate(query_rope_grad, cosine[:, None], sine[:, None], -1.0)
    query_grad_low = jnp.concatenate([query_nope_grad, query_rope_raw], axis=-1)
    query_grad_low = query_grad_low.reshape(length, q_width).astype(BF)
    head_query_grad = mm_tn(first_low, query_grad_low)
    latent_down_grad = mm_tn(first_low[:rows], down_grad_low)
    first_part = mm_nt(query_grad_low, head_query)
    first_own = mm_nt(down_grad_low, full_down)
    first_grad = scatter_column(first_part, rows) + first_own
    first_norm_grad, attn_terms = rms_back(values[:rows], first_scale[:rows], attn_gain, first_grad)
    tokens_grad = residual_grad + first_norm_grad

    small_grad = jnp.concatenate(
        [
            latent_down_grad,
            router_grad,
            jnp.sum(attn_terms, axis=0)[:, None],
            jnp.sum(post_terms, axis=0)[:, None],
            jnp.pad(
                jnp.sum(latent_terms, axis=0).reshape(device_count, latent_norm.shape[0]),
                ((0, 0), (0, weight_rows - latent_norm.shape[0])),
            ).reshape(D, 1),
            jnp.zeros((D, lanes(small_width) - small_width), F32),
        ],
        axis=1,
    )
    own_small = scatter_weight(small_grad)
    own_output = scatter_weight(output_grad)
    head_grad = jnp.concatenate(
        [
            jnp.pad(
                head_query_grad.reshape(c_size, column_size, weight_rows, q_width),
                ((0, 0), (0, 0), (0, 0), (0, kv_width - q_width)),
            ),
            head_up_grad.reshape(c_size, column_size, up_rows, kv_width),
        ],
        axis=2,
    )
    head_sum = pick(head_grad, c)
    for d in range(1, c_size):
        head_sum = head_sum + swap(pick(head_grad, c ^ d).astype(BF), "c", d).astype(F32)
    head_sum = lax.all_to_all(head_sum.astype(BF), COLUMN, split_axis=0, concat_axis=0, tiled=True)
    own_query = head_sum[:, :weight_rows, :q_width].transpose(1, 0, 2).reshape(weight_rows, -1)
    own_up = head_sum[:, weight_rows:].transpose(1, 0, 2).reshape(up_rows, -1)
    shared_back = lax.all_to_all(
        shared_in_grad.reshape(2 * width, device_count, weight_rows).transpose(1, 2, 0),
        EVERY,
        split_axis=0,
        concat_axis=0,
        tiled=True,
    ).transpose(1, 0, 2)
    own_gate = shared_back[:, :, :width].reshape(weight_rows, -1)
    own_shared_up = shared_back[:, :, width:].reshape(weight_rows, -1)
    return (
        layer_out,
        tokens_grad,
        own_small[:, down_width + experts],
        own_query.astype(F32),
        own_small[:, :down_width],
        own_small[: latent_norm.shape[0], down_width + experts + 2],
        own_up.astype(F32),
        own_output,
        own_small[:, down_width + experts + 1],
        own_gate.astype(F32),
        own_shared_up.astype(F32),
        shared_down_grad,
        own_small[:, down_width : down_width + experts],
        expert_gate_grad,
        expert_up_grad,
        expert_down_grad,
    )


def solution(mesh):
    expert_size, z_size = mesh.devices.shape
    fine = Mesh(mesh.devices.reshape(expert_size // 2, 2, z_size), EVERY)
    row, flat = P(EVERY, None), P(EVERY)
    wide, tall = P(("c", "k"), None, "z"), P(("c", "k"), "z", None)
    return jax.shard_map(
        on_device,
        mesh=fine,
        in_specs=(row, flat, row, row, flat, row, row, flat, row, row, row, row)
        + (wide, wide, tall, flat, row, row),
        out_specs=(row, row, flat, row, row, flat, row, row, flat, row, row, row, row)
        + (wide, wide, tall),
        check_vma=False,
    )
```

profile of v0, /device:TPU:0, one launch (start us, length us, event | category | flops | bytes accessed | tf_op | source)
XLA Modules:
  0.0 1295.1 jit_solution(13835030292679981420)
XLA Ops:
  14.8 25.9 %all_to_all.30 = bf16[8,80,512]{2,1,0:T(8,128)(2,1)} all-to-all(bf16[8,80,512]{2,1,0:T(8,128)(2,1)S(1)} %copy.499), channel_id=1, replica_groups=mesh['c'=4,'k'=2,'z'=4] {'k','z'}, dimensions={0} | all-to-all | bytes 1310720 | tf_op jit(solution)/shard_map/all_to_all | solution.py:424
  47.0 25.5 %collective-permute-done = bf16[128,2176]{1,0:T(8,128)(2,1)S(1)} collective-permute-done((bf16[128,2176]{1,0:T(8,128)(2,1)S(1)}, bf16[128,2176]{1,0:T(8,128)(2,1)S(1)}, u32[]{:S(2)}, u32[]{:S(2)}) %collective-permute-start) | collective-permute-done | bytes 557088 | tf_op jit(solution)/shard_map/ppermute | solution.py:29
  72.5 16.2 %collective-permute-done.1 = bf16[128,2176]{1,0:T(8,128)(2,1)S(1)} collective-permute-done((bf16[128,2176]{1,0:T(8,128)(2,1)S(1)}, bf16[128,2176]{1,0:T(8,128)(2,1)S(1)}, u32[]{:S(2)}, u32[]{:S(2)}) %collective-permute-start.1) | collective-permute-done | bytes 557088 | tf_op jit(solution)/shard_map/ppermute | solution.py:29
  118.8 20.4 %all-gather.9.cloned.1.call-done = bf16[32,80,512]{2,1,0:T(8,128)(2,1)} async-done(((bf16[8,80,512]{2,1,0:T(8,128)(2,1)}), bf16[32,80,512]{2,1,0:T(8,128)(2,1)}) %all-gather.9.cloned.1.call-update) | async-done | bytes 2621456 | tf_op jit(solution)/shard_map/all_gather | solution.py:425
  159.7 8.2 fusion.35
  185.9 32.2 %all-to-all-done.1 = bf16[8,128,256]{2,1,0:T(8,128)(2,1)S(1)} async-done(((bf16[8,128,256]{2,1,0:T(8,128)(2,1)}), bf16[8,128,256]{2,1,0:T(8,128)(2,1)S(1)}, u32[]{:S(2)}, u32[]{:S(2)}) %all-to-all-start.1) | async-done | bytes 524320 | tf_op jit(solution)/shard_map/all_to_all | solution.py:498
  218.4 37.2 %all-gather.7.cloned.1.call-done = bf16[2048,2048]{1,0:T(8,128)(2,1)} async-done(((bf16[64,2048]{1,0:T(8,128)(2,1)}), bf16[2048,2048]{1,0:T(8,128)(2,1)}) %all-gather.7.cloned.1.call-update) | async-done | bytes 8388624 | tf_op jit(solution)/shard_map/all_gather | solution.py:428
  284.1 31.8 %collective-permute-done.5 = bf16[128,2176]{1,0:T(8,128)(2,1)} collective-permute-done((bf16[128,2176]{1,0:T(8,128)(2,1)}, bf16[128,2176]{1,0:T(8,128)(2,1)}, u32[]{:S(2)}, u32[]{:S(2)}) %collective-permute-start.5) | collective-permute-done | bytes 557088 | tf_op jit(solution)/shard_map/ppermute | solution.py:29
  339.8 91.1 %all-to-all-done.2 = bf16[32,64,176]{2,1,0:T(8,128)(2,1)S(1)} async-done(((bf16[32,64,176]{2,1,0:T(8,128)(2,1)}), bf16[32,64,176]{2,1,0:T(8,128)(2,1)S(1)}, u32[]{:S(2)}, u32[]{:S(2)}) %all-to-all-start.2) | async-done | bytes 720928 | tf_op jit(solution)/shard_map/all_to_all | solution.py:436
  451.2 35.1 %collective-permute-done.14.sec_a = bf16[512,2176]{1,0:T(8,128)(2,1)} collective-permute-done((bf16[512,2176]{1,0:T(8,128)(2,1)}, bf16[512,2176]{1,0:T(8,128)(2,1)}, u32[]{:S(2)}, u32[]{:S(2)}) %collective-permute-start.14) | collective-permute-done | bytes 2228256 | tf_op jit(solution)/shard_map/ppermute | solution.py:29
  486.2 39.0 %shard_map.297 = (bf16[2,2048,2048]{2,1,0:T(8,128)(2,1)}, bf16[2,2048,2048]{2,1,0:T(8,128)(2,1)}, bf16[2,2048,352]{2,1,0:T(8,128)(2,1)}, bf16[2,2048,352]{2,1,0:...) custom-call(s32[2]{0:T(128)} %copy-done.100, ...), custom_call_target="tpu_custom_call" | custom-call | flops 16374562816 | bytes 39845888 | tf_op jit(solution)/shard_map/pallas_call | solution.py:317
  531.1 38.5 %shard_map.298 = (bf16[2,2048,2048]{2,1,0:T(8,128)(2,1)}, bf16[2,2048,2048]{2,1,0:T(8,128)(2,1)}, bf16[2,2048,352]{2,1,0:T(8,128)(2,1)}, bf16[2,2048,352]{2,1,0:...) custom-call(s32[2]{0:T(128)} %copy-done.93, ...), custom_call_target="tpu_custom_call", output_to_operand_aliasing={{0}: (10, {}), {1}: (11, {}), {2}: (12, {}), {3}: (13, {}),... | custom-call | flops 16374562816 | bytes 39845888 | tf_op jit(solution)/shard_map/pallas_call | solution.py:317
  572.9 38.9 %shard_map.299 = (bf16[2,2048,2048]{2,1,0:T(8,128)(2,1)}, bf16[2,2048,2048]{2,1,0:T(8,128)(2,1)}, bf16[2,2048,352]{2,1,0:T(8,128)(2,1)}, bf16[2,2048,352]{2,1,0:...) custom-call(s32[2]{0:T(128)} %copy-done.92, ...), custom_call_target="tpu_custom_call", output_to_operand_aliasing={{0}: (10, {}), {1}: (11, {}), {2}: (12, {}), {3}: (13, {}),... | custom-call | flops 16374562816 | bytes 39845888 | tf_op jit(solution)/shard_map/pallas_call | solution.py:317
  615.4 38.6 %shard_map.300 = (bf16[2,2048,2048]{2,1,0:T(8,128)(2,1)}, bf16[2,2048,2048]{2,1,0:T(8,128)(2,1)}, bf16[2,2048,352]{2,1,0:T(8,128)(2,1)}, bf16[2,2048,352]{2,1,0:...) custom-call(s32[2]{0:T(128)} %copy-done.91, ...), custom_call_target="tpu_custom_call", output_to_operand_aliasing={{0}: (10, {}), {1}: (11, {}), {2}: (12, {}), {3}: (13, {}),... | custom-call | flops 16374562816 | bytes 39845888 | tf_op jit(solution)/shard_map/pallas_call | solution.py:317
  659.9 12.7 fusion.130
  672.6 12.7 fusion.131
  685.3 12.9 fusion.132
  736.7 28.4 %collective-permute-done.39 = bf16[512,2176]{1,0:T(8,128)(2,1)S(1)} collective-permute-done((bf16[512,2176]{1,0:T(8,128)(2,1)}, bf16[512,2176]{1,0:T(8,128)(2,1)S(1)}, u32[]{:S(2)}, u32[]{:S(2)}) %collective-permute-start.39) | collective-permute-done | bytes 2228256 | tf_op jit(solution)/shard_map/ppermute | solution.py:29
  766.6 51.4 %collective-permute-done.37 = bf16[512,2176]{1,0:T(8,128)(2,1)} collective-permute-done((bf16[512,2176]{1,0:T(8,128)(2,1)}, bf16[512,2176]{1,0:T(8,128)(2,1)}, u32[]{:S(2)}, u32[]{:S(2)}) %collective-permute-start.37) | collective-permute-done | bytes 2228256 | tf_op jit(solution)/shard_map/ppermute | solution.py:29
  826.1 24.2 %collective-permute-start.42 = (bf16[128,2176]{1,0:T(8,128)(2,1)S(1)}, bf16[128,2176]{1,0:T(8,128)(2,1)}, u32[]{:S(2)}, u32[]{:S(2)}) collective-permute-start(bf16[128,2176]{1,0:T(8,128)(2,1)S(1)} %get-tuple-element.295), channel_id=1, source_target_pairs={{0,2},{1,3},{2,0},{3,1},{4,6},{5,7},{6,4},{7,5},{8,10},{9,11},{10,... | collective-permute-start | bytes 1671176 | tf_op jit(solution)/shard_map/ppermute | solution.py:29
  857.9 23.2 %collective-permute-start.41 = (bf16[128,2176]{1,0:T(8,128)(2,1)S(1)}, bf16[128,2176]{1,0:T(8,128)(2,1)}, u32[]{:S(2)}, u32[]{:S(2)}) collective-permute-start(bf16[128,2176]{1,0:T(8,128)(2,1)S(1)} %get-tuple-element.293), channel_id=1, source_target_pairs={{0,1},{1,0},{2,3},{3,2},{4,5},{5,4},{6,7},{7,6},{8,9},{9,8},{10,11... | collective-permute-start | bytes 1671176 | tf_op jit(solution)/shard_map/ppermute | solution.py:29
  881.1 25.6 %collective-permute-done.27 = bf16[512,2048]{1,0:T(8,128)(2,1)} collective-permute-done((bf16[512,2048]{1,0:T(8,128)(2,1)}, bf16[512,2048]{1,0:T(8,128)(2,1)}, u32[]{:S(2)}, u32[]{:S(2)}) %collective-permute-start.27) | collective-permute-done | bytes 2097184 | tf_op jit(solution)/shard_map/ppermute | solution.py:29
  913.5 23.4 %collective-permute-start.32 = (bf16[128,2048]{1,0:T(8,128)(2,1)S(1)}, bf16[128,2048]{1,0:T(8,128)(2,1)S(1)}, u32[]{:S(2)}, u32[]{:S(2)}) collective-permute-start(bf16[128,2048]{1,0:T(8,128)(2,1)S(1)} %get-tuple-element.304), channel_id=1, source_target_pairs={{0,2},{1,3},{2,0},{3,1},{4,6},{5,7},{6,4},{7,5},{8,10},{9,11},{10,... | collective-permute-start | bytes 1572872 | tf_op jit(solution)/shard_map/ppermute | solution.py:29
  941.1 29.0 %collective-permute-done.32 = bf16[128,2048]{1,0:T(8,128)(2,1)S(1)} collective-permute-done((bf16[128,2048]{1,0:T(8,128)(2,1)S(1)}, bf16[128,2048]{1,0:T(8,128)(2,1)S(1)}, u32[]{:S(2)}, u32[]{:S(2)}) %collective-permute-start.32) | collective-permute-done | bytes 524320 | tf_op jit(solution)/shard_map/ppermute | solution.py:29
  1003.2 9.3 fusion.32
  1053.9 10.4 collective-permute-done.61
  1067.9 9.7 collective-permute-done.60
  1128.9 26.3 %collective-permute-done.46 = bf16[128,2048]{1,0:T(8,128)(2,1)} collective-permute-done((bf16[128,2048]{1,0:T(8,128)(2,1)}, bf16[128,2048]{1,0:T(8,128)(2,1)}, u32[]{:S(2)}, u32[]{:S(2)}) %collective-permute-start.46) | collective-permute-done | bytes 524320 | tf_op jit(solution)/shard_map/ppermute | solution.py:29
  1162.4 8.7 concatenate.185
  1206.2 47.5 %collective-permute-done.54 = bf16[256,640]{1,0:T(8,128)(2,1)S(1)} collective-permute-done((bf16[256,640]{1,0:T(8,128)(2,1)S(1)}, bf16[256,640]{1,0:T(8,128)(2,1)S(1)}, u32[]{:S(2)}, u32[]{:S(2)}) %collective-permute-start.54) | collective-permute-done | bytes 327712 | tf_op jit(solution)/shard_map/ppermute | solution.py:29
  1263.7 10.3 collective-permute-done.57
  1276.2 10.0 collective-permute-done.67
  (620 shorter events, 424.3 us)
Async XLA Ops:
  7.2 99.4 %all-gather.5.cloned.1.call-start = ((), (), s32[]{:S(2)}) async-start(), calls=%async_computation.6 | async-start | bytes 2703360 | tf_op jit(solution)/shard_map/all_gather | solution.py:406
  12.1 127.2 %all-gather.9.cloned.1.call-start = ((), (), s32[]{:S(2)}) async-start(), calls=%async_computation.8 | async-start | bytes 3276800 | tf_op jit(solution)/shard_map/all_gather | solution.py:425
  40.7 214.9 %all-gather.7.cloned.1.call-start = ((), (), s32[]{:S(2)}) async-start(), calls=%async_computation.7 | async-start | bytes 8650752 | tf_op jit(solution)/shard_map/all_gather | solution.py:428
  181.5 84.5 %collective-permute-start.11 = (bf16[128,2176]{1,0:T(8,128)(2,1)}, bf16[128,2176]{1,0:T(8,128)(2,1)S(1)}, u32[]{:S(2)}, u32[]{:S(2)}) collective-permute-start(bf16[128,2176]{1,0:T(8,128)(2,1)} %pad_maximum_fusion.7), channel_id=1, source_target_pairs={{0,3},{1,2},{2,1},{3,0},{4,7},{5,6},{6,5},{7,4},{8,11},{9,10},{10,... | collective-permute-start | bytes 1671176 | tf_op jit(solution)/shard_map/ppermute | solution.py:29
  185.3 84.0 %collective-permute-start.10 = (bf16[128,2176]{1,0:T(8,128)(2,1)}, bf16[128,2176]{1,0:T(8,128)(2,1)}, u32[]{:S(2)}, u32[]{:S(2)}) collective-permute-start(bf16[128,2176]{1,0:T(8,128)(2,1)} %pad_maximum_fusion.7), channel_id=1, source_target_pairs={{0,2},{1,3},{2,0},{3,1},{4,6},{5,7},{6,4},{7,5},{8,10},{9,11},{10,... | collective-permute-start | bytes 1671176 | tf_op jit(solution)/shard_map/ppermute | solution.py:29
  185.3 84.0 %collective-permute-start.9 = (bf16[128,2176]{1,0:T(8,128)(2,1)}, bf16[128,2176]{1,0:T(8,128)(2,1)}, u32[]{:S(2)}, u32[]{:S(2)}) collective-permute-start(bf16[128,2176]{1,0:T(8,128)(2,1)} %pad_maximum_fusion.7), channel_id=1, source_target_pairs={{0,1},{1,0},{2,3},{3,2},{4,5},{5,4},{6,7},{7,6},{8,9},{9,8},{10,11... | collective-permute-start | bytes 1671176 | tf_op jit(solution)/shard_map/ppermute | solution.py:29
  282.6 149.8 %collective-permute-start.16 = (bf16[512,2176]{1,0:T(8,128)(2,1)S(1)}, bf16[512,2176]{1,0:T(8,128)(2,1)}, u32[]{:S(2)}, u32[]{:S(2)}) collective-permute-start(bf16[512,2176]{1,0:T(8,128)(2,1)S(1)} %pad_maximum_fusion.2.cot_a), channel_id=1, source_target_pairs={{0,16},{8,24},{16,0},{24,8},{1,17},{9,25},{17,1},{25,9},{2,18},{10... | collective-permute-start | bytes 6684680 | tf_op jit(solution)/shard_map/ppermute | solution.py:29
  315.9 116.6 %collective-permute-start.12 = (bf16[512,2176]{1,0:T(8,128)(2,1)S(1)}, bf16[512,2176]{1,0:T(8,128)(2,1)}, u32[]{:S(2)}, u32[]{:S(2)}) collective-permute-start(bf16[512,2176]{1,0:T(8,128)(2,1)S(1)} %pad_maximum_fusion.2.cot_a), channel_id=1, source_target_pairs={{0,24},{8,16},{16,8},{24,0},{1,25},{9,17},{17,9},{25,1},{2,26},{10... | collective-permute-start | bytes 6684680 | tf_op jit(solution)/shard_map/ppermute | solution.py:29
  320.3 112.9 %collective-permute-start.18 = (bf16[512,2176]{1,0:T(8,128)(2,1)}, bf16[512,2176]{1,0:T(8,128)(2,1)}, u32[]{:S(2)}, u32[]{:S(2)}) collective-permute-start(bf16[512,2176]{1,0:T(8,128)(2,1)} %pad_maximum_fusion.1.sec_a), channel_id=1, source_target_pairs={{0,8},{8,0},{16,24},{24,16},{1,9},{9,1},{17,25},{25,17},{2,10},{10... | collective-permute-start | bytes 6684680 | tf_op jit(solution)/shard_map/ppermute | solution.py:29
  323.2 107.7 %all-to-all-start.2 = ((bf16[32,64,176]{2,1,0:T(8,128)(2,1)}), bf16[32,64,176]{2,1,0:T(8,128)(2,1)S(1)}, u32[]{:S(2)}, u32[]{:S(2)}) async-start(bf16[32,64,176]{2,1,0:T(8,128)(2,1)} %maximum_bitcast_fusion), calls=%async_computation.2 | async-start | bytes 2097152 | tf_op jit(solution)/shard_map/all_to_all | solution.py:436
  325.9 124.9 %collective-permute-start.22 = (bf16[512,2176]{1,0:T(8,128)(2,1)}, bf16[512,2176]{1,0:T(8,128)(2,1)}, u32[]{:S(2)}, u32[]{:S(2)}) collective-permute-start(bf16[512,2176]{1,0:T(8,128)(2,1)} %pad_maximum_fusion.1.sec_a), channel_id=1, source_target_pairs={{0,4},{4,0},{1,5},{5,1},{2,6},{6,2},{3,7},{7,3},{8,12},{12,8},{9,1... | collective-permute-start | bytes 6684680 | tf_op jit(solution)/shard_map/ppermute | solution.py:29
  326.1 160.2 %collective-permute-start.14 = (bf16[512,2176]{1,0:T(8,128)(2,1)}, bf16[512,2176]{1,0:T(8,128)(2,1)}, u32[]{:S(2)}, u32[]{:S(2)}) collective-permute-start(bf16[512,2176]{1,0:T(8,128)(2,1)} %pad_maximum_fusion.1.sec_a), channel_id=1, source_target_pairs={{0,16},{8,24},{16,0},{24,8},{1,17},{9,25},{17,1},{25,9},{2,18},{10... | collective-permute-start | bytes 6684680 | tf_op jit(solution)/shard_map/ppermute | solution.py:29
  432.4 97.7 %collective-permute-start.21 = (bf16[512,2176]{1,0:T(8,128)(2,1)}, bf16[512,2176]{1,0:T(8,128)(2,1)}, u32[]{:S(2)}, u32[]{:S(2)}) collective-permute-start(bf16[512,2176]{1,0:T(8,128)(2,1)} %collective-permute-done.20.cot_a), channel_id=1, source_target_pairs={{0,4},{4,0},{1,5},{5,1},{2,6},{6,2},{3,7},{7,3},{8,12},{12,8},{9,1... | collective-permute-start | bytes 6684680 | tf_op jit(solution)/shard_map/ppermute | solution.py:29
  432.4 98.2 %collective-permute-start.7 = (bf16[512,2176]{1,0:T(8,128)(2,1)}, bf16[512,2176]{1,0:T(8,128)(2,1)}, u32[]{:S(2)}, u32[]{:S(2)}) collective-permute-start(bf16[512,2176]{1,0:T(8,128)(2,1)} %pad_maximum_fusion.1.sec_a), channel_id=1, source_target_pairs={{0,24},{8,16},{16,8},{24,0},{1,25},{9,17},{17,9},{25,1},{2,26},{10... | collective-permute-start | bytes 6684680 | tf_op jit(solution)/shard_map/ppermute | solution.py:29
  433.1 97.5 %collective-permute-start.19 = (bf16[512,2176]{1,0:T(8,128)(2,1)}, bf16[512,2176]{1,0:T(8,128)(2,1)}, u32[]{:S(2)}, u32[]{:S(2)}) collective-permute-start(bf16[512,2176]{1,0:T(8,128)(2,1)} %collective-permute-done.18.sec_a), channel_id=1, source_target_pairs={{0,4},{4,0},{1,5},{5,1},{2,6},{6,2},{3,7},{7,3},{8,12},{12,8},{9,1... | collective-permute-start | bytes 6684680 | tf_op jit(solution)/shard_map/ppermute | solution.py:29
  450.8 122.0 %collective-permute-start.17 = (bf16[512,2176]{1,0:T(8,128)(2,1)}, bf16[512,2176]{1,0:T(8,128)(2,1)}, u32[]{:S(2)}, u32[]{:S(2)}) collective-permute-start(bf16[512,2176]{1,0:T(8,128)(2,1)} %collective-permute-done.16.cot_a), channel_id=1, source_target_pairs={{0,4},{4,0},{1,5},{5,1},{2,6},{6,2},{3,7},{7,3},{8,12},{12,8},{9,1... | collective-permute-start | bytes 6684680 | tf_op jit(solution)/shard_map/ppermute | solution.py:29
  486.2 86.7 %collective-permute-start.15 = (bf16[512,2176]{1,0:T(8,128)(2,1)}, bf16[512,2176]{1,0:T(8,128)(2,1)}, u32[]{:S(2)}, u32[]{:S(2)}) collective-permute-start(bf16[512,2176]{1,0:T(8,128)(2,1)} %collective-permute-done.14.sec_a), channel_id=1, source_target_pairs={{0,4},{4,0},{1,5},{5,1},{2,6},{6,2},{3,7},{7,3},{8,12},{12,8},{9,1... | collective-permute-start | bytes 6684680 | tf_op jit(solution)/shard_map/ppermute | solution.py:29
  530.1 85.3 %collective-permute-start.13 = (bf16[512,2176]{1,0:T(8,128)(2,1)}, bf16[512,2176]{1,0:T(8,128)(2,1)}, u32[]{:S(2)}, u32[]{:S(2)}) collective-permute-start(bf16[512,2176]{1,0:T(8,128)(2,1)} %collective-permute-done.12.cot_a), channel_id=1, source_target_pairs={{0,4},{4,0},{1,5},{5,1},{2,6},{6,2},{3,7},{7,3},{8,12},{12,8},{9,1... | collective-permute-start | bytes 6684680 | tf_op jit(solution)/shard_map/ppermute | solution.py:29
  530.6 204.7 %collective-permute-start.40 = (bf16[512,2176]{1,0:T(8,128)(2,1)}, bf16[512,2176]{1,0:T(8,128)(2,1)}, u32[]{:S(2)}, u32[]{:S(2)}) collective-permute-start(bf16[512,2176]{1,0:T(8,128)(2,1)} %slice.352), channel_id=1, source_target_pairs={{0,4},{4,0},{1,5},{5,1},{2,6},{6,2},{3,7},{7,3},{8,12},{12,8},{9,1... | collective-permute-start | bytes 6684680 | tf_op jit(solution)/shard_map/ppermute | solution.py:29
  530.7 84.7 %collective-permute-start.8 = (bf16[512,2176]{1,0:T(8,128)(2,1)}, bf16[512,2176]{1,0:T(8,128)(2,1)}, u32[]{:S(2)}, u32[]{:S(2)}) collective-permute-start(bf16[512,2176]{1,0:T(8,128)(2,1)} %collective-permute-done.7.sec_a), channel_id=1, source_target_pairs={{0,4},{4,0},{1,5},{5,1},{2,6},{6,2},{3,7},{7,3},{8,12},{12,8},{9,1... | collective-permute-start | bytes 6684680 | tf_op jit(solution)/shard_map/ppermute | solution.py:29
  572.8 132.1 %collective-permute-start.38 = (bf16[512,2176]{1,0:T(8,128)(2,1)}, bf16[512,2176]{1,0:T(8,128)(2,1)}, u32[]{:S(2)}, u32[]{:S(2)}) collective-permute-start(bf16[512,2176]{1,0:T(8,128)(2,1)} %slice.350), channel_id=1, source_target_pairs={{0,4},{4,0},{1,5},{5,1},{2,6},{6,2},{3,7},{7,3},{8,12},{12,8},{9,1... | collective-permute-start | bytes 6684680 | tf_op jit(solution)/shard_map/ppermute | solution.py:29
  614.9 94.6 %collective-permute-start.36 = (bf16[512,2176]{1,0:T(8,128)(2,1)}, bf16[512,2176]{1,0:T(8,128)(2,1)}, u32[]{:S(2)}, u32[]{:S(2)}) collective-permute-start(bf16[512,2176]{1,0:T(8,128)(2,1)} %slice.348), channel_id=1, source_target_pairs={{0,4},{4,0},{1,5},{5,1},{2,6},{6,2},{3,7},{7,3},{8,12},{12,8},{9,1... | collective-permute-start | bytes 6684680 | tf_op jit(solution)/shard_map/ppermute | solution.py:29
  718.6 99.4 %collective-permute-start.37 = (bf16[512,2176]{1,0:T(8,128)(2,1)}, bf16[512,2176]{1,0:T(8,128)(2,1)}, u32[]{:S(2)}, u32[]{:S(2)}) collective-permute-start(bf16[512,2176]{1,0:T(8,128)(2,1)} %add_convert_fusion.1), channel_id=1, source_target_pairs={{0,16},{8,24},{16,0},{24,8},{1,17},{9,25},{17,1},{25,9},{2,18},{10... | collective-permute-start | bytes 6684680 | tf_op jit(solution)/shard_map/ppermute | solution.py:29
  720.1 100.9 %collective-permute-start.35 = (bf16[512,2176]{1,0:T(8,128)(2,1)}, bf16[512,2176]{1,0:T(8,128)(2,1)}, u32[]{:S(2)}, u32[]{:S(2)}) collective-permute-start(bf16[512,2176]{1,0:T(8,128)(2,1)} %add_convert_fusion.2), channel_id=1, source_target_pairs={{0,24},{8,16},{16,8},{24,0},{1,25},{9,17},{17,9},{25,1},{2,26},{10... | collective-permute-start | bytes 6684680 | tf_op jit(solution)/shard_map/ppermute | solution.py:29
  731.6 94.5 %collective-permute-start.30 = (bf16[512,2048]{1,0:T(8,128)(2,1)}, bf16[512,2048]{1,0:T(8,128)(2,1)}, u32[]{:S(2)}, u32[]{:S(2)}) collective-permute-start(bf16[512,2048]{1,0:T(8,128)(2,1)} %slice.340), channel_id=1, source_target_pairs={{0,4},{4,0},{1,5},{5,1},{2,6},{6,2},{3,7},{7,3},{8,12},{12,8},{9,1... | collective-permute-start | bytes 6291464 | tf_op jit(solution)/shard_map/ppermute | solution.py:29
  735.4 122.6 %collective-permute-start.29 = (bf16[512,2048]{1,0:T(8,128)(2,1)}, bf16[512,2048]{1,0:T(8,128)(2,1)}, u32[]{:S(2)}, u32[]{:S(2)}) collective-permute-start(bf16[512,2048]{1,0:T(8,128)(2,1)} %add_convert_fusion.3), channel_id=1, source_target_pairs={{0,8},{8,0},{16,24},{24,16},{1,9},{9,1},{17,25},{25,17},{2,10},{10... | collective-permute-start | bytes 6291464 | tf_op jit(solution)/shard_map/ppermute | solution.py:29
  765.1 141.6 %collective-permute-start.27 = (bf16[512,2048]{1,0:T(8,128)(2,1)}, bf16[512,2048]{1,0:T(8,128)(2,1)}, u32[]{:S(2)}, u32[]{:S(2)}) collective-permute-start(bf16[512,2048]{1,0:T(8,128)(2,1)} %add_convert_fusion.4), channel_id=1, source_target_pairs={{0,16},{8,24},{16,0},{24,8},{1,17},{9,25},{17,1},{25,9},{2,18},{10... | collective-permute-start | bytes 6291464 | tf_op jit(solution)/shard_map/ppermute | solution.py:29
  818.0 88.7 %collective-permute-start.25 = (bf16[512,2048]{1,0:T(8,128)(2,1)}, bf16[512,2048]{1,0:T(8,128)(2,1)}, u32[]{:S(2)}, u32[]{:S(2)}) collective-permute-start(bf16[512,2048]{1,0:T(8,128)(2,1)} %add_convert_fusion.5), channel_id=1, source_target_pairs={{0,24},{8,16},{16,8},{24,0},{1,25},{9,17},{17,9},{25,1},{2,26},{10... | collective-permute-start | bytes 6291464 | tf_op jit(solution)/shard_map/ppermute | solution.py:29
  825.6 111.2 %collective-permute-start.43 = (bf16[128,2176]{1,0:T(8,128)(2,1)S(1)}, bf16[128,2176]{1,0:T(8,128)(2,1)}, u32[]{:S(2)}, u32[]{:S(2)}) collective-permute-start(bf16[128,2176]{1,0:T(8,128)(2,1)S(1)} %get-tuple-element.294), channel_id=1, source_target_pairs={{0,3},{1,2},{2,1},{3,0},{4,7},{5,6},{6,5},{7,4},{8,11},{9,10},{10,... | collective-permute-start | bytes 1671176 | tf_op jit(solution)/shard_map/ppermute | solution.py:29
  826.1 110.8 %collective-permute-start.42 = (bf16[128,2176]{1,0:T(8,128)(2,1)S(1)}, bf16[128,2176]{1,0:T(8,128)(2,1)}, u32[]{:S(2)}, u32[]{:S(2)}) collective-permute-start(bf16[128,2176]{1,0:T(8,128)(2,1)S(1)} %get-tuple-element.295), channel_id=1, source_target_pairs={{0,2},{1,3},{2,0},{3,1},{4,6},{5,7},{6,4},{7,5},{8,10},{9,11},{10,... | collective-permute-start | bytes 1671176 | tf_op jit(solution)/shard_map/ppermute | solution.py:29
  993.6 110.0 %all-to-all-start.5 = ((bf16[32,64,176]{2,1,0:T(8,128)(2,1)}), bf16[32,64,176]{2,1,0:T(8,128)(2,1)S(1)}, u32[]{:S(2)}, u32[]{:S(2)}) async-start(bf16[32,64,176]{2,1,0:T(8,128)(2,1)} %maximum_bitcast_fusion.1), calls=%async_computation.5 | async-start | bytes 2097152 | tf_op jit(solution)/shard_map/all_to_all | solution.py:636
  1052.0 130.1 %collective-permute-start.62 = (bf16[4,256,2048]{2,1,0:T(8,128)(2,1)}, bf16[4,256,2048]{2,1,0:T(8,128)(2,1)}, u32[]{:S(2)}, u32[]{:S(2)}) collective-permute-start(bf16[4,256,2048]{2,1,0:T(8,128)(2,1)} %fusion.3), channel_id=1, source_target_pairs={{0,4},{4,0},{1,5},{5,1},{2,6},{6,2},{3,7},{7,3},{8,12},{12,8},{9,1... | collective-permute-start | bytes 12582920 | tf_op jit(solution)/shard_map/ppermute | solution.py:29
  (160 other events, 4277.5 us)
Sparse Core Ops, SparseCore 0:
  12.2 85.9 all-gather.4
  100.1 39.1 all-gather.8
  142.8 112.7 all-gather.6
where the time goes:
time: 1310 us; the launch traced here: 1300 us
  waiting for transfers between devices  560 us (43%)
  starting transfers between devices  155 us (12%)
  Pallas kernels  155 us (12%)
  local copies, waits for them, and re-layouts  144 us (11%)
  other arithmetic  132 us (10%)
  matrix products  106 us (8%)
  blocking collectives  25.9 us (2%)
  between operations  16.4 us (1%)
    ppermute x69, waiting for transfers between devices, swap(): return lax.ppermute(block, axis, [(i, i ^ distance) for i in range(n)])  375 us
    pallas_call x4, Pallas kernels, expert_group(): pl.pallas_call(functools.partial(expert_kernel, local_experts, capacity,...  155 us
    ppermute x69, starting transfers between devices, swap(): return lax.ppermute(block, axis, [(i, i ^ distance) for i in range(n)])  136 us
    all_to_all x1, waiting for transfers between devices, on_device(): lax.all_to_all(shared_pack, EVERY, split_axis=0, concat_axis=0, tiled=True)  91.1 us
    dot_general x9, matrix products, on_device(): ein = lambda spec, a, b: jnp.einsum(spec, a, b, preferred_element_type=F32)  56.7 us
    unnamed x263, local copies, waits for them, and re-layouts  42.5 us
    dot_general x15, matrix products, dot(): return lax.dot_general(a, b, (dims, ((), ())), preferred_element_type=F32)  38 us
    all_gather x1, waiting for transfers between devices, on_device(): lax.all_gather(output_weight.astype(BF), EVERY, axis=0, tiled=True)  37.2 us
  transfers between devices with their start and end apart: 77, of which 27 were waited for; matrix products, arithmetic and copies ran while one was open for 27% of the time, Pallas kernels for 12%

commit v1 on v0

v1 whole, which is shorter than its diff:
```python
import functools

import jax
import jax.numpy as jnp
from jax import lax
from jax.experimental import pallas as pl
from jax.experimental.pallas import tpu as pltpu
from jax.sharding import Mesh, PartitionSpec as P

D = 2048
H = 16
DN = 128
DR = 64
DV = 128
KVR = 512
TOPK = 6
PIECE = 256
EPSILON = 1e-06
ROPE_BASE = 10000.0
NEGATIVE = -1e30
BF = jnp.bfloat16
F32 = jnp.float32
EVERY = ("c", "k", "z")
COLUMN = ("k", "z")


def swap(block, axis, distance):
    n = lax.axis_size(axis)
    return lax.ppermute(block, axis, [(i, i ^ distance) for i in range(n)])


def lanes(n):
    return -(-n // 128) * 128


def widen(block, extra):
    room = lanes(extra.shape[1]) - extra.shape[1]
    return jnp.concatenate([block, jnp.pad(extra.astype(BF), ((0, 0), (0, room)))], axis=1)


def dot(a, b, dims):
    return lax.dot_general(a, b, (dims, ((), ())), preferred_element_type=F32)


def mm(a, b):
    return dot(a, b, ((1,), (0,)))


def mm_nt(a, b):
    return dot(a, b, ((1,), (1,)))


def mm_tn(a, b):
    return dot(a, b, ((0,), (0,)))


def after(array, *others):
    return lax.optimization_barrier((array, *others))[0]


def after_all(arrays, *others):
    return lax.optimization_barrier((tuple(arrays), *others))[0]


def put(buffer, block, index):
    return lax.dynamic_update_slice_in_dim(buffer, block[None], index, axis=0)


def gather_z(unit):
    return [unit] + [swap(unit, "z", d) for d in range(1, lax.axis_size("z"))]


def in_order(blocks, index):
    whole = jnp.zeros((len(blocks), *blocks[0].shape), blocks[0].dtype)
    for d, block in enumerate(blocks):
        whole = put(whole, block, index ^ d)
    return whole


def gather_weight(unit):
    c_size, k_size, _ = (lax.axis_size(a) for a in EVERY)
    c, k, z = (lax.axis_index(a) for a in EVERY)
    mine = in_order(gather_z(unit), z)
    planes = [mine] + [swap(mine, "c", d) for d in range(1, c_size)]
    own = in_order(planes, c)
    other = swap(own, "k", 1)
    halves = in_order([own, other], k)
    return halves.transpose(1, 0, 2, 3, 4), planes[1:]


def scatter_z(blocks):
    total = blocks[0]
    for d in range(1, len(blocks)):
        total = total + swap(blocks[d].astype(BF), "z", d).astype(F32)
    return total


def scatter_column(part, rows):
    z_size = lax.axis_size("z")
    k, z = lax.axis_index("k"), lax.axis_index("z")
    grid = part.reshape(2, z_size, rows, part.shape[1])
    summed = pick(grid, k) + swap(pick(grid, k ^ 1).astype(BF), "k", 1).astype(F32)
    return scatter_z([pick(summed, z ^ d) for d in range(z_size)])


def core_sum(own, other, distance):
    summed = own.astype(F32) + swap(other, "k", 1).astype(F32)
    return summed.astype(BF) if distance else summed


def plane_sum(sums, *others):
    moved = [swap(block, "c", d) for d, block in enumerate(sums) if d]
    if others:
        moved = after_all(moved, *others)
    total = sums[0]
    for block in moved:
        total = total + block.astype(F32)
    return total, moved


def z_units(total, rows):
    return [total[d * rows : (d + 1) * rows] for d in range(lax.axis_size("z"))]


def pick(array, index):
    return lax.dynamic_index_in_dim(array, index, axis=0, keepdims=False)


def core_pieces(part):
    c_size, k_size, z_size = (lax.axis_size(a) for a in EVERY)
    c, k = lax.axis_index("c"), lax.axis_index("k")
    grid = part.reshape(c_size, k_size, part.shape[0] // (c_size * k_size), part.shape[1])
    got = swap(lax.dynamic_index_in_dim(grid, k ^ 1, axis=1, keepdims=False), "k", 1)
    kept = lax.dynamic_index_in_dim(grid, k, axis=1, keepdims=False)
    pieces = []
    for d in range(c_size):
        piece = pick(kept, c ^ d).astype(F32) + pick(got, c ^ d).astype(F32)
        pieces.append(piece.astype(BF) if d else piece)
    return pieces


def pieces_sum(pieces, *others):
    total, _ = plane_sum(pieces, *others)
    return z_sum(total)


def z_sum(total):
    z_size, z = lax.axis_size("z"), lax.axis_index("z")
    total = total.reshape(z_size, total.shape[0] // z_size, total.shape[1])
    return scatter_z([pick(total, z ^ d) for d in range(z_size)])


def scatter_weight(part):
    return pieces_sum(core_pieces(part))


def rms_parts(values):
    return lax.rsqrt(jnp.mean(values * values, axis=-1, keepdims=True) + EPSILON)


def rms_back(values, scale, gain, grad):
    weighted = grad * gain
    inner = jnp.mean(weighted * values, axis=-1, keepdims=True)
    return scale * (weighted - values * (scale * scale * inner)), grad * values * scale


def rotate(values, cosine, sine, sign):
    half = values.shape[-1] // 2
    a, b = values[..., :half], values[..., half:]
    return jnp.concatenate([a * cosine - sign * b * sine, b * cosine + sign * a * sine], axis=-1)


def expert_kernel(
    local_experts,
    capacity,
    rows,
    experts,
    first,
    place_ref,
    sec_a,
    sec_b,
    cot_a,
    cot_b,
    gate_hbm,
    up_hbm,
    down_hbm,
    sin_hbm,
    sdn_hbm,
    *rest,
):
    rest = rest if first else rest[5:]
    (x_out, c_out, aw_out, gg_out, ug_out, out_a, out_b, in_a, in_b, sg_out, sd_out) = rest[:11]
    (sec_v, cot_v, gate_v, up_v, down_v, sin_v, sdn_v, x_v, c_v, y_v, z_v, aw_v, gg_v, ug_v) = rest[11:25]
    (choose_v, prob_v, sact_v, slow_v, sgp_v, sdp_v, sem_in, sem_out, sem_block) = rest[25:34]
    half = sec_a.shape[0]
    blocks = 2 * half // rows
    per = blocks * capacity
    wpad = sdn_v.shape[0]
    base = place_ref[1] * per

    def copy(src, dst, sem, i):
        made = pltpu.make_async_copy(src, dst, sem.at[i])
        made.start()
        return made

    in_sec = [
        copy(sec_a, sec_v.at[pl.ds(0, half)], sem_in, 0),
        copy(sec_b, sec_v.at[pl.ds(half, half)], sem_in, 1),
    ]
    in_cot = [
        copy(cot_a, cot_v.at[pl.ds(0, half)], sem_in, 2),
        copy(cot_b, cot_v.at[pl.ds(half, half)], sem_in, 3),
    ]
    for one in in_cot:
        one.wait()

    first_expert = place_ref[0]
    tail = cot_v.shape[1] - D
    row_i = lax.broadcasted_iota(jnp.int32, (rows, rows), 0)
    col_i = lax.broadcasted_iota(jnp.int32, (rows, rows), 1)
    earlier = (col_i < row_i).astype(BF)
    lane = lax.broadcasted_iota(jnp.int32, (rows, tail), 1)
    slot = lax.broadcasted_iota(jnp.int32, (rows, local_experts * capacity), 1).astype(F32)
    for one in in_sec:
        one.wait()
    in_sin = copy(sin_hbm, sin_v, sem_in, 7)
    in_sdn = copy(sdn_hbm, sdn_v, sem_in, 8)
    in_gate = copy(gate_hbm, gate_v, sem_in, 4)
    in_up = copy(up_hbm, up_v, sem_in, 5)
    in_down = copy(down_hbm, down_v, sem_in, 6)
    sec_tail = sec_v.shape[1] - D
    tail_lane = lax.broadcasted_iota(jnp.int32, (capacity, sec_tail), 1)

    def gather(b, carry):
        at = pl.ds(pl.multiple_of(b * rows, rows), rows)
        named = cot_v[at, D:]
        rank = mm(earlier, named)
        code = jnp.where((named.astype(F32) > 0) & (rank < capacity), rank, -1e6)
        chosen = jnp.zeros(slot.shape, F32)
        for e in range(local_experts):
            own = jnp.sum(jnp.where(lane == first_expert + e, code, 0.0), axis=1, keepdims=True)
            chosen = jnp.where(own + e * capacity == slot, 1.0, chosen)
        choose = chosen.astype(BF)
        choose_v[at, :] = choose
        picked = mm_tn(choose, sec_v[at, :])
        cots = mm_tn(choose, cot_v[at, :D])
        for e in range(local_experts):
            mine = slice(e * capacity, (e + 1) * capacity)
            to = pl.ds(pl.multiple_of(e * per + b * capacity, capacity), capacity)
            x_v[to, :] = picked[mine, :D].astype(BF)
            c_v[to, :] = cots[mine].astype(BF)
            which = first_expert + e
            hits = (tail_lane == which) | (tail_lane == which + experts)
            prob = jnp.sum(jnp.where(hits, picked[mine, D:], 0.0), axis=1, keepdims=True)
            prob_v[to, :] = jnp.broadcast_to(prob, (capacity, 128))
        return carry

    lax.fori_loop(0, blocks, gather, 0)
    outs = []
    for e in range(local_experts):
        mine = pl.ds(e * per, per)
        outs.append(copy(x_v.at[mine], x_out.at[e, pl.ds(base, per)], sem_out, 2 * e))
        outs.append(copy(c_v.at[mine], c_out.at[e, pl.ds(base, per)], sem_out, 2 * e + 1))
    used = 2 * local_experts

    in_sin.wait()
    in_sdn.wait()
    shared = mm(sec_v[:, :D], sin_v[...])
    s_gate, s_up = shared[:, :wpad], shared[:, wpad:]
    s_sigma = jax.nn.sigmoid(s_gate)
    s_silu = s_gate * s_sigma
    s_grad = mm_nt(cot_v[:, :D], sdn_v[...])
    sact_v[...] = (s_silu * s_up).astype(BF)
    slow_v[:, :wpad] = (s_grad * s_up * (s_sigma * (1.0 + s_gate * (1.0 - s_sigma)))).astype(BF)
    slow_v[:, wpad:] = (s_grad * s_silu).astype(BF)
    sgp_v[...] = mm_tn(slow_v[...], sec_v[:, :D])
    sdp_v[...] = mm_tn(sact_v[...], cot_v[:, :D])
    cot_v[:, :D] = mm(sact_v[...], sdn_v[...]).astype(BF)
    sec_v[:, :D] = mm_nt(slow_v[...], sin_v[...]).astype(BF)
    outs.append(copy(sgp_v, sg_out, sem_out, used))
    outs.append(copy(sdp_v, sd_out, sem_out, used + 1))
    used += 2

    in_gate.wait()
    in_up.wait()
    in_down.wait()
    in_tail = z_v.shape[2] - D
    pair_lane = lax.broadcasted_iota(jnp.int32, (per, in_tail), 1)
    for e in range(local_experts):
        mine = pl.ds(e * per, per)
        x_e, c_e = x_v[mine, :], c_v[mine, :]
        gate = mm_nt(x_e, gate_v[e])
        up = mm_nt(x_e, up_v[e])
        pull = mm_nt(c_e, down_v[e])
        prob = prob_v[mine, :1]
        sigma = jax.nn.sigmoid(gate)
        silu = gate * sigma
        act = silu * up
        pair = jnp.sum(pull * act, axis=1, keepdims=True)
        pull = pull * prob
        gg_v[e] = (pull * up * (sigma * (1.0 + gate * (1.0 - sigma)))).astype(BF)
        ug_v[e] = (pull * silu).astype(BF)
        aw_v[e] = (act * prob).astype(BF)
        outs.append(copy(aw_v.at[e], aw_out.at[e, pl.ds(base, per)], sem_out, used))
        outs.append(copy(gg_v.at[e], gg_out.at[e, pl.ds(base, per)], sem_out, used + 1))
        outs.append(copy(ug_v.at[e], ug_out.at[e, pl.ds(base, per)], sem_out, used + 2))
        used += 3
        y = mm(aw_v[e], down_v[e]).astype(BF)
        y_v[:, e * capacity : (e + 1) * capacity, :] = y.reshape(blocks, capacity, D)
        zed = (mm(gg_v[e], gate_v[e]) + mm(ug_v[e], up_v[e])).astype(BF)
        z_v[:, e * capacity : (e + 1) * capacity, :D] = zed.reshape(blocks, capacity, D)
        pairs = jnp.where(pair_lane == first_expert + e, pair, 0.0).astype(BF)
        z_v[:, e * capacity : (e + 1) * capacity, D:] = pairs.reshape(blocks, capacity, in_tail)

    def block_copies(b):
        moves = []
        for i, (to_in, to_out) in enumerate(((in_a, out_a), (in_b, out_b))):
            at = pl.ds(pl.multiple_of(b * rows, rows), rows)
            from_at = pl.ds(pl.multiple_of(i * half + b * rows, rows), rows)
            moves.append(pltpu.make_async_copy(sec_v.at[from_at], to_in.at[at], sem_block.at[i, 0, b]))
            moves.append(
                pltpu.make_async_copy(cot_v.at[from_at, pl.ds(0, D)], to_out.at[at], sem_block.at[i, 1, b])
            )
        return moves

    def scatter(b, carry):
        for i in range(2):
            at = pl.ds(pl.multiple_of(i * half + b * rows, rows), rows)
            choose = choose_v[at, :]
            which = i * (half // rows) + b
            cot_v[at, :D] = (mm(choose, y_v[which]) + cot_v[at, :D].astype(F32)).astype(BF)
            back = mm(choose, z_v[which])
            sec_v[at, :D] = (back[:, :D] + sec_v[at, :D].astype(F32)).astype(BF)
            sec_v[at, D:] = back[:, D:].astype(BF)
        for move in block_copies(b):
            move.start()
        return carry

    lax.fori_loop(0, half // rows, scatter, 0)
    for b in range(half // rows):
        for move in block_copies(b):
            move.wait()
    for one in outs:
        one.wait()


def expert_group(place, sec, cot, weights, kept, capacity, rows, experts, groups):
    gate, up, down, sin, sdn = weights
    local_experts, hidden, _ = gate.shape
    half = sec[0].shape[0]
    tokens = 2 * half
    blocks = tokens // rows
    per = blocks * capacity
    slots = per * groups
    wpad = sdn.shape[0]
    in_width = D + lanes(experts)
    big = (local_experts, slots)
    shapes = [
        jax.ShapeDtypeStruct((*big, D), BF),
        jax.ShapeDtypeStruct((*big, D), BF),
        jax.ShapeDtypeStruct((*big, hidden), BF),
        jax.ShapeDtypeStruct((*big, hidden), BF),
        jax.ShapeDtypeStruct((*big, hidden), BF),
        jax.ShapeDtypeStruct((half, D), BF),
        jax.ShapeDtypeStruct((half, D), BF),
        jax.ShapeDtypeStruct((half, in_width), BF),
        jax.ShapeDtypeStruct((half, in_width), BF),
        jax.ShapeDtypeStruct((2 * wpad, D), F32),
        jax.ShapeDtypeStruct((wpad, D), F32),
    ]
    first = kept is None
    operands = [place, *sec, *cot, gate, up, down, sin, sdn] + ([] if first else list(kept))
    any_space = pl.BlockSpec(memory_space=pl.ANY)
    smem = pl.BlockSpec(memory_space=pltpu.SMEM)
    return pl.pallas_call(
        functools.partial(expert_kernel, local_experts, capacity, rows, experts, first),
        out_shape=shapes,
        in_specs=[smem] + [any_space] * (len(operands) - 1),
        out_specs=[any_space] * len(shapes),
        scratch_shapes=[
            pltpu.VMEM((tokens, sec[0].shape[1]), BF),
            pltpu.VMEM((tokens, cot[0].shape[1]), BF),
            pltpu.VMEM(gate.shape, BF),
            pltpu.VMEM(up.shape, BF),
            pltpu.VMEM(down.shape, BF),
            pltpu.VMEM(sin.shape, BF),
            pltpu.VMEM(sdn.shape, BF),
            pltpu.VMEM((local_experts * per, D), BF),
            pltpu.VMEM((local_experts * per, D), BF),
            pltpu.VMEM((blocks, local_experts * capacity, D), BF),
            pltpu.VMEM((blocks, local_experts * capacity, in_width), BF),
            pltpu.VMEM((local_experts, per, hidden), BF),
            pltpu.VMEM((local_experts, per, hidden), BF),
            pltpu.VMEM((local_experts, per, hidden), BF),
            pltpu.VMEM((tokens, local_experts * capacity), BF),
            pltpu.VMEM((local_experts * per, 128), F32),
            pltpu.VMEM((tokens, wpad), BF),
            pltpu.VMEM((tokens, 2 * wpad), BF),
            pltpu.VMEM((2 * wpad, D), F32),
            pltpu.VMEM((wpad, D), F32),
            pltpu.SemaphoreType.DMA((9,)),
            pltpu.SemaphoreType.DMA((5 * local_experts + 2,)),
            pltpu.SemaphoreType.DMA((2, 2, half // rows)),
        ],
        input_output_aliases={} if first else {10 + i: i for i in range(5)},
        compiler_params=pltpu.CompilerParams(vmem_limit_bytes=63 * 1024 * 1024),
        cost_estimate=pl.CostEstimate(flops=1 << 20, bytes_accessed=1 << 16, transcendentals=0),
    )(*operands)


def turn(values, cosine, sine):
    lane = lax.broadcasted_iota(jnp.int32, values.shape, 1)
    partner = jnp.where(
        lane % DR < DR // 2, pltpu.roll(values, 2 * DR - DR // 2, 1), pltpu.roll(values, DR // 2, 1)
    )
    return values * cosine + partner * sine


def score_block(i, block, image, scores):
    row = lax.broadcasted_iota(jnp.int32, scores.shape, 0) + i * block
    column = lax.broadcasted_iota(jnp.int32, scores.shape, 1)
    allowed = (column <= row) | ((column >= i * block) & image)
    return jnp.where(allowed, scores * ((DN + DR) ** (-0.5)), NEGATIVE)


def head_part(values, h):
    lane = lax.broadcasted_iota(jnp.int32, values.shape, 1)
    return jnp.where(lane // DR == h, values.astype(F32), 0.0).astype(BF)


def attend_kernel(
    heads, rows, place, seq, gain, lgain, wq, wd, wup, cos, sin, out, first, q_out, lat_out, kr_out, ex_out, own_out, down_v
):
    block = PIECE
    nope = heads * DN
    for i in range(seq.shape[0] // block):
        at = slice(i * block, (i + 1) * block)
        values = seq[at, :D].astype(F32)
        low = (values * rms_parts(values) * gain[...]).astype(BF)
        first[at, :] = low
        q = mm(low, wq[...])
        down = mm(low, wd[...])
        down_v[at, :] = down
        latent = down[:, :KVR]
        lat = (latent * rms_parts(latent) * lgain[...]).astype(BF)
        lat_out[at, :] = lat
        ex_out[at, :] = mm(lat, wup[...]).astype(BF)
        turned = turn(down[:, KVR : KVR + 2 * DR], cos[at, :], sin[at, :])
        lane = lax.broadcasted_iota(jnp.int32, turned.shape, 1)
        turned = jnp.where(lane < DR, turned, 0.0)
        kr_out[at, :] = (turned + pltpu.roll(turned, DR, 1)).astype(BF)
        q_rope = turn(q[:, nope:], cos[at, :], sin[at, :]).astype(BF)
        q_out[at, :nope] = q[:, :nope].astype(BF)
        q_out[at, nope:] = q_rope
        image = seq[at, D : D + 128][:, :1].astype(F32) > 0
        n = (i + 1) * block
        for h in range(heads):
            mine = slice(h * (DN + DV), h * (DN + DV) + DN)
            scores = mm_nt(q_out[at, h * DN : (h + 1) * DN], ex_out[:n, mine])
            scores = scores + mm_nt(head_part(q_rope, h), kr_out[:n, :])
            scores = score_block(i, block, image, scores)
            weight = jnp.exp(scores - jnp.max(scores, axis=1, keepdims=True))
            weight = weight / jnp.sum(weight, axis=1, keepdims=True)
            value = ex_out[:n, h * (DN + DV) + DN : (h + 1) * (DN + DV)]
            out[at, h * DV : (h + 1) * DV] = mm(weight.astype(BF), value).astype(BF)
    own_out[...] = down_v[pl.ds(pl.multiple_of(place[0] * rows, rows), rows), :]


def attend(place, seq, gain, lgain, wq, wd, wup, cos, sin, heads, rows):
    length = seq.shape[0]
    shapes = [
        jax.ShapeDtypeStruct((length, heads * DV), BF),
        jax.ShapeDtypeStruct((length, D), BF),
        jax.ShapeDtypeStruct((length, wq.shape[1]), BF),
        jax.ShapeDtypeStruct((length, KVR), BF),
        jax.ShapeDtypeStruct((length, 2 * DR), BF),
        jax.ShapeDtypeStruct((length, wup.shape[1]), BF),
        jax.ShapeDtypeStruct((rows, wd.shape[1]), F32),
    ]
    vmem = pl.BlockSpec(memory_space=pltpu.VMEM)
    return pl.pallas_call(
        functools.partial(attend_kernel, heads, rows),
        out_shape=shapes,
        in_specs=[pl.BlockSpec(memory_space=pltpu.SMEM)] + [vmem] * 8,
        out_specs=[vmem] * len(shapes),
        scratch_shapes=[pltpu.VMEM((length, wd.shape[1]), F32)],
        compiler_params=pltpu.CompilerParams(vmem_limit_bytes=56 * 1024 * 1024),
        cost_estimate=pl.CostEstimate(flops=1 << 20, bytes_accessed=1 << 16, transcendentals=0),
    )(place, seq, gain, lgain, wq, wd, wup, cos, sin)


def attend_back_kernel(
    heads, place, grad, flags, first, q, kr, ex, lat, wq, wup, cos, sin,
    gain_out, first_keep, first_send, lat_keep, lat_send, pack_out,
    dk_v, dv_v, dr_v, qg_v, eg_v,
):
    block = PIECE
    nope = heads * DN
    length = first.shape[0]
    half = length // 2
    scale = (DN + DR) ** (-0.5)
    dk_v[...] = jnp.zeros_like(dk_v)
    dv_v[...] = jnp.zeros_like(dv_v)
    dr_v[...] = jnp.zeros_like(dr_v)
    for i in range(length // block):
        at = slice(i * block, (i + 1) * block)
        n = (i + 1) * block
        image = flags[at, :1].astype(F32) > 0
        rope_grad = jnp.zeros((block, 2 * DR), F32)
        for h in range(heads):
            mine = slice(h * (DN + DV), h * (DN + DV) + DN)
            value = ex[:n, h * (DN + DV) + DN : (h + 1) * (DN + DV)]
            q_nope = q[at, h * DN : (h + 1) * DN]
            q_rope = head_part(q[at, nope:], h)
            scores = mm_nt(q_nope, ex[:n, mine]) + mm_nt(q_rope, kr[:n, :])
            scores = score_block(i, block, image, scores)
            weight = jnp.exp(scores - jnp.max(scores, axis=1, keepdims=True))
            weight = weight / jnp.sum(weight, axis=1, keepdims=True)
            upstream = grad[at, h * DV : (h + 1) * DV]
            dprob = mm_nt(upstream, value)
            dv_v[:n, h * DV : (h + 1) * DV] += mm_tn(weight.astype(BF), upstream)
            inner = jnp.sum(weight * dprob, axis=1, keepdims=True)
            back = (weight * (dprob - inner)).astype(BF)
            qg_v[at, h * DN : (h + 1) * DN] = (mm(back, ex[:n, mine]) * scale).astype(BF)
            turned = mm(back, kr[:n, :])
            lane = lax.broadcasted_iota(jnp.int32, turned.shape, 1)
            rope_grad = jnp.where(lane // DR == h, turned * scale, rope_grad)
            dk_v[:n, h * DN : (h + 1) * DN] += mm_tn(back, q_nope)
            dr_v[:n, :] += mm_tn(back, q_rope)
        qg_v[at, nope:] = turn(rope_grad, cos[at, :], -sin[at, :]).astype(BF)
    for h in range(heads):
        mine = slice(h * (DN + DV), h * (DN + DV) + DN)
        eg_v[:, mine] = (dk_v[:, h * DN : (h + 1) * DN] * scale).astype(BF)
        eg_v[:, h * (DN + DV) + DN : (h + 1) * (DN + DV)] = dv_v[:, h * DV : (h + 1) * DV].astype(BF)
    key_rope = dr_v[...]
    key_rope = (key_rope + pltpu.roll(key_rope, DR, 1)) * scale
    dr_v[...] = key_rope
    keep = pl.ds(pl.multiple_of(place[1] * half, half), half)
    send = pl.ds(pl.multiple_of((1 - place[1]) * half, half), half)
    total = jnp.zeros((1, D), F32)
    for at, to_lat, to_first in ((send, lat_send, first_send), (keep, lat_keep, first_keep)):
        to_lat[:, :KVR] = mm_nt(eg_v[at, :], wup[...]).astype(BF)
        to_lat[:, KVR:] = dr_v[at, :].astype(BF)
        part = mm_nt(qg_v[at, :], wq[...])
        to_first[...] = part.astype(BF)
        total = total + jnp.sum(part * first[at, :].astype(F32), axis=0, keepdims=True)
    gain_out[...] = total
    owners, pack_rows, _ = pack_out.shape
    wide = wq.shape[1]
    q_rows = D // owners
    pack_out[:, :q_rows, :wide] = mm_tn(first[...], qg_v[...]).astype(BF).reshape(owners, q_rows, wide)
    pack_out[:, :q_rows, wide:] = jnp.zeros((owners, q_rows, pack_out.shape[2] - wide), BF)
    pack_out[:, q_rows:, :] = mm_tn(lat[...], eg_v[...]).astype(BF).reshape(owners, pack_rows - q_rows, -1)


def attend_back(place, grad, flags, first, q, kr, ex, lat, wq, wup, cos, sin, heads, owners):
    length = first.shape[0]
    half = length // 2
    wide = KVR + 2 * DR
    shapes = [
        jax.ShapeDtypeStruct((1, D), F32),
        jax.ShapeDtypeStruct((half, D), BF),
        jax.ShapeDtypeStruct((half, D), BF),
        jax.ShapeDtypeStruct((half, wide), BF),
        jax.ShapeDtypeStruct((half, wide), BF),
        jax.ShapeDtypeStruct((owners, (D + KVR) // owners, wup.shape[1]), BF),
    ]
    vmem = pl.BlockSpec(memory_space=pltpu.VMEM)
    return pl.pallas_call(
        functools.partial(attend_back_kernel, heads),
        out_shape=shapes,
        in_specs=[pl.BlockSpec(memory_space=pltpu.SMEM)] + [vmem] * 11,
        out_specs=[vmem] * len(shapes),
        scratch_shapes=[
            pltpu.VMEM((length, heads * DN), F32),
            pltpu.VMEM((length, heads * DV), F32),
            pltpu.VMEM((length, 2 * DR), F32),
            pltpu.VMEM((length, q.shape[1]), BF),
            pltpu.VMEM((length, ex.shape[1]), BF),
        ],
        compiler_params=pltpu.CompilerParams(vmem_limit_bytes=56 * 1024 * 1024),
        cost_estimate=pl.CostEstimate(flops=1 << 20, bytes_accessed=1 << 16, transcendentals=0),
    )(place, grad, flags, first, q, kr, ex, lat, wq, wup, cos, sin)


def on_device(
    tokens,
    attention_norm,
    query_weight,
    latent_down,
    latent_norm,
    latent_up,
    output_weight,
    post_norm,
    shared_gate,
    shared_up,
    shared_down,
    router_weight,
    expert_gate,
    expert_up,
    expert_down,
    image_piece_index,
    routes,
    cotangent,
):
    rows = tokens.shape[0]
    c_size, k_size, z_size = (lax.axis_size(a) for a in EVERY)
    c, k, z = (lax.axis_index(a) for a in EVERY)
    column_size = k_size * z_size
    device_count = c_size * column_size
    local_experts = expert_gate.shape[0]
    experts = router_weight.shape[1]
    capacity = rows * TOPK * 4 // (3 * experts)
    length = column_size * rows
    heads = H // column_size
    width = shared_down.shape[0]
    score_scale = (DN + DR) ** (-0.5)
    weight_rows = query_weight.shape[0]
    up_rows = latent_up.shape[0]

    paired = H == 4 * c_size and heads == 2 and column_size == 8

    def by_owner(array, n):
        if paired:
            array = array.reshape(-1, 2, 2, 4, n).transpose(0, 3, 1, 2, 4)
        return array.reshape(-1, column_size, heads * n)

    def by_head(array, n):
        if paired:
            array = array.reshape(-1, 4, 2, 2, n).transpose(0, 2, 3, 1, 4)
        return array.reshape(-1, H * n)

    flag = (image_piece_index > 0).astype(BF)[:, None]
    expert_ids = jnp.arange(experts, dtype=jnp.int32)
    named = jnp.any(routes[:, :, None] == expert_ids[None, None, :], axis=1)

    out_mine = in_order(gather_z(output_weight.astype(BF)), z)
    extra = -(-weight_rows // 8) * 8 + 8 - weight_rows
    down_width = KVR + DR
    small_width = lanes(max(down_width + experts + 8, weight_rows))
    gains = jnp.stack(
        [attention_norm, post_norm, jnp.pad(latent_norm, (0, weight_rows - latent_norm.shape[0]))]
    )
    small = jnp.concatenate([latent_down, router_weight], axis=1).astype(BF)
    small = jnp.pad(small, ((0, 0), (0, small_width - small.shape[1])))
    gains = jnp.pad(gains.astype(BF), ((0, extra - 3), (0, small_width - weight_rows)))
    small = jnp.concatenate([small, gains], axis=0)
    q_width = heads * (DN + DR)
    kv_width = heads * (DN + DV)
    q_out = by_owner(query_weight.astype(BF), DN + DR).transpose(1, 0, 2)
    q_out = q_out.reshape(column_size, weight_rows, heads, DN + DR)
    q_out = jnp.concatenate(
        [q_out[..., :DN].reshape(column_size, weight_rows, -1), q_out[..., DN:].reshape(column_size, weight_rows, -1)],
        axis=2,
    )
    q_out = jnp.pad(q_out, ((0, 0), (0, 0), (0, kv_width - q_width)))
    up_out = by_owner(latent_up.astype(BF), DN + DV).transpose(1, 0, 2)
    head_pack = jnp.concatenate([q_out, up_out], axis=1)
    head_pack = lax.all_to_all(head_pack, COLUMN, split_axis=0, concat_axis=0, tiled=True)
    token_units = gather_z(after(widen(tokens, flag), head_pack))
    cot_units = gather_z(after(widen(cotangent, named), *token_units[1:]))
    head_pack = [head_pack] + [swap(head_pack, "c", d) for d in range(1, c_size)]
    small, small_recv = gather_weight(small)
    mine = in_order(after_all(token_units, *head_pack[1:], *small_recv), z)
    sequence = in_order([mine, swap(mine, "k", 1)], k).reshape(length, -1)
    small = small.reshape(device_count, weight_rows + extra, small_width)
    full_small = small[:, :weight_rows].reshape(D, small_width)
    full_router = full_small[:, down_width : down_width + experts]
    full_gains = small[:, weight_rows : weight_rows + 3, :weight_rows].astype(F32)
    attn_gain = full_gains[:, 0].reshape(D)
    post_gain = full_gains[:, 1].reshape(D)
    latent_gain = full_gains[:, 2, : latent_norm.shape[0]].reshape(KVR)
    out_mine = after(out_mine, *head_pack[1:])
    out_planes = [out_mine] + [swap(out_mine, "c", d) for d in range(1, c_size)]
    head_pack = in_order(head_pack, c)
    head_query = head_pack[:, :, :weight_rows, :q_width].reshape(D, q_width)
    head_up = head_pack[:, :, weight_rows:].reshape(KVR, kv_width)
    shared_pack = jnp.concatenate(
        [
            shared_gate.astype(BF).reshape(weight_rows, device_count, width),
            shared_up.astype(BF).reshape(weight_rows, device_count, width),
        ],
        axis=2,
    ).transpose(1, 0, 2)
    shared_in = lax.all_to_all(after(shared_pack, *token_units[1:]), EVERY, split_axis=0, concat_axis=0, tiled=True)
    shared_low = shared_down.astype(BF)

    places = jnp.arange(length, dtype=F32)
    frequency = ROPE_BASE ** (-2.0 * jnp.arange(DR // 2, dtype=F32) / DR)
    angles = places[:, None] * frequency[None, :]
    cosine, sine = jnp.cos(angles), jnp.sin(angles)
    cosine_wide = jnp.tile(cosine, (1, 4))
    sine_wide = jnp.tile(jnp.concatenate([-sine, sine], axis=1), (1, 2))
    here = k * z_size + z

    def own_rows(array):
        return lax.dynamic_slice_in_dim(array, here * rows, rows, axis=0)

    spot = jnp.stack([here, k]).astype(jnp.int32)
    heads_out, first_low, query_low, latent_low, rope_low, expanded, down_raw = attend(
        spot, sequence, attn_gain[None], latent_gain[None], head_query, full_small, head_up,
        cosine_wide, sine_wide, heads, rows,
    )
    own_values = tokens.astype(F32)
    own_scale = rms_parts(own_values)
    own_first_low = (own_values * own_scale * attn_gain).astype(BF)
    latent_raw = down_raw[:, :KVR]
    latent_scale = rms_parts(latent_raw)

    def heads_to_tokens(array):
        n = array.shape[1]
        moved = lax.all_to_all(
            array.reshape(column_size, rows, n), COLUMN, split_axis=0, concat_axis=0, tiled=True
        )
        return by_head(moved.transpose(1, 0, 2), n // heads)

    def tokens_to_heads(array):
        n = array.shape[1] // H
        moved = lax.all_to_all(
            by_owner(array, n).transpose(1, 0, 2), COLUMN, split_axis=0, concat_axis=0, tiled=True
        )
        return moved.reshape(length, heads * n)

    shared_in, *cot_units = after_all([shared_in, *cot_units], heads_out)
    cot_own = jnp.concatenate(cot_units, axis=0)
    shared_in = shared_in.reshape(D, 2 * width)
    room = ((0, 0), (0, lanes(width) - width))
    shared_in = jnp.concatenate(
        [jnp.pad(shared_in[:, :width], room), jnp.pad(shared_in[:, width:], room)], axis=1
    )
    out_planes = in_order(after_all(out_planes, heads_out, cot_own), c)
    full_out = in_order([out_planes, swap(out_planes, "k", 1)], k)
    full_out = full_out.transpose(1, 0, 2, 3, 4).reshape(D, D)

    def plane_groups(own):
        near = [swap(own, "c", d) for d in range(1, c_size - 1)]
        return [own, *near, swap(after(own, *near), "c", c_size - 1)]

    cot_groups = plane_groups(cot_own)
    heads_low = after(
        heads_to_tokens(after(heads_out, cot_own, shared_in)), full_out, *cot_groups[1:-1]
    )
    residual = tokens.astype(F32) + mm(heads_low, full_out)
    second_scale = rms_parts(residual)
    second_low = (residual * second_scale * post_gain).astype(BF)
    router_probs = jax.nn.softmax(mm(second_low, full_router), axis=-1)

    probs_high = router_probs.astype(BF)
    probs_rest = (router_probs - probs_high.astype(F32)).astype(BF)
    second_own = jnp.concatenate(
        gather_z(widen(second_low, jnp.concatenate([probs_high, probs_rest], axis=1))), axis=0
    )
    second_own = after(second_own, cot_groups[-1])
    second_groups = plane_groups(second_own)
    pair = lambda group: (group, swap(group, "k", 1))
    cot_groups = [pair(g) for g in cot_groups]
    wpad = lanes(width)
    place = jnp.stack([(c * k_size + k) * local_experts, jnp.zeros((), jnp.int32)]).astype(jnp.int32)
    shared_rows = jnp.pad(shared_low, ((0, wpad - width), (0, 0)))
    weights = (
        jnp.swapaxes(expert_gate, 1, 2),
        jnp.swapaxes(expert_up, 1, 2),
        expert_down,
        shared_in,
        shared_rows,
    )
    kept, sg_parts, sd_parts, sums, out_sums, marks = None, [], [], [], [], []
    arrived = []
    for d in range(c_size):
        where = place.at[1].set(d)
        group = second_groups[d]
        if d:
            group = after(group, marks[max(d - 2, 0)])
        if d > 1:
            where = after(where, out_sums[d - 2], sums[d - 1])
        results = list(
            expert_group(
                where, pair(group), cot_groups[d], weights, kept, capacity, rows, experts, c_size
            )
        )
        kept = results[:5]
        marks.append(results[10])
        if d == c_size - 1:
            results[8] = after(results[8], *arrived)
        sums.append(core_sum(*results[7:9], d))
        if d:
            arrived.append(swap(sums[d], "c", d))
        if d == c_size - 1:
            kept = after_all(kept, *arrived[:-1])
            results[6] = after(results[6], arrived[-1])
        out_sums.append(core_sum(*results[5:7], d))
        sg_parts.append(results[9])
        sd_parts.append(results[10])
    plane = functools.reduce(lambda total, block: total + block.astype(F32), arrived, sums[0])
    expert_in, cot_in, act_weighted, gate_grad, up_grad = kept
    ein = lambda spec, a, b: jnp.einsum(spec, a, b, preferred_element_type=F32)
    expert_down_grad = ein("esf,esd->efd", act_weighted, cot_in)
    expert_gate_grad = jnp.swapaxes(ein("esf,esd->efd", gate_grad, expert_in), 1, 2)
    expert_up_grad = jnp.swapaxes(ein("esf,esd->efd", up_grad, expert_in), 1, 2)
    plane = after(plane, expert_down_grad, expert_gate_grad, expert_up_grad)
    second_sum = scatter_z(z_units(plane, rows))
    out_near = [swap(after(out_sums[d], *arrived), "c", d) for d in range(1, c_size - 1)]
    second_sum = after(second_sum, *out_near, out_sums[-1])
    out_far = swap(after(out_sums[-1], *out_near), "c", c_size - 1)
    probs_grad = second_sum[:, D : D + experts]
    logits_grad = (
        router_probs * (probs_grad - jnp.sum(router_probs * probs_grad, axis=-1, keepdims=True))
    ).astype(BF)
    second_grad = second_sum[:, :D] + mm_nt(logits_grad, full_router)
    norm_part, post_terms = rms_back(residual, second_scale, post_gain, second_grad)
    residual_grad = cotangent.astype(F32) + norm_part
    attn_grad_low = residual_grad.astype(BF)
    heads_grad = tokens_to_heads(mm_nt(attn_grad_low, full_out).astype(BF))
    output_pieces = core_pieces(mm_tn(heads_low, attn_grad_low).astype(BF))

    gain_part, first_keep, first_send, latent_keep, latent_send, head_grad = attend_back(
        after(spot, *output_pieces), heads_grad, sequence[:, D:], first_low, query_low,
        rope_low, expanded, latent_low, head_query, head_up, cosine_wide, sine_wide, heads, device_count,
    )
    def column_sum(keep, send):
        summed = keep.astype(F32) + swap(send, "k", 1).astype(F32)
        summed = summed.reshape(z_size, rows, keep.shape[1])
        return scatter_z([pick(summed, z ^ d) for d in range(z_size)])

    latent_sum = column_sum(latent_keep, after(latent_send, out_far))
    out_plane = functools.reduce(
        lambda total, block: total + block.astype(F32),
        after_all([*out_near, out_far], latent_sum),
        out_sums[0],
    )
    out_units = z_units(out_plane, rows)
    out_units = out_units[:1] + [swap(unit.astype(BF), "z", d) for d, unit in enumerate(out_units) if d]
    first_keep = after(first_keep, latent_sum)
    shared_in_grad = sum(sg_parts[1:], sg_parts[0])
    shared_in_grad = jnp.concatenate(
        [shared_in_grad[:width], shared_in_grad[wpad : wpad + width]], axis=0
    ).astype(BF)
    shared_down_grad = sum(sd_parts[1:], sd_parts[0])[:width]
    shared_back = shared_in_grad.reshape(2 * width, c_size, column_size, weight_rows).transpose(2, 1, 3, 0)
    shared_back = lax.all_to_all(
        after(shared_back, latent_keep), COLUMN, split_axis=0, concat_axis=0, tiled=True
    )
    latent_raw_grad, latent_terms = rms_back(
        latent_raw, latent_scale, latent_gain, latent_sum[:, :KVR]
    )
    rope_raw_grad = rotate(
        latent_sum[:, KVR:down_width], own_rows(cosine), own_rows(sine), -1.0
    )
    down_grad_low = jnp.concatenate([latent_raw_grad, rope_raw_grad], axis=-1).astype(BF)
    first_own = mm_nt(down_grad_low, full_small[:, :down_width])
    attn_gain_grad = gain_part[0] / attn_gain + jnp.sum(
        first_own * (own_values * own_scale), axis=0
    )
    gain_grads = jnp.stack(
        [
            attn_gain_grad,
            jnp.sum(post_terms, axis=0),
            jnp.pad(
                jnp.sum(latent_terms, axis=0).reshape(device_count, latent_norm.shape[0]),
                ((0, 0), (0, weight_rows - latent_norm.shape[0])),
            ).reshape(D),
        ]
    )
    first_gain = down_width + experts
    small_right = jnp.zeros((2 * rows + 8, small_width), BF)
    small_right = small_right.at[:rows, :down_width].set(down_grad_low)
    small_right = small_right.at[rows : 2 * rows, down_width:first_gain].set(logits_grad)
    ones = (jnp.arange(8)[:, None] == jnp.arange(small_width)[None, :] - first_gain).astype(BF)
    small_right = small_right.at[2 * rows :].set(ones)
    small_left = jnp.concatenate(
        [own_first_low, second_low, jnp.pad(gain_grads, ((0, 5), (0, 0))).astype(BF)], axis=0
    )
    output_moved = [swap(block, "c", d) for d, block in enumerate(output_pieces) if d]
    small_left = after(small_left, *output_moved)
    small_pieces = core_pieces(mm_tn(small_left, small_right).astype(BF))
    head_grad = head_grad.reshape(c_size, column_size, weight_rows + up_rows, kv_width)
    head_moved = [swap(pick(head_grad, c ^ d), "c", d) for d in range(1, c_size)]
    small_plane, _ = plane_sum(small_pieces, *head_moved)
    output_plane = functools.reduce(
        lambda total, block: total + block.astype(F32),
        after_all(output_moved, small_plane),
        output_pieces[0],
    )
    shared_back = after(shared_back, small_plane)
    shared_back = in_order(
        [
            swap(lax.dynamic_index_in_dim(shared_back, c ^ d, axis=1, keepdims=False), "c", d)
            if d
            else lax.dynamic_index_in_dim(shared_back, c, axis=1, keepdims=False)
            for d in range(c_size)
        ],
        c,
    ).reshape(device_count, weight_rows, 2 * width).transpose(1, 0, 2)
    first_grad = after(column_sum(first_keep, first_send), small_plane) + first_own
    out_sum = functools.reduce(
        lambda total, block: total + block.astype(F32), after_all(out_units[1:], first_grad), out_units[0]
    )
    layer_out = (residual + out_sum).astype(BF)
    first_norm_grad, _ = rms_back(own_values, own_scale, attn_gain, first_grad)
    tokens_grad = residual_grad + first_norm_grad
    own_small = z_sum(small_plane)
    own_output = z_sum(output_plane)
    head_sum = pick(head_grad, c).astype(F32)
    for block in after_all(head_moved, small_plane):
        head_sum = head_sum + block.astype(F32)
    head_sum = lax.all_to_all(head_sum.astype(BF), COLUMN, split_axis=0, concat_axis=0, tiled=True)
    own_query = head_sum[:, :weight_rows, :q_width].transpose(1, 0, 2)
    own_query = jnp.concatenate(
        [
            own_query[..., : heads * DN].reshape(weight_rows, column_size, heads, DN),
            own_query[..., heads * DN :].reshape(weight_rows, column_size, heads, DR),
        ],
        axis=3,
    )
    own_query = by_head(own_query.reshape(weight_rows, column_size, q_width), DN + DR)
    own_up = by_head(head_sum[:, weight_rows:].transpose(1, 0, 2), DN + DV)
    own_gate = shared_back[:, :, :width].reshape(weight_rows, -1)
    own_shared_up = shared_back[:, :, width:].reshape(weight_rows, -1)
    return (
        layer_out,
        tokens_grad,
        own_small[:, first_gain],
        own_query.astype(F32),
        own_small[:, :down_width],
        own_small[: latent_norm.shape[0], first_gain + 2],
        own_up.astype(F32),
        own_output,
        own_small[:, first_gain + 1],
        own_gate.astype(F32),
        own_shared_up.astype(F32),
        shared_down_grad,
        own_small[:, down_width:first_gain],
        expert_gate_grad,
        expert_up_grad,
        expert_down_grad,
    )


def solution(mesh):
    expert_size, z_size = mesh.devices.shape
    fine = Mesh(mesh.devices.reshape(expert_size // 2, 2, z_size), EVERY)
    row, flat = P(EVERY, None), P(EVERY)
    wide, tall = P(("c", "k"), None, "z"), P(("c", "k"), "z", None)
    return jax.shard_map(
        on_device,
        mesh=fine,
        in_specs=(row, flat, row, row, flat, row, row, flat, row, row, row, row)
        + (wide, wide, tall, flat, row, row),
        out_specs=(row, row, flat, row, row, flat, row, row, flat, row, row, row, row)
        + (wide, wide, tall),
        check_vma=False,
    )
```

time: 1310 us -> 966 us (0.74)
  waiting for transfers between devices: 560 us -> 329 us
  matrix products: 106 us -> 59.9 us
  other arithmetic: 132 us -> 92.4 us
  blocking collectives: 25.9 us -> 0 us
  Pallas kernels: 155 us -> 177 us
  between operations: 16.4 us -> 2.43 us
    all_to_all x4 -> x5, waiting for transfers between devices: 127 us -> 7.85 us  [the longest x1 5.7 us: heads_to_tokens(): lax.all_to_all(array.reshape(column_size, rows, n), COLUMN, split_axis=0,...]
    all_gather x3 -> x0, waiting for transfers between devices: 57.7 us -> none  [the longest x1 37.2 us: on_device(): lax.all_gather(output_weight.astype(BF), EVERY, axis=0, tiled=True)]
    ppermute x69 -> x89, waiting for transfers between devices: 375 us -> 321 us  [swap(): return lax.ppermute(block, axis, [(i, i ^ distance) for i in range(n)])]
    dynamic_update_slice x0 -> x32, local copies, waits for them, and re-layouts: none -> 47.1 us  [put(): return lax.dynamic_update_slice_in_dim(buffer, block[None], index, axis=0)]
    pallas_call x0 -> x2, Pallas kernels: none -> 37.6 us  [the longest x1 20.4 us: attend_back(): pl.pallas_call(functools.partial(attend_back_kernel, heads), out_shape=sh...]
    concatenate x25 -> x6, local copies, waits for them, and re-layouts: 34.9 us -> 2.96 us  [the longest x1 1.9 us: on_device(): cot_own = jnp.concatenate(cot_units, axis=0)]
    all_to_all x1 -> x0, blocking collectives: 25.9 us -> none  [on_device(): lax.all_to_all(head_pack, COLUMN, split_axis=0, concat_axis=0, tiled=True)]
    unnamed x263 -> x145, local copies, waits for them, and re-layouts: 42.5 us -> 18.5 us
  transfers between devices with their start and end apart: 77 -> 95, of which waited for: 27 -> 34; matrix products, arithmetic and copies ran while one was open for 27% -> 28% of each run, Pallas kernels for 12% -> 18%
where the time goes in v1:
time: 966 us; the launch traced here: 960 us
  waiting for transfers between devices  329 us (34%)
  Pallas kernels  177 us (18%)
  local copies, waits for them, and re-layouts  152 us (16%)
  starting transfers between devices  148 us (15%)
  other arithmetic  92.4 us (10%)
  matrix products  59.9 us (6%)
    ppermute x89, waiting for transfers between devices, swap(): return lax.ppermute(block, axis, [(i, i ^ distance) for i in range(n)])  321 us
    pallas_call x4, Pallas kernels, expert_group(): pl.pallas_call(functools.partial(expert_kernel, local_experts, capacity,...  139 us
    ppermute x89, starting transfers between devices, swap(): return lax.ppermute(block, axis, [(i, i ^ distance) for i in range(n)])  120 us
    dynamic_update_slice x32, local copies, waits for them, and re-layouts, put(): return lax.dynamic_update_slice_in_dim(buffer, block[None], index, axis=0)  47.1 us
    dot_general x3, matrix products, on_device(): ein = lambda spec, a, b: jnp.einsum(spec, a, b, preferred_element_type=F32)  37.8 us
    dot_general x7, matrix products, dot(): return lax.dot_general(a, b, (dims, ((), ())), preferred_element_type=F32)  22 us
    pallas_call x1, Pallas kernels, attend_back(): pl.pallas_call(functools.partial(attend_back_kernel, heads), out_shape=sh...  20.4 us
  transfers between devices with their start and end apart: 95, of which 34 were waited for; matrix products, arithmetic and copies ran while one was open for 28% of the time, Pallas kernels for 18%

profile of v1, /device:TPU:0, one launch (start us, length us, event | category | flops | bytes accessed | tf_op | source)
XLA Modules:
  0.0 960.4 jit_solution(14638991938004068283)
XLA Ops:
  56.3 9.7 %collective-permute-done.9 = bf16[4,72,640]{2,1,0:T(8,128)(2,1)S(1)} collective-permute-done((bf16[4,72,640]{2,1,0:T(8,128)(2,1)S(1)}, bf16[4,72,640]{2,1,0:T(8,128)(2,1)S(1)}, u32[]{:S(2)}, u32[]{:S(2)}) %collective-permute-start.9) | collective-permute-done | bytes 368672 | tf_op jit(solution)/shard_map/ppermute | solution.py:29
  84.8 19.3 %collective-permute-done.1 = bf16[128,2176]{1,0:T(8,128)(2,1)S(1)} collective-permute-done((bf16[128,2176]{1,0:T(8,128)(2,1)S(1)}, bf16[128,2176]{1,0:T(8,128)(2,1)S(1)}, u32[]{:S(2)}, u32[]{:S(2)}) %collective-permute-start.1) | collective-permute-done | bytes 557088 | tf_op jit(solution)/shard_map/ppermute | solution.py:29
  149.9 17.2 %shard_map.297 = (bf16[1024,256]{1,0:T(8,128)(2,1)}, bf16[1024,2048]{1,0:T(8,128)(2,1)}, bf16[1024,384]{1,0:T(8,128)(2,1)}, bf16[1024,512]{1,0:T(8,128)(2,1)}, b...) custom-call(s32[2]{0:T(128)} %pad_add_fusion.place, bf16[1024,2176]{1,0:T(8,128)(2,1)} %bitcast.20.seq, ...), custom_call_target="tpu_custom_call" | custom-call | flops 1048576 | bytes 65536 | tf_op jit(solution)/shard_map/pallas_call | solution.py:481
  167.7 15.5 %collective-permute-done.15 = bf16[128,2176]{1,0:T(8,128)(2,1)} collective-permute-done((bf16[128,2176]{1,0:T(8,128)(2,1)}, bf16[128,2176]{1,0:T(8,128)(2,1)}, u32[]{:S(2)}, u32[]{:S(2)}) %collective-permute-start.15) | collective-permute-done | bytes 557088 | tf_op jit(solution)/shard_map/ppermute | solution.py:29
  209.4 6.6 all-to-all-start.2
  232.1 20.6 %collective-permute-done.25.cot_a = bf16[512,2176]{1,0:T(8,128)(2,1)S(1)} collective-permute-done((bf16[512,2176]{1,0:T(8,128)(2,1)}, bf16[512,2176]{1,0:T(8,128)(2,1)S(1)}, u32[]{:S(2)}, u32[]{:S(2)}) %collective-permute-start.25) | collective-permute-done | bytes 2228256 | tf_op jit(solution)/shard_map/ppermute | solution.py:29
  274.5 10.7 %collective-permute-done.28 = bf16[128,2176]{1,0:T(8,128)(2,1)S(1)} collective-permute-done((bf16[128,2176]{1,0:T(8,128)(2,1)S(1)}, bf16[128,2176]{1,0:T(8,128)(2,1)S(1)}, u32[]{:S(2)}, u32[]{:S(2)}) %collective-permute-start.28) | collective-permute-done | bytes 557088 | tf_op jit(solution)/shard_map/ppermute | solution.py:29
  285.2 33.8 %collective-permute-done.27 = bf16[128,2176]{1,0:T(8,128)(2,1)S(1)} collective-permute-done((bf16[128,2176]{1,0:T(8,128)(2,1)S(1)}, bf16[128,2176]{1,0:T(8,128)(2,1)S(1)}, u32[]{:S(2)}, u32[]{:S(2)}) %collective-permute-start.27) | collective-permute-done | bytes 557088 | tf_op jit(solution)/shard_map/ppermute | solution.py:29
  327.9 35.0 %shard_map.298 = (bf16[2,2048,2048]{2,1,0:T(8,128)(2,1)}, bf16[2,2048,2048]{2,1,0:T(8,128)(2,1)}, bf16[2,2048,352]{2,1,0:T(8,128)(2,1)}, bf16[2,2048,352]{2,1,0:...) custom-call(s32[2]{0:T(128)} %copy-done.66, ...), custom_call_target="tpu_custom_call" | custom-call | flops 1048576 | bytes 65536 | tf_op jit(solution)/shard_map/pallas_call | solution.py:375
  362.9 11.5 %collective-permute-done.33.sec_a = bf16[512,2176]{1,0:T(8,128)(2,1)} collective-permute-done((bf16[512,2176]{1,0:T(8,128)(2,1)}, bf16[512,2176]{1,0:T(8,128)(2,1)}, u32[]{:S(2)}, u32[]{:S(2)}) %collective-permute-start.33) | collective-permute-done | bytes 2228256 | tf_op jit(solution)/shard_map/ppermute | solution.py:29
  379.1 34.5 %shard_map.299 = (bf16[2,2048,2048]{2,1,0:T(8,128)(2,1)}, bf16[2,2048,2048]{2,1,0:T(8,128)(2,1)}, bf16[2,2048,352]{2,1,0:T(8,128)(2,1)}, bf16[2,2048,352]{2,1,0:...) custom-call(s32[2]{0:T(128)} %copy-done.63, ...), custom_call_target="tpu_custom_call", output_to_operand_aliasing={{0}: (10, {}), {1}: (11, {}), {2}: (12, {}), {3}: (13, {}),... | custom-call | flops 1048576 | bytes 65536 | tf_op jit(solution)/shard_map/pallas_call | solution.py:375
  414.2 11.4 %collective-permute-done.39.sec_a = bf16[512,2176]{1,0:T(8,128)(2,1)} collective-permute-done((bf16[512,2176]{1,0:T(8,128)(2,1)}, bf16[512,2176]{1,0:T(8,128)(2,1)}, u32[]{:S(2)}, u32[]{:S(2)}) %collective-permute-start.39) | collective-permute-done | bytes 2228256 | tf_op jit(solution)/shard_map/ppermute | solution.py:29
  431.6 34.8 %shard_map.300 = (bf16[2,2048,2048]{2,1,0:T(8,128)(2,1)}, bf16[2,2048,2048]{2,1,0:T(8,128)(2,1)}, bf16[2,2048,352]{2,1,0:T(8,128)(2,1)}, bf16[2,2048,352]{2,1,0:...) custom-call(s32[2]{0:T(128)} %copy-done.64, ...), custom_call_target="tpu_custom_call", output_to_operand_aliasing={{0}: (10, {}), {1}: (11, {}), {2}: (12, {}), {3}: (13, {}),... | custom-call | flops 1048576 | bytes 65536 | tf_op jit(solution)/shard_map/pallas_call | solution.py:375
  467.0 10.8 %collective-permute-done.44.sec_a = bf16[512,2176]{1,0:T(8,128)(2,1)} collective-permute-done((bf16[512,2176]{1,0:T(8,128)(2,1)}, bf16[512,2176]{1,0:T(8,128)(2,1)}, u32[]{:S(2)}, u32[]{:S(2)}) %collective-permute-start.44) | collective-permute-done | bytes 2228256 | tf_op jit(solution)/shard_map/ppermute | solution.py:29
  487.8 35.0 %shard_map.301 = (bf16[2,2048,2048]{2,1,0:T(8,128)(2,1)}, bf16[2,2048,2048]{2,1,0:T(8,128)(2,1)}, bf16[2,2048,352]{2,1,0:T(8,128)(2,1)}, bf16[2,2048,352]{2,1,0:...) custom-call(s32[2]{0:T(128)} %copy-done.62, ...), custom_call_target="tpu_custom_call", output_to_operand_aliasing={{0}: (10, {}), {1}: (11, {}), {2}: (12, {}), {3}: (13, {}),... | custom-call | flops 1048576 | bytes 65536 | tf_op jit(solution)/shard_map/pallas_call | solution.py:375
  533.8 12.4 %fusion.95 = f32[2,2048,352]{1,2,0:T(8,128)} fusion(bf16[2,2048,2048]{2,1,0:T(8,128)(2,1)} %get-tuple-element.291, bf16[2,2048,352]{2,1,0:T(8,128)(2,1)} %get-tuple-element.292), kind=kOutput, calls=%fused_computation.262 | convolution fusion | flops 5905580032 | bytes 25427968 | tf_op jit(solution)/shard_map/esf,esd->efd/dot_general | solution.py:796
  552.6 12.6 %fusion.96 = f32[2,2048,352]{1,2,0:T(8,128)} fusion(bf16[2,2048,2048]{2,1,0:T(8,128)(2,1)} %get-tuple-element.291, bf16[2,2048,352]{2,1,0:T(8,128)(2,1)S(1)} %copy-done.2), kind=kOutput, calls=%fused_computation.263 | convolution fusion | flops 5905580032 | bytes 25427968 | tf_op jit(solution)/shard_map/esf,esd->efd/dot_general | solution.py:796
  565.2 12.9 %fusion.94 = f32[2,352,2048]{2,1,0:T(8,128)} fusion(bf16[2,2048,352]{2,1,0:T(8,128)(2,1)S(1)} %copy-done, bf16[2,2048,2048]{2,1,0:T(8,128)(2,1)} %get-tuple-element.290), kind=kOutput, calls=%fused_computation.261 | convolution fusion | flops 5905580032 | bytes 25427968 | tf_op jit(solution)/shard_map/esf,esd->efd/dot_general | solution.py:796
  578.1 25.0 %collective-permute-done.48 = bf16[512,2176]{1,0:T(8,128)(2,1)} collective-permute-done((bf16[512,2176]{1,0:T(8,128)(2,1)}, bf16[512,2176]{1,0:T(8,128)(2,1)}, u32[]{:S(2)}, u32[]{:S(2)}) %collective-permute-start.48) | collective-permute-done | bytes 2228256 | tf_op jit(solution)/shard_map/ppermute | solution.py:29
  623.5 13.4 %collective-permute-start.56 = (bf16[128,2176]{1,0:T(8,128)(2,1)S(1)}, bf16[128,2176]{1,0:T(8,128)(2,1)S(1)}, u32[]{:S(2)}, u32[]{:S(2)}) collective-permute-start(bf16[128,2176]{1,0:T(8,128)(2,1)S(1)} %get-tuple-element.475), channel_id=1, source_target_pairs={{0,2},{1,3},{2,0},{3,1},{4,6},{5,7},{6,4},{7,5},{8,10},{9,11},{10,... | collective-permute-start | bytes 1671176 | tf_op jit(solution)/shard_map/ppermute | solution.py:29
  637.2 28.2 %collective-permute-done.56 = bf16[128,2176]{1,0:T(8,128)(2,1)S(1)} collective-permute-done((bf16[128,2176]{1,0:T(8,128)(2,1)S(1)}, bf16[128,2176]{1,0:T(8,128)(2,1)S(1)}, u32[]{:S(2)}, u32[]{:S(2)}) %collective-permute-start.56) | collective-permute-done | bytes 557088 | tf_op jit(solution)/shard_map/ppermute | solution.py:29
  682.5 7.1 convolution_convert_fusion.2
  705.8 7.2 fusion.2
  715.2 20.4 %shard_map.302 = (f32[1,2048]{1,0:T(1,128)}, bf16[512,2048]{1,0:T(8,128)(2,1)}, bf16[512,2048]{1,0:T(8,128)(2,1)}, bf16[512,640]{1,0:T(8,128)(2,1)}, bf16[512,64...) custom-call(s32[2]{0:T(128)} %pad_add_fusion.place, bf16[1024,256]{1,0:T(8,128)(2,1)} %bitcast.73.grad, ...), custom_call_target="tpu_custom_call" | custom-call | flops 1048576 | bytes 65536 | tf_op jit(solution)/shard_map/pallas_call | solution.py:569
  777.8 21.0 %collective-permute-done.71 = bf16[256,2048]{1,0:T(8,128)(2,1)} collective-permute-done((bf16[256,2048]{1,0:T(8,128)(2,1)}, bf16[256,2048]{1,0:T(8,128)(2,1)}, u32[]{:S(2)}, u32[]{:S(2)}) %collective-permute-start.71) | collective-permute-done | bytes 1048608 | tf_op jit(solution)/shard_map/ppermute | solution.py:29
  804.3 6.7 fusion.88
  818.6 10.6 %collective-permute-done.67 = bf16[128,2048]{1,0:T(8,128)(2,1)S(1)} collective-permute-done((bf16[128,2048]{1,0:T(8,128)(2,1)S(1)}, bf16[128,2048]{1,0:T(8,128)(2,1)S(1)}, u32[]{:S(2)}, u32[]{:S(2)}) %collective-permute-start.67) | collective-permute-done | bytes 524320 | tf_op jit(solution)/shard_map/ppermute | solution.py:29
  830.8 9.8 %collective-permute-done.69 = bf16[128,2048]{1,0:T(8,128)(2,1)S(1)} collective-permute-done((bf16[128,2048]{1,0:T(8,128)(2,1)S(1)}, bf16[128,2048]{1,0:T(8,128)(2,1)S(1)}, u32[]{:S(2)}, u32[]{:S(2)}) %collective-permute-start.69) | collective-permute-done | bytes 524320 | tf_op jit(solution)/shard_map/ppermute | solution.py:29
  841.1 20.7 %collective-permute-done.68 = bf16[128,2048]{1,0:T(8,128)(2,1)S(1)} collective-permute-done((bf16[128,2048]{1,0:T(8,128)(2,1)S(1)}, bf16[128,2048]{1,0:T(8,128)(2,1)S(1)}, u32[]{:S(2)}, u32[]{:S(2)}) %collective-permute-start.68) | collective-permute-done | bytes 524320 | tf_op jit(solution)/shard_map/ppermute | solution.py:29
  892.4 12.0 %collective-permute-start.81 = (bf16[64,640]{1,0:T(8,128)(2,1)S(1)}, bf16[64,640]{1,0:T(8,128)(2,1)S(1)}, u32[]{:S(2)}, u32[]{:S(2)}) collective-permute-start(bf16[64,640]{1,0:T(8,128)(2,1)S(1)} %get-tuple-element.496), channel_id=1, source_target_pairs={{0,2},{1,3},{2,0},{3,1},{4,6},{5,7},{6,4},{7,5},{8,10},{9,11},{10,... | collective-permute-start | bytes 245768 | tf_op jit(solution)/shard_map/ppermute | solution.py:29
  904.4 17.4 %collective-permute-done.64 = bf16[128,2048]{1,0:T(8,128)(2,1)} collective-permute-done((bf16[128,2048]{1,0:T(8,128)(2,1)}, bf16[128,2048]{1,0:T(8,128)(2,1)}, u32[]{:S(2)}, u32[]{:S(2)}) %collective-permute-start.64) | collective-permute-done | bytes 524320 | tf_op jit(solution)/shard_map/ppermute | solution.py:29
  943.0 8.7 collective-permute-done.84
  (540 shorter events, 405.8 us)
Async XLA Ops:
  104.9 78.3 %all-to-all-start.1 = ((bf16[32,64,176]{2,1,0:T(8,128)(2,1)}), bf16[32,64,176]{2,1,0:T(8,128)(2,1)}, u32[]{:S(2)}, u32[]{:S(2)}) async-start(bf16[32,64,176]{2,1,0:T(8,128)(2,1)} %maximum_bitcast_fusion), calls=%async_computation.1 | async-start | bytes 2097152 | tf_op jit(solution)/shard_map/all_to_all | solution.py:685
  109.2 57.9 %collective-permute-start.16 = (bf16[128,2176]{1,0:T(8,128)(2,1)}, bf16[128,2176]{1,0:T(8,128)(2,1)}, u32[]{:S(2)}, u32[]{:S(2)}) collective-permute-start(bf16[128,2176]{1,0:T(8,128)(2,1)} %pad_maximum_fusion.4), channel_id=1, source_target_pairs={{0,3},{1,2},{2,1},{3,0},{4,7},{5,6},{6,5},{7,4},{8,11},{9,10},{10,... | collective-permute-start | bytes 1671176 | tf_op jit(solution)/shard_map/ppermute | solution.py:29
  112.8 70.3 %collective-permute-start.15 = (bf16[128,2176]{1,0:T(8,128)(2,1)}, bf16[128,2176]{1,0:T(8,128)(2,1)}, u32[]{:S(2)}, u32[]{:S(2)}) collective-permute-start(bf16[128,2176]{1,0:T(8,128)(2,1)} %pad_maximum_fusion.4), channel_id=1, source_target_pairs={{0,2},{1,3},{2,0},{3,1},{4,6},{5,7},{6,4},{7,5},{8,10},{9,11},{10,... | collective-permute-start | bytes 1671176 | tf_op jit(solution)/shard_map/ppermute | solution.py:29
  112.8 70.3 %collective-permute-start.14 = (bf16[128,2176]{1,0:T(8,128)(2,1)}, bf16[128,2176]{1,0:T(8,128)(2,1)}, u32[]{:S(2)}, u32[]{:S(2)}) collective-permute-start(bf16[128,2176]{1,0:T(8,128)(2,1)} %pad_maximum_fusion.4), channel_id=1, source_target_pairs={{0,1},{1,0},{2,3},{3,2},{4,5},{5,4},{6,7},{7,6},{8,9},{9,8},{10,11... | collective-permute-start | bytes 1671176 | tf_op jit(solution)/shard_map/ppermute | solution.py:29
  129.3 61.9 %collective-permute-start.22 = (bf16[4,64,2048]{2,1,0:T(8,128)(2,1)}, bf16[4,64,2048]{2,1,0:T(8,128)(2,1)}, u32[]{:S(2)}, u32[]{:S(2)}) collective-permute-start(bf16[4,64,2048]{2,1,0:T(8,128)(2,1)} %bitcast_dynamic-update-slice_fusion.24), channel_id=1, source_target_pairs={{0,24},{8,16},{16,8},{24,0},{1,25},{9,17},{17,9},{25,1},{2,26},{10... | collective-permute-start | bytes 3145736 | tf_op jit(solution)/shard_map/ppermute | solution.py:29
  201.6 52.9 %collective-permute-start.23 = (bf16[4,4,64,2048]{3,2,1,0:T(8,128)(2,1)}, bf16[4,4,64,2048]{3,2,1,0:T(8,128)(2,1)}, u32[]{:S(2)}, u32[]{:S(2)}) collective-permute-start(bf16[4,4,64,2048]{3,2,1,0:T(8,128)(2,1)} %bitcast_dynamic-update-slice_fusion.4), channel_id=1, source_target_pairs={{0,4},{4,0},{1,5},{5,1},{2,6},{6,2},{3,7},{7,3},{8,12},{12,8},{9,1... | collective-permute-start | bytes 12582920 | tf_op jit(solution)/shard_map/ppermute | solution.py:29
  201.6 51.1 %collective-permute-start.25 = (bf16[512,2176]{1,0:T(8,128)(2,1)}, bf16[512,2176]{1,0:T(8,128)(2,1)S(1)}, u32[]{:S(2)}, u32[]{:S(2)}) collective-permute-start(bf16[512,2176]{1,0:T(8,128)(2,1)} %constant_dynamic-update-slice_fusion.1.cot_a), channel_id=1, source_target_pairs={{0,16},{8,24},{16,0},{24,8},{1,17},{9,25},{17,1},{25,9},{2,18},{10... | collective-permute-start | bytes 6684680 | tf_op jit(solution)/shard_map/ppermute | solution.py:29
  203.0 50.9 %collective-permute-start.24 = (bf16[512,2176]{1,0:T(8,128)(2,1)}, bf16[512,2176]{1,0:T(8,128)(2,1)}, u32[]{:S(2)}, u32[]{:S(2)}) collective-permute-start(bf16[512,2176]{1,0:T(8,128)(2,1)} %constant_dynamic-update-slice_fusion.1.cot_a), channel_id=1, source_target_pairs={{0,8},{8,0},{16,24},{24,16},{1,9},{9,1},{17,25},{25,17},{2,10},{10... | collective-permute-start | bytes 6684680 | tf_op jit(solution)/shard_map/ppermute | solution.py:29
  253.9 69.3 %collective-permute-start.29 = (bf16[512,2176]{1,0:T(8,128)(2,1)}, bf16[512,2176]{1,0:T(8,128)(2,1)}, u32[]{:S(2)}, u32[]{:S(2)}) collective-permute-start(bf16[512,2176]{1,0:T(8,128)(2,1)} %constant_dynamic-update-slice_fusion.1.cot_a), channel_id=1, source_target_pairs={{0,24},{8,16},{16,8},{24,0},{1,25},{9,17},{17,9},{25,1},{2,26},{10... | collective-permute-start | bytes 6684680 | tf_op jit(solution)/shard_map/ppermute | solution.py:29
  271.0 48.0 %collective-permute-start.27 = (bf16[128,2176]{1,0:T(8,128)(2,1)S(1)}, bf16[128,2176]{1,0:T(8,128)(2,1)S(1)}, u32[]{:S(2)}, u32[]{:S(2)}) collective-permute-start(bf16[128,2176]{1,0:T(8,128)(2,1)S(1)} %pad_maximum_fusion.5), channel_id=1, source_target_pairs={{0,2},{1,3},{2,0},{3,1},{4,6},{5,7},{6,4},{7,5},{8,10},{9,11},{10,... | collective-permute-start | bytes 1671176 | tf_op jit(solution)/shard_map/ppermute | solution.py:29
  274.5 51.5 %collective-permute-start.31 = (bf16[512,2176]{1,0:T(8,128)(2,1)}, bf16[512,2176]{1,0:T(8,128)(2,1)}, u32[]{:S(2)}, u32[]{:S(2)}) collective-permute-start(bf16[512,2176]{1,0:T(8,128)(2,1)} %constant_dynamic-update-slice_fusion.1.cot_a), channel_id=1, source_target_pairs={{0,4},{4,0},{1,5},{5,1},{2,6},{6,2},{3,7},{7,3},{8,12},{12,8},{9,1... | collective-permute-start | bytes 6684680 | tf_op jit(solution)/shard_map/ppermute | solution.py:29
  323.3 51.2 %collective-permute-start.33 = (bf16[512,2176]{1,0:T(8,128)(2,1)}, bf16[512,2176]{1,0:T(8,128)(2,1)}, u32[]{:S(2)}, u32[]{:S(2)}) collective-permute-start(bf16[512,2176]{1,0:T(8,128)(2,1)} %pad_maximum_fusion.sec_a), channel_id=1, source_target_pairs={{0,8},{8,0},{16,24},{24,16},{1,9},{9,1},{17,25},{25,17},{2,10},{10... | collective-permute-start | bytes 6684680 | tf_op jit(solution)/shard_map/ppermute | solution.py:29
  325.8 50.1 %collective-permute-start.35 = (bf16[512,2176]{1,0:T(8,128)(2,1)}, bf16[512,2176]{1,0:T(8,128)(2,1)}, u32[]{:S(2)}, u32[]{:S(2)}) collective-permute-start(bf16[512,2176]{1,0:T(8,128)(2,1)} %collective-permute-done.24.cot_a), channel_id=1, source_target_pairs={{0,4},{4,0},{1,5},{5,1},{2,6},{6,2},{3,7},{7,3},{8,12},{12,8},{9,1... | collective-permute-start | bytes 6684680 | tf_op jit(solution)/shard_map/ppermute | solution.py:29
  374.4 51.2 %collective-permute-start.39 = (bf16[512,2176]{1,0:T(8,128)(2,1)}, bf16[512,2176]{1,0:T(8,128)(2,1)}, u32[]{:S(2)}, u32[]{:S(2)}) collective-permute-start(bf16[512,2176]{1,0:T(8,128)(2,1)} %pad_maximum_fusion.sec_a), channel_id=1, source_target_pairs={{0,16},{8,24},{16,0},{24,8},{1,17},{9,25},{17,1},{25,9},{2,18},{10... | collective-permute-start | bytes 6684680 | tf_op jit(solution)/shard_map/ppermute | solution.py:29
  425.6 52.1 %collective-permute-start.44 = (bf16[512,2176]{1,0:T(8,128)(2,1)}, bf16[512,2176]{1,0:T(8,128)(2,1)}, u32[]{:S(2)}, u32[]{:S(2)}) collective-permute-start(bf16[512,2176]{1,0:T(8,128)(2,1)} %pad_maximum_fusion.sec_a), channel_id=1, source_target_pairs={{0,24},{8,16},{16,8},{24,0},{1,25},{9,17},{17,9},{25,1},{2,26},{10... | collective-permute-start | bytes 6684680 | tf_op jit(solution)/shard_map/ppermute | solution.py:29
  478.2 50.7 %collective-permute-start.38 = (bf16[512,2176]{1,0:T(8,128)(2,1)}, bf16[512,2176]{1,0:T(8,128)(2,1)}, u32[]{:S(2)}, u32[]{:S(2)}) collective-permute-start(bf16[512,2176]{1,0:T(8,128)(2,1)} %add_convert_fusion.2), channel_id=1, source_target_pairs={{0,8},{8,0},{16,24},{24,16},{1,9},{9,1},{17,25},{25,17},{2,10},{10... | collective-permute-start | bytes 6684680 | tf_op jit(solution)/shard_map/ppermute | solution.py:29
  483.4 50.4 %collective-permute-start.43 = (bf16[512,2176]{1,0:T(8,128)(2,1)}, bf16[512,2176]{1,0:T(8,128)(2,1)}, u32[]{:S(2)}, u32[]{:S(2)}) collective-permute-start(bf16[512,2176]{1,0:T(8,128)(2,1)} %add_convert_fusion.1), channel_id=1, source_target_pairs={{0,16},{8,24},{16,0},{24,8},{1,17},{9,25},{17,1},{25,9},{2,18},{10... | collective-permute-start | bytes 6684680 | tf_op jit(solution)/shard_map/ppermute | solution.py:29
  485.1 118.1 %collective-permute-start.54 = (bf16[512,2176]{1,0:T(8,128)(2,1)}, bf16[512,2176]{1,0:T(8,128)(2,1)}, u32[]{:S(2)}, u32[]{:S(2)}) collective-permute-start(bf16[512,2176]{1,0:T(8,128)(2,1)} %get-tuple-element.283), channel_id=1, source_target_pairs={{0,4},{4,0},{1,5},{5,1},{2,6},{6,2},{3,7},{7,3},{8,12},{12,8},{9,1... | collective-permute-start | bytes 6684680 | tf_op jit(solution)/shard_map/ppermute | solution.py:29
  487.4 121.6 %collective-permute-start.50 = (bf16[512,2048]{1,0:T(8,128)(2,1)}, bf16[512,2048]{1,0:T(8,128)(2,1)}, u32[]{:S(2)}, u32[]{:S(2)}) collective-permute-start(bf16[512,2048]{1,0:T(8,128)(2,1)} %get-tuple-element.276), channel_id=1, source_target_pairs={{0,4},{4,0},{1,5},{5,1},{2,6},{6,2},{3,7},{7,3},{8,12},{12,8},{9,1... | collective-permute-start | bytes 6291464 | tf_op jit(solution)/shard_map/ppermute | solution.py:29
  551.2 51.9 %collective-permute-start.48 = (bf16[512,2176]{1,0:T(8,128)(2,1)}, bf16[512,2176]{1,0:T(8,128)(2,1)}, u32[]{:S(2)}, u32[]{:S(2)}) collective-permute-start(bf16[512,2176]{1,0:T(8,128)(2,1)} %add_convert_fusion), channel_id=1, source_target_pairs={{0,24},{8,16},{16,8},{24,0},{1,25},{9,17},{17,9},{25,1},{2,26},{10... | collective-permute-start | bytes 6684680 | tf_op jit(solution)/shard_map/ppermute | solution.py:29
  603.1 62.5 %collective-permute-start.52 = (bf16[512,2048]{1,0:T(8,128)(2,1)S(1)}, bf16[512,2048]{1,0:T(8,128)(2,1)S(1)}, u32[]{:S(2)}, u32[]{:S(2)}) collective-permute-start(bf16[512,2048]{1,0:T(8,128)(2,1)S(1)} %copy-done.67), channel_id=1, source_target_pairs={{0,4},{4,0},{1,5},{5,1},{2,6},{6,2},{3,7},{7,3},{8,12},{12,8},{9,1... | collective-permute-start | bytes 6291464 | tf_op jit(solution)/shard_map/ppermute | solution.py:29
  612.6 55.3 %collective-permute-start.49 = (bf16[512,2048]{1,0:T(8,128)(2,1)S(1)}, bf16[512,2048]{1,0:T(8,128)(2,1)S(1)}, u32[]{:S(2)}, u32[]{:S(2)}) collective-permute-start(bf16[512,2048]{1,0:T(8,128)(2,1)S(1)} %copy-done.23), channel_id=1, source_target_pairs={{0,8},{8,0},{16,24},{24,16},{1,9},{9,1},{17,25},{25,17},{2,10},{10... | collective-permute-start | bytes 6291464 | tf_op jit(solution)/shard_map/ppermute | solution.py:29
  613.2 54.7 %collective-permute-start.51 = (bf16[512,2048]{1,0:T(8,128)(2,1)S(1)}, bf16[512,2048]{1,0:T(8,128)(2,1)S(1)}, u32[]{:S(2)}, u32[]{:S(2)}) collective-permute-start(bf16[512,2048]{1,0:T(8,128)(2,1)S(1)} %add_convert_fusion.4), channel_id=1, source_target_pairs={{0,16},{8,24},{16,0},{24,8},{1,17},{9,25},{17,1},{25,9},{2,18},{10... | collective-permute-start | bytes 6291464 | tf_op jit(solution)/shard_map/ppermute | solution.py:29
  678.6 57.0 %collective-permute-start.53 = (bf16[512,2048]{1,0:T(8,128)(2,1)}, bf16[512,2048]{1,0:T(8,128)(2,1)}, u32[]{:S(2)}, u32[]{:S(2)}) collective-permute-start(bf16[512,2048]{1,0:T(8,128)(2,1)} %add_convert_fusion.3), channel_id=1, source_target_pairs={{0,24},{8,16},{16,8},{24,0},{1,25},{9,17},{17,9},{25,1},{2,26},{10... | collective-permute-start | bytes 6291464 | tf_op jit(solution)/shard_map/ppermute | solution.py:29
  682.2 120.5 %collective-permute-start.32 = (bf16[512,2048]{1,0:T(8,128)(2,1)}, bf16[512,2048]{1,0:T(8,128)(2,1)}, u32[]{:S(2)}, u32[]{:S(2)}) collective-permute-start(bf16[512,2048]{1,0:T(8,128)(2,1)} %get-tuple-element.241), channel_id=1, source_target_pairs={{0,4},{4,0},{1,5},{5,1},{2,6},{6,2},{3,7},{7,3},{8,12},{12,8},{9,1... | collective-permute-start | bytes 6291464 | tf_op jit(solution)/shard_map/ppermute | solution.py:29
  751.6 119.1 %all-to-all-start.5 = ((bf16[8,4,64,176]{3,2,1,0:T(8,128)(2,1)}), bf16[8,4,64,176]{3,2,1,0:T(8,128)(2,1)}, u32[]{:S(2)}, u32[]{:S(2)}) async-start(bf16[8,4,64,176]{3,2,1,0:T(8,128)(2,1)} %copy.267), calls=%async_computation.5 | async-start | bytes 2097152 | tf_op jit(solution)/shard_map/all_to_all | solution.py:840
  764.3 46.7 %collective-permute-start.66 = (bf16[512,2048]{1,0:T(8,128)(2,1)}, bf16[512,2048]{1,0:T(8,128)(2,1)}, u32[]{:S(2)}, u32[]{:S(2)}) collective-permute-start(bf16[512,2048]{1,0:T(8,128)(2,1)} %get-tuple-element.310), channel_id=1, source_target_pairs={{0,4},{4,0},{1,5},{5,1},{2,6},{6,2},{3,7},{7,3},{8,12},{12,8},{9,1... | collective-permute-start | bytes 6291464 | tf_op jit(solution)/shard_map/ppermute | solution.py:29
  798.8 65.7 %collective-permute-start.78 = (bf16[8,80,512]{2,1,0:T(8,128)(2,1)}, bf16[8,80,512]{2,1,0:T(8,128)(2,1)}, u32[]{:S(2)}, u32[]{:S(2)}) collective-permute-start(bf16[8,80,512]{2,1,0:T(8,128)(2,1)} %get-tuple-element.471), channel_id=1, source_target_pairs={{0,16},{8,24},{16,0},{24,8},{1,17},{9,25},{17,1},{25,9},{2,18},{10... | collective-permute-start | bytes 1966088 | tf_op jit(solution)/shard_map/ppermute | solution.py:29
  800.2 65.5 %collective-permute-start.77 = (bf16[8,80,512]{2,1,0:T(8,128)(2,1)}, bf16[8,80,512]{2,1,0:T(8,128)(2,1)}, u32[]{:S(2)}, u32[]{:S(2)}) collective-permute-start(bf16[8,80,512]{2,1,0:T(8,128)(2,1)} %get-tuple-element.472), channel_id=1, source_target_pairs={{0,8},{8,0},{16,24},{24,16},{1,9},{9,1},{17,25},{25,17},{2,10},{10... | collective-permute-start | bytes 1966088 | tf_op jit(solution)/shard_map/ppermute | solution.py:29
  865.7 56.0 %collective-permute-start.64 = (bf16[128,2048]{1,0:T(8,128)(2,1)}, bf16[128,2048]{1,0:T(8,128)(2,1)}, u32[]{:S(2)}, u32[]{:S(2)}) collective-permute-start(bf16[128,2048]{1,0:T(8,128)(2,1)} %get-tuple-element.480), channel_id=1, source_target_pairs={{0,2},{1,3},{2,0},{3,1},{4,6},{5,7},{6,4},{7,5},{8,10},{9,11},{10,... | collective-permute-start | bytes 1572872 | tf_op jit(solution)/shard_map/ppermute | solution.py:29
  865.8 56.6 %collective-permute-start.63 = (bf16[128,2048]{1,0:T(8,128)(2,1)}, bf16[128,2048]{1,0:T(8,128)(2,1)}, u32[]{:S(2)}, u32[]{:S(2)}) collective-permute-start(bf16[128,2048]{1,0:T(8,128)(2,1)} %get-tuple-element.481), channel_id=1, source_target_pairs={{0,1},{1,0},{2,3},{3,2},{4,5},{5,4},{6,7},{7,6},{8,9},{9,8},{10,11... | collective-permute-start | bytes 1572872 | tf_op jit(solution)/shard_map/ppermute | solution.py:29
  875.6 78.2 %all-to-all-start.4 = ((bf16[8,80,512]{2,1,0:T(8,128)(2,1)}), bf16[8,80,512]{2,1,0:T(8,128)(2,1)}, u32[]{:S(2)}, u32[]{:S(2)}) async-start(bf16[8,80,512]{2,1,0:T(8,128)(2,1)} %fusion.8), calls=%async_computation.4 | async-start | bytes 1310720 | tf_op jit(solution)/shard_map/all_to_all | solution.py:906
  (133 other events, 2145.3 us)

commit v2 on v1

--- a/solution.py
+++ b/solution.py
@@ -736,10 +736,8 @@
         near = [swap(own, "c", d) for d in range(1, c_size - 1)]
         return [own, *near, swap(after(own, *near), "c", c_size - 1)]
 
-    cot_groups = plane_groups(cot_own)
-    heads_low = after(
-        heads_to_tokens(after(heads_out, cot_own, shared_in)), full_out, *cot_groups[1:-1]
-    )
+    cot_groups = [cot_own] + [swap(cot_own, "c", d) for d in range(1, c_size)]
+    heads_low = after(heads_to_tokens(after(heads_out, cot_own, shared_in)), full_out)
     residual = tokens.astype(F32) + mm(heads_low, full_out)
     second_scale = rms_parts(residual)
     second_low = (residual * second_scale * post_gain).astype(BF)
@@ -750,7 +748,7 @@
     second_own = jnp.concatenate(
         gather_z(widen(second_low, jnp.concatenate([probs_high, probs_rest], axis=1))), axis=0
     )
-    second_own = after(second_own, cot_groups[-1])
+    second_own = after(second_own, *cot_groups[1:])
     second_groups = plane_groups(second_own)
     pair = lambda group: (group, swap(group, "k", 1))
     cot_groups = [pair(g) for g in cot_groups]
@@ -769,8 +767,11 @@
     for d in range(c_size):
         where = place.at[1].set(d)
         group = second_groups[d]
-        if d:
-            group = after(group, marks[max(d - 2, 0)])
+        if d == 1:
+            group, *second_groups[2:-1] = after_all([group, *second_groups[2:-1]], marks[0])
+        if d == c_size - 2:
+            second_groups[-1] = after(second_groups[-1], marks[d - 1])
+            where = after(where, second_groups[-1])
         if d > 1:
             where = after(where, out_sums[d - 2], sums[d - 1])
         results = list(
@@ -823,14 +824,6 @@
         return scatter_z([pick(summed, z ^ d) for d in range(z_size)])
 
     latent_sum = column_sum(latent_keep, after(latent_send, out_far))
-    out_plane = functools.reduce(
-        lambda total, block: total + block.astype(F32),
-        after_all([*out_near, out_far], latent_sum),
-        out_sums[0],
-    )
-    out_units = z_units(out_plane, rows)
-    out_units = out_units[:1] + [swap(unit.astype(BF), "z", d) for d, unit in enumerate(out_units) if d]
-    first_keep = after(first_keep, latent_sum)
     shared_in_grad = sum(sg_parts[1:], sg_parts[0])
     shared_in_grad = jnp.concatenate(
         [shared_in_grad[:width], shared_in_grad[wpad : wpad + width]], axis=0
@@ -870,9 +863,20 @@
     small_left = jnp.concatenate(
         [own_first_low, second_low, jnp.pad(gain_grads, ((0, 5), (0, 0))).astype(BF)], axis=0
     )
-    output_moved = [swap(block, "c", d) for d, block in enumerate(output_pieces) if d]
-    small_left = after(small_left, *output_moved)
+    output_near = [swap(output_pieces[d], "c", d) for d in range(1, c_size - 1)]
     small_pieces = core_pieces(mm_tn(small_left, small_right).astype(BF))
+    first_sum = column_sum(first_keep, first_send)
+    first_sum, *small_pieces = after_all([first_sum, *small_pieces], *output_near)
+    out_plane = functools.reduce(
+        lambda total, block: total + block.astype(F32),
+        after_all([*out_near, out_far], first_sum),
+        out_sums[0],
+    )
+    out_units = z_units(out_plane, rows)
+    out_units = out_units[:1] + [swap(unit.astype(BF), "z", d) for d, unit in enumerate(out_units) if d]
+    output_moved = [
+        *output_near, swap(after(output_pieces[-1], *output_near), "c", c_size - 1)
+    ]
     head_grad = head_grad.reshape(c_size, column_size, weight_rows + up_rows, kv_width)
     head_moved = [swap(pick(head_grad, c ^ d), "c", d) for d in range(1, c_size)]
     small_plane, _ = plane_sum(small_pieces, *head_moved)
@@ -882,24 +886,26 @@
         output_pieces[0],
     )
     shared_back = after(shared_back, small_plane)
+    shared_moved = [
+        swap(lax.dynamic_index_in_dim(shared_back, c ^ d, axis=1, keepdims=False), "c", d)
+        for d in range(1, c_size)
+    ]
+    first_grad = first_sum + first_own
+    out_sum = functools.reduce(
+        lambda total, block: total + block.astype(F32), after_all(out_units[1:], first_grad), out_units[0]
+    )
+    layer_out = (residual + out_sum).astype(BF)
+    first_norm_grad, _ = rms_back(own_values, own_scale, attn_gain, first_grad)
+    tokens_grad = residual_grad + first_norm_grad
+    own_both = z_sum(jnp.concatenate([output_plane, small_plane], axis=1))
+    own_output, own_small = own_both[:, :D], own_both[:, D:]
     shared_back = in_order(
         [
-            swap(lax.dynamic_index_in_dim(shared_back, c ^ d, axis=1, keepdims=False), "c", d)
-            if d
-            else lax.dynamic_index_in_dim(shared_back, c, axis=1, keepdims=False)
-            for d in range(c_size)
+            lax.dynamic_index_in_dim(shared_back, c, axis=1, keepdims=False),
+            *after_all(shared_moved, own_both),
         ],
         c,
     ).reshape(device_count, weight_rows, 2 * width).transpose(1, 0, 2)
-    first_grad = after(column_sum(first_keep, first_send), small_plane) + first_own
-    out_sum = functools.reduce(
-        lambda total, block: total + block.astype(F32), after_all(out_units[1:], first_grad), out_units[0]
-    )
-    layer_out = (residual + out_sum).astype(BF)
-    first_norm_grad, _ = rms_back(own_values, own_scale, attn_gain, first_grad)
-    tokens_grad = residual_grad + first_norm_grad
-    own_small = z_sum(small_plane)
-    own_output = z_sum(output_plane)
     head_sum = pick(head_grad, c).astype(F32)
     for block in after_all(head_moved, small_plane):
         head_sum = head_sum + block.astype(F32)

time: 966 us -> 940 us (0.973)
  starting transfers between devices: 148 us -> 133 us
    ppermute x89 -> x86, starting transfers between devices: 120 us -> 106 us  [swap(): return lax.ppermute(block, axis, [(i, i ^ distance) for i in range(n)])]
    ppermute x89 -> x86, waiting for transfers between devices: 321 us -> 316 us  [swap(): return lax.ppermute(block, axis, [(i, i ^ distance) for i in range(n)])]
  transfers between devices with their start and end apart: 95 -> 92, of which waited for: 34 -> 35; matrix products, arithmetic and copies ran while one was open for 28% -> 28% of each run, Pallas kernels for 18% -> 15%
where the time goes in v2:
time: 940 us; the launch traced here: 935 us
  waiting for transfers between devices  322 us (34%)
  Pallas kernels  177 us (19%)
  local copies, waits for them, and re-layouts  150 us (16%)
  starting transfers between devices  133 us (14%)
  other arithmetic  88.4 us (9%)
  matrix products  61.5 us (7%)
    ppermute x86, waiting for transfers between devices, swap(): return lax.ppermute(block, axis, [(i, i ^ distance) for i in range(n)])  316 us
    pallas_call x4, Pallas kernels, expert_group(): pl.pallas_call(functools.partial(expert_kernel, local_experts, capacity,...  139 us
    ppermute x86, starting transfers between devices, swap(): return lax.ppermute(block, axis, [(i, i ^ distance) for i in range(n)])  106 us
    dynamic_update_slice x32, local copies, waits for them, and re-layouts, put(): return lax.dynamic_update_slice_in_dim(buffer, block[None], index, axis=0)  48.2 us
    dot_general x3, matrix products, on_device(): ein = lambda spec, a, b: jnp.einsum(spec, a, b, preferred_element_type=F32)  37.8 us
    dot_general x7, matrix products, dot(): return lax.dot_general(a, b, (dims, ((), ())), preferred_element_type=F32)  23.7 us
    pallas_call x1, Pallas kernels, attend_back(): pl.pallas_call(functools.partial(attend_back_kernel, heads), out_shape=sh...  20.4 us
  transfers between devices with their start and end apart: 92, of which 35 were waited for; matrix products, arithmetic and copies ran while one was open for 28% of the time, Pallas kernels for 15%

profile of v2, /device:TPU:0, one launch (start us, length us, event | category | flops | bytes accessed | tf_op | source)
XLA Modules:
  0.0 934.7 jit_solution(17703377131996529789)
XLA Ops:
  56.3 9.6 %collective-permute-done.9 = bf16[4,72,640]{2,1,0:T(8,128)(2,1)S(1)} collective-permute-done((bf16[4,72,640]{2,1,0:T(8,128)(2,1)S(1)}, bf16[4,72,640]{2,1,0:T(8,128)(2,1)S(1)}, u32[]{:S(2)}, u32[]{:S(2)}) %collective-permute-start.9) | collective-permute-done | bytes 368672 | tf_op jit(solution)/shard_map/ppermute | solution.py:29
  84.7 19.2 %collective-permute-done.1 = bf16[128,2176]{1,0:T(8,128)(2,1)S(1)} collective-permute-done((bf16[128,2176]{1,0:T(8,128)(2,1)S(1)}, bf16[128,2176]{1,0:T(8,128)(2,1)S(1)}, u32[]{:S(2)}, u32[]{:S(2)}) %collective-permute-start.1) | collective-permute-done | bytes 557088 | tf_op jit(solution)/shard_map/ppermute | solution.py:29
  149.9 17.2 %shard_map.297 = (bf16[1024,256]{1,0:T(8,128)(2,1)}, bf16[1024,2048]{1,0:T(8,128)(2,1)}, bf16[1024,384]{1,0:T(8,128)(2,1)}, bf16[1024,512]{1,0:T(8,128)(2,1)}, b...) custom-call(s32[2]{0:T(128)} %pad_add_fusion.place, bf16[1024,2176]{1,0:T(8,128)(2,1)} %bitcast.20.seq, ...), custom_call_target="tpu_custom_call" | custom-call | flops 1048576 | bytes 65536 | tf_op jit(solution)/shard_map/pallas_call | solution.py:481
  167.6 15.4 %collective-permute-done.15 = bf16[128,2176]{1,0:T(8,128)(2,1)} collective-permute-done((bf16[128,2176]{1,0:T(8,128)(2,1)}, bf16[128,2176]{1,0:T(8,128)(2,1)}, u32[]{:S(2)}, u32[]{:S(2)}) %collective-permute-start.15) | collective-permute-done | bytes 557088 | tf_op jit(solution)/shard_map/ppermute | solution.py:29
  242.1 15.7 %collective-permute-done.26 = bf16[128,2176]{1,0:T(8,128)(2,1)S(1)} collective-permute-done((bf16[128,2176]{1,0:T(8,128)(2,1)S(1)}, bf16[128,2176]{1,0:T(8,128)(2,1)S(1)}, u32[]{:S(2)}, u32[]{:S(2)}) %collective-permute-start.26) | collective-permute-done | bytes 557088 | tf_op jit(solution)/shard_map/ppermute | solution.py:29
  257.8 21.9 %collective-permute-start.24 = (bf16[128,2176]{1,0:T(8,128)(2,1)S(1)}, bf16[128,2176]{1,0:T(8,128)(2,1)S(1)}, u32[]{:S(2)}, u32[]{:S(2)}) collective-permute-start(bf16[128,2176]{1,0:T(8,128)(2,1)S(1)} %pad_maximum_fusion.5), channel_id=1, source_target_pairs={{0,1},{1,0},{2,3},{3,2},{4,5},{5,4},{6,7},{7,6},{8,9},{9,8},{10,11... | collective-permute-start | bytes 1671176 | tf_op jit(solution)/shard_map/ppermute | solution.py:29
  279.7 10.5 %collective-permute-done.25 = bf16[128,2176]{1,0:T(8,128)(2,1)S(1)} collective-permute-done((bf16[128,2176]{1,0:T(8,128)(2,1)S(1)}, bf16[128,2176]{1,0:T(8,128)(2,1)S(1)}, u32[]{:S(2)}, u32[]{:S(2)}) %collective-permute-start.25) | collective-permute-done | bytes 557088 | tf_op jit(solution)/shard_map/ppermute | solution.py:29
  290.2 11.7 %collective-permute-done.24 = bf16[128,2176]{1,0:T(8,128)(2,1)S(1)} collective-permute-done((bf16[128,2176]{1,0:T(8,128)(2,1)S(1)}, bf16[128,2176]{1,0:T(8,128)(2,1)S(1)}, u32[]{:S(2)}, u32[]{:S(2)}) %collective-permute-start.24) | collective-permute-done | bytes 557088 | tf_op jit(solution)/shard_map/ppermute | solution.py:29
  316.9 35.0 %shard_map.298 = (bf16[2,2048,2048]{2,1,0:T(8,128)(2,1)}, bf16[2,2048,2048]{2,1,0:T(8,128)(2,1)}, bf16[2,2048,352]{2,1,0:T(8,128)(2,1)}, bf16[2,2048,352]{2,1,0:...) custom-call(s32[2]{0:T(128)} %copy-done.80, ...), custom_call_target="tpu_custom_call" | custom-call | flops 1048576 | bytes 65536 | tf_op jit(solution)/shard_map/pallas_call | solution.py:375
  351.9 11.5 %collective-permute-done.34.sec_a = bf16[512,2176]{1,0:T(8,128)(2,1)} collective-permute-done((bf16[512,2176]{1,0:T(8,128)(2,1)}, bf16[512,2176]{1,0:T(8,128)(2,1)}, u32[]{:S(2)}, u32[]{:S(2)}) %collective-permute-start.34) | collective-permute-done | bytes 2228256 | tf_op jit(solution)/shard_map/ppermute | solution.py:29
  369.2 34.5 %shard_map.299 = (bf16[2,2048,2048]{2,1,0:T(8,128)(2,1)}, bf16[2,2048,2048]{2,1,0:T(8,128)(2,1)}, bf16[2,2048,352]{2,1,0:T(8,128)(2,1)}, bf16[2,2048,352]{2,1,0:...) custom-call(s32[2]{0:T(128)} %copy-done.75, ...), custom_call_target="tpu_custom_call", output_to_operand_aliasing={{0}: (10, {}), {1}: (11, {}), {2}: (12, {}), {3}: (13, {}),... | custom-call | flops 1048576 | bytes 65536 | tf_op jit(solution)/shard_map/pallas_call | solution.py:375
  404.5 12.2 %collective-permute-done.40.sec_a = bf16[512,2176]{1,0:T(8,128)(2,1)} collective-permute-done((bf16[512,2176]{1,0:T(8,128)(2,1)}, bf16[512,2176]{1,0:T(8,128)(2,1)}, u32[]{:S(2)}, u32[]{:S(2)}) %collective-permute-start.40) | collective-permute-done | bytes 2228256 | tf_op jit(solution)/shard_map/ppermute | solution.py:29
  420.2 34.7 %shard_map.300 = (bf16[2,2048,2048]{2,1,0:T(8,128)(2,1)}, bf16[2,2048,2048]{2,1,0:T(8,128)(2,1)}, bf16[2,2048,352]{2,1,0:T(8,128)(2,1)}, bf16[2,2048,352]{2,1,0:...) custom-call(s32[2]{0:T(128)} %copy-done.74, ...), custom_call_target="tpu_custom_call", output_to_operand_aliasing={{0}: (10, {}), {1}: (11, {}), {2}: (12, {}), {3}: (13, {}),... | custom-call | flops 1048576 | bytes 65536 | tf_op jit(solution)/shard_map/pallas_call | solution.py:375
  470.6 34.9 %shard_map.301 = (bf16[2,2048,2048]{2,1,0:T(8,128)(2,1)}, bf16[2,2048,2048]{2,1,0:T(8,128)(2,1)}, bf16[2,2048,352]{2,1,0:T(8,128)(2,1)}, bf16[2,2048,352]{2,1,0:...) custom-call(s32[2]{0:T(128)} %copy-done.73, ...), custom_call_target="tpu_custom_call", output_to_operand_aliasing={{0}: (10, {}), {1}: (11, {}), {2}: (12, {}), {3}: (13, {}),... | custom-call | flops 1048576 | bytes 65536 | tf_op jit(solution)/shard_map/pallas_call | solution.py:375
  506.7 9.7 %collective-permute-done.44 = bf16[512,2176]{1,0:T(8,128)(2,1)} collective-permute-done((bf16[512,2176]{1,0:T(8,128)(2,1)}, bf16[512,2176]{1,0:T(8,128)(2,1)}, u32[]{:S(2)}, u32[]{:S(2)}) %collective-permute-start.44) | collective-permute-done | bytes 2228256 | tf_op jit(solution)/shard_map/ppermute | solution.py:29
  516.3 12.4 %fusion.93 = f32[2,2048,352]{1,2,0:T(8,128)} fusion(bf16[2,2048,2048]{2,1,0:T(8,128)(2,1)} %get-tuple-element.297, bf16[2,2048,352]{2,1,0:T(8,128)(2,1)} %get-tuple-element.298), kind=kOutput, calls=%fused_computation.257 | convolution fusion | flops 5905580032 | bytes 25427968 | tf_op jit(solution)/shard_map/esf,esd->efd/dot_general | solution.py:797
  535.1 12.6 %fusion.94 = f32[2,2048,352]{1,2,0:T(8,128)} fusion(bf16[2,2048,2048]{2,1,0:T(8,128)(2,1)} %get-tuple-element.297, bf16[2,2048,352]{2,1,0:T(8,128)(2,1)S(1)} %copy-done.2), kind=kOutput, calls=%fused_computation.258 | convolution fusion | flops 5905580032 | bytes 25427968 | tf_op jit(solution)/shard_map/esf,esd->efd/dot_general | solution.py:797
  547.6 12.9 %fusion.92 = f32[2,352,2048]{2,1,0:T(8,128)} fusion(bf16[2,2048,352]{2,1,0:T(8,128)(2,1)S(1)} %copy-done, bf16[2,2048,2048]{2,1,0:T(8,128)(2,1)} %get-tuple-element.296), kind=kOutput, calls=%fused_computation.256 | convolution fusion | flops 5905580032 | bytes 25427968 | tf_op jit(solution)/shard_map/esf,esd->efd/dot_general | solution.py:797
  560.5 25.2 %collective-permute-done.48 = bf16[512,2176]{1,0:T(8,128)(2,1)} collective-permute-done((bf16[512,2176]{1,0:T(8,128)(2,1)}, bf16[512,2176]{1,0:T(8,128)(2,1)}, u32[]{:S(2)}, u32[]{:S(2)}) %collective-permute-start.48) | collective-permute-done | bytes 2228256 | tf_op jit(solution)/shard_map/ppermute | solution.py:29
  609.0 11.5 %collective-permute-done.57 = bf16[128,2176]{1,0:T(8,128)(2,1)S(1)} collective-permute-done((bf16[128,2176]{1,0:T(8,128)(2,1)S(1)}, bf16[128,2176]{1,0:T(8,128)(2,1)S(1)}, u32[]{:S(2)}, u32[]{:S(2)}) %collective-permute-start.57) | collective-permute-done | bytes 557088 | tf_op jit(solution)/shard_map/ppermute | solution.py:29
  620.5 28.3 %collective-permute-done.56 = bf16[128,2176]{1,0:T(8,128)(2,1)S(1)} collective-permute-done((bf16[128,2176]{1,0:T(8,128)(2,1)S(1)}, bf16[128,2176]{1,0:T(8,128)(2,1)S(1)}, u32[]{:S(2)}, u32[]{:S(2)}) %collective-permute-start.56) | collective-permute-done | bytes 557088 | tf_op jit(solution)/shard_map/ppermute | solution.py:29
  663.3 7.1 convolution_convert_fusion.2
  684.5 7.2 fusion.2
  696.1 20.4 %shard_map.302 = (f32[1,2048]{1,0:T(1,128)}, bf16[512,2048]{1,0:T(8,128)(2,1)}, bf16[512,2048]{1,0:T(8,128)(2,1)}, bf16[512,640]{1,0:T(8,128)(2,1)}, bf16[512,64...) custom-call(s32[2]{0:T(128)} %pad_add_fusion.place, bf16[1024,256]{1,0:T(8,128)(2,1)} %bitcast.73.grad, ...), custom_call_target="tpu_custom_call" | custom-call | flops 1048576 | bytes 65536 | tf_op jit(solution)/shard_map/pallas_call | solution.py:569
  731.9 7.4 collective-permute-done.65
  773.1 7.3 collective-permute-done.60
  782.6 34.4 %collective-permute-done.61 = bf16[128,2048]{1,0:T(8,128)(2,1)} collective-permute-done((bf16[128,2048]{1,0:T(8,128)(2,1)}, bf16[128,2048]{1,0:T(8,128)(2,1)}, u32[]{:S(2)}, u32[]{:S(2)}) %collective-permute-start.61) | collective-permute-done | bytes 524320 | tf_op jit(solution)/shard_map/ppermute | solution.py:29
  822.4 6.6 fusion.86
  835.8 12.3 %collective-permute-done.74 = bf16[256,640]{1,0:T(8,128)(2,1)S(1)} collective-permute-done((bf16[256,640]{1,0:T(8,128)(2,1)S(1)}, bf16[256,640]{1,0:T(8,128)(2,1)S(1)}, u32[]{:S(2)}, u32[]{:S(2)}) %collective-permute-start.74) | collective-permute-done | bytes 327712 | tf_op jit(solution)/shard_map/ppermute | solution.py:29
  873.5 12.3 %collective-permute-done.71 = bf16[128,2048]{1,0:T(8,128)(2,1)} collective-permute-done((bf16[128,2048]{1,0:T(8,128)(2,1)}, bf16[128,2048]{1,0:T(8,128)(2,1)}, u32[]{:S(2)}, u32[]{:S(2)}) %collective-permute-start.71) | collective-permute-done | bytes 524320 | tf_op jit(solution)/shard_map/ppermute | solution.py:29
  890.4 8.2 collective-permute-done.80
  899.9 18.7 %collective-permute-done.81 = bf16[64,2688]{1,0:T(8,128)(2,1)S(1)} collective-permute-done((bf16[64,2688]{1,0:T(8,128)(2,1)S(1)}, bf16[64,2688]{1,0:T(8,128)(2,1)S(1)}, u32[]{:S(2)}, u32[]{:S(2)}) %collective-permute-start.81) | collective-permute-done | bytes 344096 | tf_op jit(solution)/shard_map/ppermute | solution.py:29
  (562 shorter events, 393.8 us)
Async XLA Ops:
  104.8 78.3 %all-to-all-start.1 = ((bf16[32,64,176]{2,1,0:T(8,128)(2,1)}), bf16[32,64,176]{2,1,0:T(8,128)(2,1)}, u32[]{:S(2)}, u32[]{:S(2)}) async-start(bf16[32,64,176]{2,1,0:T(8,128)(2,1)} %maximum_bitcast_fusion), calls=%async_computation.1 | async-start | bytes 2097152 | tf_op jit(solution)/shard_map/all_to_all | solution.py:685
  109.1 57.9 %collective-permute-start.16 = (bf16[128,2176]{1,0:T(8,128)(2,1)}, bf16[128,2176]{1,0:T(8,128)(2,1)}, u32[]{:S(2)}, u32[]{:S(2)}) collective-permute-start(bf16[128,2176]{1,0:T(8,128)(2,1)} %pad_maximum_fusion.4), channel_id=1, source_target_pairs={{0,3},{1,2},{2,1},{3,0},{4,7},{5,6},{6,5},{7,4},{8,11},{9,10},{10,... | collective-permute-start | bytes 1671176 | tf_op jit(solution)/shard_map/ppermute | solution.py:29
  112.7 70.3 %collective-permute-start.15 = (bf16[128,2176]{1,0:T(8,128)(2,1)}, bf16[128,2176]{1,0:T(8,128)(2,1)}, u32[]{:S(2)}, u32[]{:S(2)}) collective-permute-start(bf16[128,2176]{1,0:T(8,128)(2,1)} %pad_maximum_fusion.4), channel_id=1, source_target_pairs={{0,2},{1,3},{2,0},{3,1},{4,6},{5,7},{6,4},{7,5},{8,10},{9,11},{10,... | collective-permute-start | bytes 1671176 | tf_op jit(solution)/shard_map/ppermute | solution.py:29
  112.8 70.3 %collective-permute-start.14 = (bf16[128,2176]{1,0:T(8,128)(2,1)}, bf16[128,2176]{1,0:T(8,128)(2,1)}, u32[]{:S(2)}, u32[]{:S(2)}) collective-permute-start(bf16[128,2176]{1,0:T(8,128)(2,1)} %pad_maximum_fusion.4), channel_id=1, source_target_pairs={{0,1},{1,0},{2,3},{3,2},{4,5},{5,4},{6,7},{7,6},{8,9},{9,8},{10,11... | collective-permute-start | bytes 1671176 | tf_op jit(solution)/shard_map/ppermute | solution.py:29
  129.3 61.8 %collective-permute-start.22 = (bf16[4,64,2048]{2,1,0:T(8,128)(2,1)}, bf16[4,64,2048]{2,1,0:T(8,128)(2,1)}, u32[]{:S(2)}, u32[]{:S(2)}) collective-permute-start(bf16[4,64,2048]{2,1,0:T(8,128)(2,1)} %bitcast_dynamic-update-slice_fusion.24), channel_id=1, source_target_pairs={{0,24},{8,16},{16,8},{24,0},{1,25},{9,17},{17,9},{25,1},{2,26},{10... | collective-permute-start | bytes 3145736 | tf_op jit(solution)/shard_map/ppermute | solution.py:29
  146.2 44.9 %collective-permute-start.21 = (bf16[4,64,2048]{2,1,0:T(8,128)(2,1)}, bf16[4,64,2048]{2,1,0:T(8,128)(2,1)S(1)}, u32[]{:S(2)}, u32[]{:S(2)}) collective-permute-start(bf16[4,64,2048]{2,1,0:T(8,128)(2,1)} %bitcast_dynamic-update-slice_fusion.24), channel_id=1, source_target_pairs={{0,16},{8,24},{16,0},{24,8},{1,17},{9,25},{17,1},{25,9},{2,18},{10... | collective-permute-start | bytes 3145736 | tf_op jit(solution)/shard_map/ppermute | solution.py:29
  212.2 93.9 %collective-permute-start.29 = (bf16[512,2176]{1,0:T(8,128)(2,1)}, bf16[512,2176]{1,0:T(8,128)(2,1)}, u32[]{:S(2)}, u32[]{:S(2)}) collective-permute-start(bf16[512,2176]{1,0:T(8,128)(2,1)} %constant_dynamic-update-slice_fusion.1.cot_a), channel_id=1, source_target_pairs={{0,24},{8,16},{16,8},{24,0},{1,25},{9,17},{17,9},{25,1},{2,26},{10... | collective-permute-start | bytes 6684680 | tf_op jit(solution)/shard_map/ppermute | solution.py:29
  214.5 97.5 %collective-permute-start.28 = (bf16[512,2176]{1,0:T(8,128)(2,1)}, bf16[512,2176]{1,0:T(8,128)(2,1)}, u32[]{:S(2)}, u32[]{:S(2)}) collective-permute-start(bf16[512,2176]{1,0:T(8,128)(2,1)} %constant_dynamic-update-slice_fusion.1.cot_a), channel_id=1, source_target_pairs={{0,16},{8,24},{16,0},{24,8},{1,17},{9,25},{17,1},{25,9},{2,18},{10... | collective-permute-start | bytes 6684680 | tf_op jit(solution)/shard_map/ppermute | solution.py:29
  215.1 97.1 %collective-permute-start.27 = (bf16[512,2176]{1,0:T(8,128)(2,1)}, bf16[512,2176]{1,0:T(8,128)(2,1)}, u32[]{:S(2)}, u32[]{:S(2)}) collective-permute-start(bf16[512,2176]{1,0:T(8,128)(2,1)} %constant_dynamic-update-slice_fusion.1.cot_a), channel_id=1, source_target_pairs={{0,8},{8,0},{16,24},{24,16},{1,9},{9,1},{17,25},{25,17},{2,10},{10... | collective-permute-start | bytes 6684680 | tf_op jit(solution)/shard_map/ppermute | solution.py:29
  242.1 48.1 %collective-permute-start.25 = (bf16[128,2176]{1,0:T(8,128)(2,1)S(1)}, bf16[128,2176]{1,0:T(8,128)(2,1)S(1)}, u32[]{:S(2)}, u32[]{:S(2)}) collective-permute-start(bf16[128,2176]{1,0:T(8,128)(2,1)S(1)} %pad_maximum_fusion.5), channel_id=1, source_target_pairs={{0,2},{1,3},{2,0},{3,1},{4,6},{5,7},{6,4},{7,5},{8,10},{9,11},{10,... | collective-permute-start | bytes 1671176 | tf_op jit(solution)/shard_map/ppermute | solution.py:29
  312.2 51.2 %collective-permute-start.34 = (bf16[512,2176]{1,0:T(8,128)(2,1)}, bf16[512,2176]{1,0:T(8,128)(2,1)}, u32[]{:S(2)}, u32[]{:S(2)}) collective-permute-start(bf16[512,2176]{1,0:T(8,128)(2,1)} %pad_maximum_fusion.1.sec_a), channel_id=1, source_target_pairs={{0,16},{8,24},{16,0},{24,8},{1,17},{9,25},{17,1},{25,9},{2,18},{10... | collective-permute-start | bytes 6684680 | tf_op jit(solution)/shard_map/ppermute | solution.py:29
  313.6 50.8 %collective-permute-start.33 = (bf16[512,2176]{1,0:T(8,128)(2,1)}, bf16[512,2176]{1,0:T(8,128)(2,1)}, u32[]{:S(2)}, u32[]{:S(2)}) collective-permute-start(bf16[512,2176]{1,0:T(8,128)(2,1)} %pad_maximum_fusion.1.sec_a), channel_id=1, source_target_pairs={{0,8},{8,0},{16,24},{24,16},{1,9},{9,1},{17,25},{25,17},{2,10},{10... | collective-permute-start | bytes 6684680 | tf_op jit(solution)/shard_map/ppermute | solution.py:29
  315.3 50.6 %collective-permute-start.36 = (bf16[512,2176]{1,0:T(8,128)(2,1)}, bf16[512,2176]{1,0:T(8,128)(2,1)}, u32[]{:S(2)}, u32[]{:S(2)}) collective-permute-start(bf16[512,2176]{1,0:T(8,128)(2,1)} %collective-permute-done.27.cot_a), channel_id=1, source_target_pairs={{0,4},{4,0},{1,5},{5,1},{2,6},{6,2},{3,7},{7,3},{8,12},{12,8},{9,1... | collective-permute-start | bytes 6684680 | tf_op jit(solution)/shard_map/ppermute | solution.py:29
  364.5 52.1 %collective-permute-start.40 = (bf16[512,2176]{1,0:T(8,128)(2,1)}, bf16[512,2176]{1,0:T(8,128)(2,1)}, u32[]{:S(2)}, u32[]{:S(2)}) collective-permute-start(bf16[512,2176]{1,0:T(8,128)(2,1)} %pad_maximum_fusion.1.sec_a), channel_id=1, source_target_pairs={{0,24},{8,16},{16,8},{24,0},{1,25},{9,17},{17,9},{25,1},{2,26},{10... | collective-permute-start | bytes 6684680 | tf_op jit(solution)/shard_map/ppermute | solution.py:29
  455.9 50.7 %collective-permute-start.39 = (bf16[512,2176]{1,0:T(8,128)(2,1)}, bf16[512,2176]{1,0:T(8,128)(2,1)}, u32[]{:S(2)}, u32[]{:S(2)}) collective-permute-start(bf16[512,2176]{1,0:T(8,128)(2,1)} %add_convert_fusion.2), channel_id=1, source_target_pairs={{0,8},{8,0},{16,24},{24,16},{1,9},{9,1},{17,25},{25,17},{2,10},{10... | collective-permute-start | bytes 6684680 | tf_op jit(solution)/shard_map/ppermute | solution.py:29
  465.5 50.8 %collective-permute-start.44 = (bf16[512,2176]{1,0:T(8,128)(2,1)}, bf16[512,2176]{1,0:T(8,128)(2,1)}, u32[]{:S(2)}, u32[]{:S(2)}) collective-permute-start(bf16[512,2176]{1,0:T(8,128)(2,1)} %add_convert_fusion.1), channel_id=1, source_target_pairs={{0,16},{8,24},{16,0},{24,8},{1,17},{9,25},{17,1},{25,9},{2,18},{10... | collective-permute-start | bytes 6684680 | tf_op jit(solution)/shard_map/ppermute | solution.py:29
  467.9 117.8 %collective-permute-start.54 = (bf16[512,2176]{1,0:T(8,128)(2,1)}, bf16[512,2176]{1,0:T(8,128)(2,1)}, u32[]{:S(2)}, u32[]{:S(2)}) collective-permute-start(bf16[512,2176]{1,0:T(8,128)(2,1)} %get-tuple-element.289), channel_id=1, source_target_pairs={{0,4},{4,0},{1,5},{5,1},{2,6},{6,2},{3,7},{7,3},{8,12},{12,8},{9,1... | collective-permute-start | bytes 6684680 | tf_op jit(solution)/shard_map/ppermute | solution.py:29
  470.2 122.6 %collective-permute-start.50 = (bf16[512,2048]{1,0:T(8,128)(2,1)}, bf16[512,2048]{1,0:T(8,128)(2,1)}, u32[]{:S(2)}, u32[]{:S(2)}) collective-permute-start(bf16[512,2048]{1,0:T(8,128)(2,1)} %get-tuple-element.282), channel_id=1, source_target_pairs={{0,4},{4,0},{1,5},{5,1},{2,6},{6,2},{3,7},{7,3},{8,12},{12,8},{9,1... | collective-permute-start | bytes 6291464 | tf_op jit(solution)/shard_map/ppermute | solution.py:29
  533.7 51.9 %collective-permute-start.48 = (bf16[512,2176]{1,0:T(8,128)(2,1)}, bf16[512,2176]{1,0:T(8,128)(2,1)}, u32[]{:S(2)}, u32[]{:S(2)}) collective-permute-start(bf16[512,2176]{1,0:T(8,128)(2,1)} %add_convert_fusion), channel_id=1, source_target_pairs={{0,24},{8,16},{16,8},{24,0},{1,25},{9,17},{17,9},{25,1},{2,26},{10... | collective-permute-start | bytes 6684680 | tf_op jit(solution)/shard_map/ppermute | solution.py:29
  585.7 63.3 %collective-permute-start.52 = (bf16[512,2048]{1,0:T(8,128)(2,1)S(1)}, bf16[512,2048]{1,0:T(8,128)(2,1)S(1)}, u32[]{:S(2)}, u32[]{:S(2)}) collective-permute-start(bf16[512,2048]{1,0:T(8,128)(2,1)S(1)} %copy-done.81), channel_id=1, source_target_pairs={{0,4},{4,0},{1,5},{5,1},{2,6},{6,2},{3,7},{7,3},{8,12},{12,8},{9,1... | collective-permute-start | bytes 6291464 | tf_op jit(solution)/shard_map/ppermute | solution.py:29
  595.5 55.7 %collective-permute-start.49 = (bf16[512,2048]{1,0:T(8,128)(2,1)S(1)}, bf16[512,2048]{1,0:T(8,128)(2,1)S(1)}, u32[]{:S(2)}, u32[]{:S(2)}) collective-permute-start(bf16[512,2048]{1,0:T(8,128)(2,1)S(1)} %copy-done.24), channel_id=1, source_target_pairs={{0,8},{8,0},{16,24},{24,16},{1,9},{9,1},{17,25},{25,17},{2,10},{10... | collective-permute-start | bytes 6291464 | tf_op jit(solution)/shard_map/ppermute | solution.py:29
  596.4 54.7 %collective-permute-start.51 = (bf16[512,2048]{1,0:T(8,128)(2,1)S(1)}, bf16[512,2048]{1,0:T(8,128)(2,1)S(1)}, u32[]{:S(2)}, u32[]{:S(2)}) collective-permute-start(bf16[512,2048]{1,0:T(8,128)(2,1)S(1)} %add_convert_fusion.4), channel_id=1, source_target_pairs={{0,16},{8,24},{16,0},{24,8},{1,17},{9,25},{17,1},{25,9},{2,18},{10... | collective-permute-start | bytes 6291464 | tf_op jit(solution)/shard_map/ppermute | solution.py:29
  661.7 54.8 %collective-permute-start.53 = (bf16[512,2048]{1,0:T(8,128)(2,1)}, bf16[512,2048]{1,0:T(8,128)(2,1)}, u32[]{:S(2)}, u32[]{:S(2)}) collective-permute-start(bf16[512,2048]{1,0:T(8,128)(2,1)} %add_convert_fusion.3), channel_id=1, source_target_pairs={{0,24},{8,16},{16,8},{24,0},{1,25},{9,17},{17,9},{25,1},{2,26},{10... | collective-permute-start | bytes 6291464 | tf_op jit(solution)/shard_map/ppermute | solution.py:29
  684.1 136.9 %collective-permute-start.32 = (bf16[512,2048]{1,0:T(8,128)(2,1)}, bf16[512,2048]{1,0:T(8,128)(2,1)}, u32[]{:S(2)}, u32[]{:S(2)}) collective-permute-start(bf16[512,2048]{1,0:T(8,128)(2,1)} %get-tuple-element.246), channel_id=1, source_target_pairs={{0,4},{4,0},{1,5},{5,1},{2,6},{6,2},{3,7},{7,3},{8,12},{12,8},{9,1... | collective-permute-start | bytes 6291464 | tf_op jit(solution)/shard_map/ppermute | solution.py:29
  756.6 60.4 %collective-permute-start.61 = (bf16[128,2048]{1,0:T(8,128)(2,1)}, bf16[128,2048]{1,0:T(8,128)(2,1)}, u32[]{:S(2)}, u32[]{:S(2)}) collective-permute-start(bf16[128,2048]{1,0:T(8,128)(2,1)} %get-tuple-element.478), channel_id=1, source_target_pairs={{0,2},{1,3},{2,0},{3,1},{4,6},{5,7},{6,4},{7,5},{8,10},{9,11},{10,... | collective-permute-start | bytes 1572872 | tf_op jit(solution)/shard_map/ppermute | solution.py:29
  763.7 89.7 %all-to-all-start.5 = ((bf16[8,4,64,176]{3,2,1,0:T(8,128)(2,1)}), bf16[8,4,64,176]{3,2,1,0:T(8,128)(2,1)}, u32[]{:S(2)}, u32[]{:S(2)}) async-start(bf16[8,4,64,176]{3,2,1,0:T(8,128)(2,1)} %copy.268), calls=%async_computation.5 | async-start | bytes 2097152 | tf_op jit(solution)/shard_map/all_to_all | solution.py:833
  769.9 60.5 %collective-permute-start.79 = (bf16[8,80,512]{2,1,0:T(8,128)(2,1)S(1)}, bf16[8,80,512]{2,1,0:T(8,128)(2,1)S(1)}, u32[]{:S(2)}, u32[]{:S(2)}) collective-permute-start(bf16[8,80,512]{2,1,0:T(8,128)(2,1)S(1)} %get-tuple-element.486), channel_id=1, source_target_pairs={{0,24},{8,16},{16,8},{24,0},{1,25},{9,17},{17,9},{25,1},{2,26},{10... | collective-permute-start | bytes 1966088 | tf_op jit(solution)/shard_map/ppermute | solution.py:29
  780.5 50.7 %collective-permute-start.78 = (bf16[8,80,512]{2,1,0:T(8,128)(2,1)S(1)}, bf16[8,80,512]{2,1,0:T(8,128)(2,1)S(1)}, u32[]{:S(2)}, u32[]{:S(2)}) collective-permute-start(bf16[8,80,512]{2,1,0:T(8,128)(2,1)S(1)} %get-tuple-element.487), channel_id=1, source_target_pairs={{0,16},{8,24},{16,0},{24,8},{1,17},{9,25},{17,1},{25,9},{2,18},{10... | collective-permute-start | bytes 1966088 | tf_op jit(solution)/shard_map/ppermute | solution.py:29
  781.1 52.7 %collective-permute-start.77 = (bf16[8,80,512]{2,1,0:T(8,128)(2,1)S(1)}, bf16[8,80,512]{2,1,0:T(8,128)(2,1)S(1)}, u32[]{:S(2)}, u32[]{:S(2)}) collective-permute-start(bf16[8,80,512]{2,1,0:T(8,128)(2,1)S(1)} %get-tuple-element.488), channel_id=1, source_target_pairs={{0,8},{8,0},{16,24},{24,16},{1,9},{9,1},{17,25},{25,17},{2,10},{10... | collective-permute-start | bytes 1966088 | tf_op jit(solution)/shard_map/ppermute | solution.py:29
  862.6 67.4 %all-to-all-start.4 = ((bf16[8,80,512]{2,1,0:T(8,128)(2,1)}), bf16[8,80,512]{2,1,0:T(8,128)(2,1)S(1)}, u32[]{:S(2)}, u32[]{:S(2)}) async-start(bf16[8,80,512]{2,1,0:T(8,128)(2,1)} %fusion.8), calls=%async_computation.4 | async-start | bytes 1310720 | tf_op jit(solution)/shard_map/all_to_all | solution.py:912
  866.4 55.2 %collective-permute-start.85 = (bf16[8,64,176]{2,1,0:T(8,128)(2,1)}, bf16[8,64,176]{2,1,0:T(8,128)(2,1)}, u32[]{:S(2)}, u32[]{:S(2)}) collective-permute-start(bf16[8,64,176]{2,1,0:T(8,128)(2,1)} %get-tuple-element.502), channel_id=1, source_target_pairs={{0,24},{8,16},{16,8},{24,0},{1,25},{9,17},{17,9},{25,1},{2,26},{10... | collective-permute-start | bytes 540680 | tf_op jit(solution)/shard_map/ppermute | solution.py:29
  868.0 53.6 %collective-permute-start.84 = (bf16[8,64,176]{2,1,0:T(8,128)(2,1)}, bf16[8,64,176]{2,1,0:T(8,128)(2,1)}, u32[]{:S(2)}, u32[]{:S(2)}) collective-permute-start(bf16[8,64,176]{2,1,0:T(8,128)(2,1)} %get-tuple-element.503), channel_id=1, source_target_pairs={{0,16},{8,24},{16,0},{24,8},{1,17},{9,25},{17,1},{25,9},{2,18},{10... | collective-permute-start | bytes 540680 | tf_op jit(solution)/shard_map/ppermute | solution.py:29
  (144 other events, 2285.7 us)

commit v3 on v2

--- a/solution.py
+++ b/solution.py
@@ -203,17 +203,10 @@
         made.start()
         return made
 
-    in_sec = [
+    near = [
         copy(sec_a, sec_v.at[pl.ds(0, half)], sem_in, 0),
-        copy(sec_b, sec_v.at[pl.ds(half, half)], sem_in, 1),
+        copy(cot_a, cot_v.at[pl.ds(0, half)], sem_in, 2),
     ]
-    in_cot = [
-        copy(cot_a, cot_v.at[pl.ds(0, half)], sem_in, 2),
-        copy(cot_b, cot_v.at[pl.ds(half, half)], sem_in, 3),
-    ]
-    for one in in_cot:
-        one.wait()
-
     first_expert = place_ref[0]
     tail = cot_v.shape[1] - D
     row_i = lax.broadcasted_iota(jnp.int32, (rows, rows), 0)
@@ -221,13 +214,6 @@
     earlier = (col_i < row_i).astype(BF)
     lane = lax.broadcasted_iota(jnp.int32, (rows, tail), 1)
     slot = lax.broadcasted_iota(jnp.int32, (rows, local_experts * capacity), 1).astype(F32)
-    for one in in_sec:
-        one.wait()
-    in_sin = copy(sin_hbm, sin_v, sem_in, 7)
-    in_sdn = copy(sdn_hbm, sdn_v, sem_in, 8)
-    in_gate = copy(gate_hbm, gate_v, sem_in, 4)
-    in_up = copy(up_hbm, up_v, sem_in, 5)
-    in_down = copy(down_hbm, down_v, sem_in, 6)
     sec_tail = sec_v.shape[1] - D
     tail_lane = lax.broadcasted_iota(jnp.int32, (capacity, sec_tail), 1)
 
@@ -255,7 +241,21 @@
             prob_v[to, :] = jnp.broadcast_to(prob, (capacity, 128))
         return carry
 
-    lax.fori_loop(0, blocks, gather, 0)
+    for one in near:
+        one.wait()
+    far = [
+        copy(sec_b, sec_v.at[pl.ds(half, half)], sem_in, 1),
+        copy(cot_b, cot_v.at[pl.ds(half, half)], sem_in, 3),
+    ]
+    in_sin = copy(sin_hbm, sin_v, sem_in, 7)
+    in_sdn = copy(sdn_hbm, sdn_v, sem_in, 8)
+    lax.fori_loop(0, blocks // 2, gather, 0, unroll=True)
+    for one in far:
+        one.wait()
+    in_gate = copy(gate_hbm, gate_v, sem_in, 4)
+    in_up = copy(up_hbm, up_v, sem_in, 5)
+    in_down = copy(down_hbm, down_v, sem_in, 6)
+    lax.fori_loop(blocks // 2, blocks, gather, 0, unroll=True)
     outs = []
     for e in range(local_experts):
         mine = pl.ds(e * per, per)
@@ -336,7 +336,7 @@
             move.start()
         return carry
 
-    lax.fori_loop(0, half // rows, scatter, 0)
+    lax.fori_loop(0, half // rows, scatter, 0, unroll=True)
     for b in range(half // rows):
         for move in block_copies(b):
             move.wait()
@@ -782,12 +782,12 @@
         kept = results[:5]
         marks.append(results[10])
         if d == c_size - 1:
-            results[8] = after(results[8], *arrived)
+            results[7] = after(results[7], *arrived)
         sums.append(core_sum(*results[7:9], d))
         if d:
             arrived.append(swap(sums[d], "c", d))
         if d == c_size - 1:
-            kept = after_all(kept, *arrived[:-1])
+            kept = after_all(kept, *arrived[:-1], sums[d])
             results[6] = after(results[6], arrived[-1])
         out_sums.append(core_sum(*results[5:7], d))
         sg_parts.append(results[9])

time: 940 us -> 923 us (0.982)
  waiting for transfers between devices: 322 us -> 312 us
    ppermute x86, waiting for transfers between devices: 316 us -> 305 us  [swap(): return lax.ppermute(block, axis, [(i, i ^ distance) for i in range(n)])]
  transfers between devices with their start and end apart: 92 -> 92, of which waited for: 35 -> 35; matrix products, arithmetic and copies ran while one was open for 28% -> 29% of each run, Pallas kernels for 15% -> 18%
where the time goes in v3:
time: 923 us; the launch traced here: 917 us
  waiting for transfers between devices  312 us (34%)
  Pallas kernels  169 us (18%)
  local copies, waits for them, and re-layouts  149 us (16%)
  starting transfers between devices  133 us (14%)
  other arithmetic  89.4 us (10%)
  matrix products  62.4 us (7%)
    ppermute x86, waiting for transfers between devices, swap(): return lax.ppermute(block, axis, [(i, i ^ distance) for i in range(n)])  305 us
    pallas_call x4, Pallas kernels, expert_group(): pl.pallas_call(functools.partial(expert_kernel, local_experts, capacity,...  131 us
    ppermute x86, starting transfers between devices, swap(): return lax.ppermute(block, axis, [(i, i ^ distance) for i in range(n)])  107 us
    dynamic_update_slice x32, local copies, waits for them, and re-layouts, put(): return lax.dynamic_update_slice_in_dim(buffer, block[None], index, axis=0)  48.2 us
    dot_general x3, matrix products, on_device(): ein = lambda spec, a, b: jnp.einsum(spec, a, b, preferred_element_type=F32)  38.7 us
    dot_general x7, matrix products, dot(): return lax.dot_general(a, b, (dims, ((), ())), preferred_element_type=F32)  23.7 us
    pallas_call x1, Pallas kernels, attend_back(): pl.pallas_call(functools.partial(attend_back_kernel, heads), out_shape=sh...  20.7 us
    convert_element_type x6, other arithmetic, core_sum(): return summed.astype(BF) if distance else summed  18.6 us
  transfers between devices with their start and end apart: 92, of which 35 were waited for; matrix products, arithmetic and copies ran while one was open for 29% of the time, Pallas kernels for 18%

profile of v3, /device:TPU:0, one launch (start us, length us, event | category | flops | bytes accessed | tf_op | source)
XLA Modules:
  0.0 917.2 jit_solution(8731345885754156702)
XLA Ops:
  56.3 9.7 %collective-permute-done.9 = bf16[4,72,640]{2,1,0:T(8,128)(2,1)S(1)} collective-permute-done((bf16[4,72,640]{2,1,0:T(8,128)(2,1)S(1)}, bf16[4,72,640]{2,1,0:T(8,128)(2,1)S(1)}, u32[]{:S(2)}, u32[]{:S(2)}) %collective-permute-start.9) | collective-permute-done | bytes 368672 | tf_op jit(solution)/shard_map/ppermute | solution.py:29
  84.8 19.2 %collective-permute-done.1 = bf16[128,2176]{1,0:T(8,128)(2,1)S(1)} collective-permute-done((bf16[128,2176]{1,0:T(8,128)(2,1)S(1)}, bf16[128,2176]{1,0:T(8,128)(2,1)S(1)}, u32[]{:S(2)}, u32[]{:S(2)}) %collective-permute-start.1) | collective-permute-done | bytes 557088 | tf_op jit(solution)/shard_map/ppermute | solution.py:29
  149.9 17.2 %shard_map.297 = (bf16[1024,256]{1,0:T(8,128)(2,1)}, bf16[1024,2048]{1,0:T(8,128)(2,1)}, bf16[1024,384]{1,0:T(8,128)(2,1)}, bf16[1024,512]{1,0:T(8,128)(2,1)}, b...) custom-call(s32[2]{0:T(128)} %pad_add_fusion.place, bf16[1024,2176]{1,0:T(8,128)(2,1)} %bitcast.20.seq, ...), custom_call_target="tpu_custom_call" | custom-call | flops 1048576 | bytes 65536 | tf_op jit(solution)/shard_map/pallas_call | solution.py:481
  167.7 15.3 %collective-permute-done.15 = bf16[128,2176]{1,0:T(8,128)(2,1)} collective-permute-done((bf16[128,2176]{1,0:T(8,128)(2,1)}, bf16[128,2176]{1,0:T(8,128)(2,1)}, u32[]{:S(2)}, u32[]{:S(2)}) %collective-permute-start.15) | collective-permute-done | bytes 557088 | tf_op jit(solution)/shard_map/ppermute | solution.py:29
  242.2 15.7 %collective-permute-done.26 = bf16[128,2176]{1,0:T(8,128)(2,1)S(1)} collective-permute-done((bf16[128,2176]{1,0:T(8,128)(2,1)S(1)}, bf16[128,2176]{1,0:T(8,128)(2,1)S(1)}, u32[]{:S(2)}, u32[]{:S(2)}) %collective-permute-start.26) | collective-permute-done | bytes 557088 | tf_op jit(solution)/shard_map/ppermute | solution.py:29
  257.9 21.9 %collective-permute-start.24 = (bf16[128,2176]{1,0:T(8,128)(2,1)S(1)}, bf16[128,2176]{1,0:T(8,128)(2,1)S(1)}, u32[]{:S(2)}, u32[]{:S(2)}) collective-permute-start(bf16[128,2176]{1,0:T(8,128)(2,1)S(1)} %pad_maximum_fusion.5), channel_id=1, source_target_pairs={{0,1},{1,0},{2,3},{3,2},{4,5},{5,4},{6,7},{7,6},{8,9},{9,8},{10,11... | collective-permute-start | bytes 1671176 | tf_op jit(solution)/shard_map/ppermute | solution.py:29
  279.7 10.5 %collective-permute-done.25 = bf16[128,2176]{1,0:T(8,128)(2,1)S(1)} collective-permute-done((bf16[128,2176]{1,0:T(8,128)(2,1)S(1)}, bf16[128,2176]{1,0:T(8,128)(2,1)S(1)}, u32[]{:S(2)}, u32[]{:S(2)}) %collective-permute-start.25) | collective-permute-done | bytes 557088 | tf_op jit(solution)/shard_map/ppermute | solution.py:29
  290.2 11.7 %collective-permute-done.24 = bf16[128,2176]{1,0:T(8,128)(2,1)S(1)} collective-permute-done((bf16[128,2176]{1,0:T(8,128)(2,1)S(1)}, bf16[128,2176]{1,0:T(8,128)(2,1)S(1)}, u32[]{:S(2)}, u32[]{:S(2)}) %collective-permute-start.24) | collective-permute-done | bytes 557088 | tf_op jit(solution)/shard_map/ppermute | solution.py:29
  316.8 32.5 %shard_map.298 = (bf16[2,2048,2048]{2,1,0:T(8,128)(2,1)}, bf16[2,2048,2048]{2,1,0:T(8,128)(2,1)}, bf16[2,2048,352]{2,1,0:T(8,128)(2,1)}, bf16[2,2048,352]{2,1,0:...) custom-call(s32[2]{0:T(128)} %copy-done.79, ...), custom_call_target="tpu_custom_call" | custom-call | flops 1048576 | bytes 65536 | tf_op jit(solution)/shard_map/pallas_call | solution.py:375
  349.3 14.0 %collective-permute-done.34.sec_a = bf16[512,2176]{1,0:T(8,128)(2,1)} collective-permute-done((bf16[512,2176]{1,0:T(8,128)(2,1)}, bf16[512,2176]{1,0:T(8,128)(2,1)}, u32[]{:S(2)}, u32[]{:S(2)}) %collective-permute-start.34) | collective-permute-done | bytes 2228256 | tf_op jit(solution)/shard_map/ppermute | solution.py:29
  369.2 32.8 %shard_map.299 = (bf16[2,2048,2048]{2,1,0:T(8,128)(2,1)}, bf16[2,2048,2048]{2,1,0:T(8,128)(2,1)}, bf16[2,2048,352]{2,1,0:T(8,128)(2,1)}, bf16[2,2048,352]{2,1,0:...) custom-call(s32[2]{0:T(128)} %copy-done.74, ...), custom_call_target="tpu_custom_call", output_to_operand_aliasing={{0}: (10, {}), {1}: (11, {}), {2}: (12, {}), {3}: (13, {}),... | custom-call | flops 1048576 | bytes 65536 | tf_op jit(solution)/shard_map/pallas_call | solution.py:375
  402.7 13.9 %collective-permute-done.40.sec_a = bf16[512,2176]{1,0:T(8,128)(2,1)} collective-permute-done((bf16[512,2176]{1,0:T(8,128)(2,1)}, bf16[512,2176]{1,0:T(8,128)(2,1)}, u32[]{:S(2)}, u32[]{:S(2)}) %collective-permute-start.40) | collective-permute-done | bytes 2228256 | tf_op jit(solution)/shard_map/ppermute | solution.py:29
  420.1 32.9 %shard_map.300 = (bf16[2,2048,2048]{2,1,0:T(8,128)(2,1)}, bf16[2,2048,2048]{2,1,0:T(8,128)(2,1)}, bf16[2,2048,352]{2,1,0:T(8,128)(2,1)}, bf16[2,2048,352]{2,1,0:...) custom-call(s32[2]{0:T(128)} %copy-done.73, ...), custom_call_target="tpu_custom_call", output_to_operand_aliasing={{0}: (10, {}), {1}: (11, {}), {2}: (12, {}), {3}: (13, {}),... | custom-call | flops 1048576 | bytes 65536 | tf_op jit(solution)/shard_map/pallas_call | solution.py:375
  464.3 32.7 %shard_map.301 = (bf16[2,2048,2048]{2,1,0:T(8,128)(2,1)}, bf16[2,2048,2048]{2,1,0:T(8,128)(2,1)}, bf16[2,2048,352]{2,1,0:T(8,128)(2,1)}, bf16[2,2048,352]{2,1,0:...) custom-call(s32[2]{0:T(128)} %copy-done.72, ...), custom_call_target="tpu_custom_call", output_to_operand_aliasing={{0}: (10, {}), {1}: (11, {}), {2}: (12, {}), {3}: (13, {}),... | custom-call | flops 1048576 | bytes 65536 | tf_op jit(solution)/shard_map/pallas_call | solution.py:375
  497.9 11.6 %collective-permute-done.39 = bf16[512,2176]{1,0:T(8,128)(2,1)} collective-permute-done((bf16[512,2176]{1,0:T(8,128)(2,1)}, bf16[512,2176]{1,0:T(8,128)(2,1)}, u32[]{:S(2)}, u32[]{:S(2)}) %collective-permute-start.39) | collective-permute-done | bytes 2228256 | tf_op jit(solution)/shard_map/ppermute | solution.py:29
  518.3 13.1 %fusion.93 = f32[2,2048,352]{1,2,0:T(8,128)} fusion(bf16[2,2048,2048]{2,1,0:T(8,128)(2,1)} %get-tuple-element.297, bf16[2,2048,352]{2,1,0:T(8,128)(2,1)S(1)} %copy-done.2), kind=kOutput, calls=%fused_computation.257 | convolution fusion | flops 5905580032 | bytes 25427968 | tf_op jit(solution)/shard_map/esf,esd->efd/dot_general | solution.py:797
  531.4 12.7 %fusion.94 = f32[2,2048,352]{1,2,0:T(8,128)} fusion(bf16[2,2048,2048]{2,1,0:T(8,128)(2,1)} %get-tuple-element.297, bf16[2,2048,352]{2,1,0:T(8,128)(2,1)S(1)} %copy-done.3), kind=kOutput, calls=%fused_computation.258 | convolution fusion | flops 5905580032 | bytes 25427968 | tf_op jit(solution)/shard_map/esf,esd->efd/dot_general | solution.py:797
  544.1 12.9 %fusion.92 = f32[2,352,2048]{2,1,0:T(8,128)} fusion(bf16[2,2048,352]{2,1,0:T(8,128)(2,1)S(1)} %copy-done, bf16[2,2048,2048]{2,1,0:T(8,128)(2,1)} %get-tuple-element.296), kind=kOutput, calls=%fused_computation.256 | convolution fusion | flops 5905580032 | bytes 25427968 | tf_op jit(solution)/shard_map/esf,esd->efd/dot_general | solution.py:797
  557.0 11.0 %collective-permute-done.48 = bf16[512,2176]{1,0:T(8,128)(2,1)} collective-permute-done((bf16[512,2176]{1,0:T(8,128)(2,1)}, bf16[512,2176]{1,0:T(8,128)(2,1)}, u32[]{:S(2)}, u32[]{:S(2)}) %collective-permute-start.48) | collective-permute-done | bytes 2228256 | tf_op jit(solution)/shard_map/ppermute | solution.py:29
  591.4 11.5 %collective-permute-done.57 = bf16[128,2176]{1,0:T(8,128)(2,1)S(1)} collective-permute-done((bf16[128,2176]{1,0:T(8,128)(2,1)S(1)}, bf16[128,2176]{1,0:T(8,128)(2,1)S(1)}, u32[]{:S(2)}, u32[]{:S(2)}) %collective-permute-start.57) | collective-permute-done | bytes 557088 | tf_op jit(solution)/shard_map/ppermute | solution.py:29
  602.9 28.3 %collective-permute-done.56 = bf16[128,2176]{1,0:T(8,128)(2,1)S(1)} collective-permute-done((bf16[128,2176]{1,0:T(8,128)(2,1)S(1)}, bf16[128,2176]{1,0:T(8,128)(2,1)S(1)}, u32[]{:S(2)}, u32[]{:S(2)}) %collective-permute-start.56) | collective-permute-done | bytes 557088 | tf_op jit(solution)/shard_map/ppermute | solution.py:29
  645.7 7.1 convolution_convert_fusion.2
  666.7 7.3 fusion.2
  678.5 20.7 %shard_map.302 = (f32[1,2048]{1,0:T(1,128)}, bf16[512,2048]{1,0:T(8,128)(2,1)}, bf16[512,2048]{1,0:T(8,128)(2,1)}, bf16[512,640]{1,0:T(8,128)(2,1)}, bf16[512,64...) custom-call(s32[2]{0:T(128)} %pad_add_fusion.place, bf16[1024,256]{1,0:T(8,128)(2,1)} %bitcast.73.grad, ...), custom_call_target="tpu_custom_call" | custom-call | flops 1048576 | bytes 65536 | tf_op jit(solution)/shard_map/pallas_call | solution.py:569
  714.5 7.4 collective-permute-done.65
  755.7 7.4 collective-permute-done.60
  765.2 34.4 %collective-permute-done.61 = bf16[128,2048]{1,0:T(8,128)(2,1)} collective-permute-done((bf16[128,2048]{1,0:T(8,128)(2,1)}, bf16[128,2048]{1,0:T(8,128)(2,1)}, u32[]{:S(2)}, u32[]{:S(2)}) %collective-permute-start.61) | collective-permute-done | bytes 524320 | tf_op jit(solution)/shard_map/ppermute | solution.py:29
  805.0 6.6 fusion.86
  818.4 12.3 %collective-permute-done.74 = bf16[256,640]{1,0:T(8,128)(2,1)S(1)} collective-permute-done((bf16[256,640]{1,0:T(8,128)(2,1)S(1)}, bf16[256,640]{1,0:T(8,128)(2,1)S(1)}, u32[]{:S(2)}, u32[]{:S(2)}) %collective-permute-start.74) | collective-permute-done | bytes 327712 | tf_op jit(solution)/shard_map/ppermute | solution.py:29
  856.1 12.3 %collective-permute-done.71 = bf16[128,2048]{1,0:T(8,128)(2,1)} collective-permute-done((bf16[128,2048]{1,0:T(8,128)(2,1)}, bf16[128,2048]{1,0:T(8,128)(2,1)}, u32[]{:S(2)}, u32[]{:S(2)}) %collective-permute-start.71) | collective-permute-done | bytes 524320 | tf_op jit(solution)/shard_map/ppermute | solution.py:29
  873.0 8.3 collective-permute-done.80
  882.6 18.7 %collective-permute-done.81 = bf16[64,2688]{1,0:T(8,128)(2,1)S(1)} collective-permute-done((bf16[64,2688]{1,0:T(8,128)(2,1)S(1)}, bf16[64,2688]{1,0:T(8,128)(2,1)S(1)}, u32[]{:S(2)}, u32[]{:S(2)}) %collective-permute-start.81) | collective-permute-done | bytes 344096 | tf_op jit(solution)/shard_map/ppermute | solution.py:29
  (560 shorter events, 391.4 us)
Async XLA Ops:
  104.8 78.3 %all-to-all-start.1 = ((bf16[32,64,176]{2,1,0:T(8,128)(2,1)}), bf16[32,64,176]{2,1,0:T(8,128)(2,1)}, u32[]{:S(2)}, u32[]{:S(2)}) async-start(bf16[32,64,176]{2,1,0:T(8,128)(2,1)} %maximum_bitcast_fusion), calls=%async_computation.1 | async-start | bytes 2097152 | tf_op jit(solution)/shard_map/all_to_all | solution.py:685
  109.1 58.0 %collective-permute-start.16 = (bf16[128,2176]{1,0:T(8,128)(2,1)}, bf16[128,2176]{1,0:T(8,128)(2,1)}, u32[]{:S(2)}, u32[]{:S(2)}) collective-permute-start(bf16[128,2176]{1,0:T(8,128)(2,1)} %pad_maximum_fusion.4), channel_id=1, source_target_pairs={{0,3},{1,2},{2,1},{3,0},{4,7},{5,6},{6,5},{7,4},{8,11},{9,10},{10,... | collective-permute-start | bytes 1671176 | tf_op jit(solution)/shard_map/ppermute | solution.py:29
  112.8 70.3 %collective-permute-start.15 = (bf16[128,2176]{1,0:T(8,128)(2,1)}, bf16[128,2176]{1,0:T(8,128)(2,1)}, u32[]{:S(2)}, u32[]{:S(2)}) collective-permute-start(bf16[128,2176]{1,0:T(8,128)(2,1)} %pad_maximum_fusion.4), channel_id=1, source_target_pairs={{0,2},{1,3},{2,0},{3,1},{4,6},{5,7},{6,4},{7,5},{8,10},{9,11},{10,... | collective-permute-start | bytes 1671176 | tf_op jit(solution)/shard_map/ppermute | solution.py:29
  112.8 70.3 %collective-permute-start.14 = (bf16[128,2176]{1,0:T(8,128)(2,1)}, bf16[128,2176]{1,0:T(8,128)(2,1)}, u32[]{:S(2)}, u32[]{:S(2)}) collective-permute-start(bf16[128,2176]{1,0:T(8,128)(2,1)} %pad_maximum_fusion.4), channel_id=1, source_target_pairs={{0,1},{1,0},{2,3},{3,2},{4,5},{5,4},{6,7},{7,6},{8,9},{9,8},{10,11... | collective-permute-start | bytes 1671176 | tf_op jit(solution)/shard_map/ppermute | solution.py:29
  129.3 61.9 %collective-permute-start.22 = (bf16[4,64,2048]{2,1,0:T(8,128)(2,1)}, bf16[4,64,2048]{2,1,0:T(8,128)(2,1)}, u32[]{:S(2)}, u32[]{:S(2)}) collective-permute-start(bf16[4,64,2048]{2,1,0:T(8,128)(2,1)} %bitcast_dynamic-update-slice_fusion.24), channel_id=1, source_target_pairs={{0,24},{8,16},{16,8},{24,0},{1,25},{9,17},{17,9},{25,1},{2,26},{10... | collective-permute-start | bytes 3145736 | tf_op jit(solution)/shard_map/ppermute | solution.py:29
  146.2 44.9 %collective-permute-start.21 = (bf16[4,64,2048]{2,1,0:T(8,128)(2,1)}, bf16[4,64,2048]{2,1,0:T(8,128)(2,1)S(1)}, u32[]{:S(2)}, u32[]{:S(2)}) collective-permute-start(bf16[4,64,2048]{2,1,0:T(8,128)(2,1)} %bitcast_dynamic-update-slice_fusion.24), channel_id=1, source_target_pairs={{0,16},{8,24},{16,0},{24,8},{1,17},{9,25},{17,1},{25,9},{2,18},{10... | collective-permute-start | bytes 3145736 | tf_op jit(solution)/shard_map/ppermute | solution.py:29
  212.2 94.0 %collective-permute-start.29 = (bf16[512,2176]{1,0:T(8,128)(2,1)}, bf16[512,2176]{1,0:T(8,128)(2,1)}, u32[]{:S(2)}, u32[]{:S(2)}) collective-permute-start(bf16[512,2176]{1,0:T(8,128)(2,1)} %constant_dynamic-update-slice_fusion.1.cot_a), channel_id=1, source_target_pairs={{0,24},{8,16},{16,8},{24,0},{1,25},{9,17},{17,9},{25,1},{2,26},{10... | collective-permute-start | bytes 6684680 | tf_op jit(solution)/shard_map/ppermute | solution.py:29
  214.5 97.6 %collective-permute-start.28 = (bf16[512,2176]{1,0:T(8,128)(2,1)}, bf16[512,2176]{1,0:T(8,128)(2,1)}, u32[]{:S(2)}, u32[]{:S(2)}) collective-permute-start(bf16[512,2176]{1,0:T(8,128)(2,1)} %constant_dynamic-update-slice_fusion.1.cot_a), channel_id=1, source_target_pairs={{0,16},{8,24},{16,0},{24,8},{1,17},{9,25},{17,1},{25,9},{2,18},{10... | collective-permute-start | bytes 6684680 | tf_op jit(solution)/shard_map/ppermute | solution.py:29
  215.1 97.1 %collective-permute-start.27 = (bf16[512,2176]{1,0:T(8,128)(2,1)}, bf16[512,2176]{1,0:T(8,128)(2,1)}, u32[]{:S(2)}, u32[]{:S(2)}) collective-permute-start(bf16[512,2176]{1,0:T(8,128)(2,1)} %constant_dynamic-update-slice_fusion.1.cot_a), channel_id=1, source_target_pairs={{0,8},{8,0},{16,24},{24,16},{1,9},{9,1},{17,25},{25,17},{2,10},{10... | collective-permute-start | bytes 6684680 | tf_op jit(solution)/shard_map/ppermute | solution.py:29
  242.2 48.1 %collective-permute-start.25 = (bf16[128,2176]{1,0:T(8,128)(2,1)S(1)}, bf16[128,2176]{1,0:T(8,128)(2,1)S(1)}, u32[]{:S(2)}, u32[]{:S(2)}) collective-permute-start(bf16[128,2176]{1,0:T(8,128)(2,1)S(1)} %pad_maximum_fusion.5), channel_id=1, source_target_pairs={{0,2},{1,3},{2,0},{3,1},{4,6},{5,7},{6,4},{7,5},{8,10},{9,11},{10,... | collective-permute-start | bytes 1671176 | tf_op jit(solution)/shard_map/ppermute | solution.py:29
  312.1 51.2 %collective-permute-start.34 = (bf16[512,2176]{1,0:T(8,128)(2,1)}, bf16[512,2176]{1,0:T(8,128)(2,1)}, u32[]{:S(2)}, u32[]{:S(2)}) collective-permute-start(bf16[512,2176]{1,0:T(8,128)(2,1)} %pad_maximum_fusion.1.sec_a), channel_id=1, source_target_pairs={{0,16},{8,24},{16,0},{24,8},{1,17},{9,25},{17,1},{25,9},{2,18},{10... | collective-permute-start | bytes 6684680 | tf_op jit(solution)/shard_map/ppermute | solution.py:29
  313.6 50.8 %collective-permute-start.33 = (bf16[512,2176]{1,0:T(8,128)(2,1)}, bf16[512,2176]{1,0:T(8,128)(2,1)}, u32[]{:S(2)}, u32[]{:S(2)}) collective-permute-start(bf16[512,2176]{1,0:T(8,128)(2,1)} %pad_maximum_fusion.1.sec_a), channel_id=1, source_target_pairs={{0,8},{8,0},{16,24},{24,16},{1,9},{9,1},{17,25},{25,17},{2,10},{10... | collective-permute-start | bytes 6684680 | tf_op jit(solution)/shard_map/ppermute | solution.py:29
  315.4 50.5 %collective-permute-start.36 = (bf16[512,2176]{1,0:T(8,128)(2,1)}, bf16[512,2176]{1,0:T(8,128)(2,1)}, u32[]{:S(2)}, u32[]{:S(2)}) collective-permute-start(bf16[512,2176]{1,0:T(8,128)(2,1)} %collective-permute-done.27.cot_a), channel_id=1, source_target_pairs={{0,4},{4,0},{1,5},{5,1},{2,6},{6,2},{3,7},{7,3},{8,12},{12,8},{9,1... | collective-permute-start | bytes 6684680 | tf_op jit(solution)/shard_map/ppermute | solution.py:29
  364.5 52.1 %collective-permute-start.40 = (bf16[512,2176]{1,0:T(8,128)(2,1)}, bf16[512,2176]{1,0:T(8,128)(2,1)}, u32[]{:S(2)}, u32[]{:S(2)}) collective-permute-start(bf16[512,2176]{1,0:T(8,128)(2,1)} %pad_maximum_fusion.1.sec_a), channel_id=1, source_target_pairs={{0,24},{8,16},{16,8},{24,0},{1,25},{9,17},{17,9},{25,1},{2,26},{10... | collective-permute-start | bytes 6684680 | tf_op jit(solution)/shard_map/ppermute | solution.py:29
  458.7 50.7 %collective-permute-start.39 = (bf16[512,2176]{1,0:T(8,128)(2,1)}, bf16[512,2176]{1,0:T(8,128)(2,1)}, u32[]{:S(2)}, u32[]{:S(2)}) collective-permute-start(bf16[512,2176]{1,0:T(8,128)(2,1)} %add_convert_fusion.2), channel_id=1, source_target_pairs={{0,8},{8,0},{16,24},{24,16},{1,9},{9,1},{17,25},{25,17},{2,10},{10... | collective-permute-start | bytes 6684680 | tf_op jit(solution)/shard_map/ppermute | solution.py:29
  462.2 51.0 %collective-permute-start.44 = (bf16[512,2176]{1,0:T(8,128)(2,1)}, bf16[512,2176]{1,0:T(8,128)(2,1)}, u32[]{:S(2)}, u32[]{:S(2)}) collective-permute-start(bf16[512,2176]{1,0:T(8,128)(2,1)} %add_convert_fusion.1), channel_id=1, source_target_pairs={{0,16},{8,24},{16,0},{24,8},{1,17},{9,25},{17,1},{25,9},{2,18},{10... | collective-permute-start | bytes 6684680 | tf_op jit(solution)/shard_map/ppermute | solution.py:29
  497.4 70.6 %collective-permute-start.54 = (bf16[512,2176]{1,0:T(8,128)(2,1)}, bf16[512,2176]{1,0:T(8,128)(2,1)}, u32[]{:S(2)}, u32[]{:S(2)}) collective-permute-start(bf16[512,2176]{1,0:T(8,128)(2,1)} %get-tuple-element.289), channel_id=1, source_target_pairs={{0,4},{4,0},{1,5},{5,1},{2,6},{6,2},{3,7},{7,3},{8,12},{12,8},{9,1... | collective-permute-start | bytes 6684680 | tf_op jit(solution)/shard_map/ppermute | solution.py:29
  497.5 77.7 %collective-permute-start.50 = (bf16[512,2048]{1,0:T(8,128)(2,1)}, bf16[512,2048]{1,0:T(8,128)(2,1)}, u32[]{:S(2)}, u32[]{:S(2)}) collective-permute-start(bf16[512,2048]{1,0:T(8,128)(2,1)} %get-tuple-element.282), channel_id=1, source_target_pairs={{0,4},{4,0},{1,5},{5,1},{2,6},{6,2},{3,7},{7,3},{8,12},{12,8},{9,1... | collective-permute-start | bytes 6291464 | tf_op jit(solution)/shard_map/ppermute | solution.py:29
  516.9 51.1 %collective-permute-start.48 = (bf16[512,2176]{1,0:T(8,128)(2,1)}, bf16[512,2176]{1,0:T(8,128)(2,1)}, u32[]{:S(2)}, u32[]{:S(2)}) collective-permute-start(bf16[512,2176]{1,0:T(8,128)(2,1)} %add_convert_fusion), channel_id=1, source_target_pairs={{0,24},{8,16},{16,8},{24,0},{1,25},{9,17},{17,9},{25,1},{2,26},{10... | collective-permute-start | bytes 6684680 | tf_op jit(solution)/shard_map/ppermute | solution.py:29
  568.0 63.4 %collective-permute-start.52 = (bf16[512,2048]{1,0:T(8,128)(2,1)S(1)}, bf16[512,2048]{1,0:T(8,128)(2,1)S(1)}, u32[]{:S(2)}, u32[]{:S(2)}) collective-permute-start(bf16[512,2048]{1,0:T(8,128)(2,1)S(1)} %copy-done.80), channel_id=1, source_target_pairs={{0,4},{4,0},{1,5},{5,1},{2,6},{6,2},{3,7},{7,3},{8,12},{12,8},{9,1... | collective-permute-start | bytes 6291464 | tf_op jit(solution)/shard_map/ppermute | solution.py:29
  577.9 55.7 %collective-permute-start.49 = (bf16[512,2048]{1,0:T(8,128)(2,1)S(1)}, bf16[512,2048]{1,0:T(8,128)(2,1)S(1)}, u32[]{:S(2)}, u32[]{:S(2)}) collective-permute-start(bf16[512,2048]{1,0:T(8,128)(2,1)S(1)} %copy-done.23), channel_id=1, source_target_pairs={{0,8},{8,0},{16,24},{24,16},{1,9},{9,1},{17,25},{25,17},{2,10},{10... | collective-permute-start | bytes 6291464 | tf_op jit(solution)/shard_map/ppermute | solution.py:29
  578.8 54.8 %collective-permute-start.51 = (bf16[512,2048]{1,0:T(8,128)(2,1)S(1)}, bf16[512,2048]{1,0:T(8,128)(2,1)S(1)}, u32[]{:S(2)}, u32[]{:S(2)}) collective-permute-start(bf16[512,2048]{1,0:T(8,128)(2,1)S(1)} %add_convert_fusion.4), channel_id=1, source_target_pairs={{0,16},{8,24},{16,0},{24,8},{1,17},{9,25},{17,1},{25,9},{2,18},{10... | collective-permute-start | bytes 6291464 | tf_op jit(solution)/shard_map/ppermute | solution.py:29
  644.1 55.0 %collective-permute-start.53 = (bf16[512,2048]{1,0:T(8,128)(2,1)}, bf16[512,2048]{1,0:T(8,128)(2,1)}, u32[]{:S(2)}, u32[]{:S(2)}) collective-permute-start(bf16[512,2048]{1,0:T(8,128)(2,1)} %add_convert_fusion.3), channel_id=1, source_target_pairs={{0,24},{8,16},{16,8},{24,0},{1,25},{9,17},{17,9},{25,1},{2,26},{10... | collective-permute-start | bytes 6291464 | tf_op jit(solution)/shard_map/ppermute | solution.py:29
  666.3 137.3 %collective-permute-start.32 = (bf16[512,2048]{1,0:T(8,128)(2,1)}, bf16[512,2048]{1,0:T(8,128)(2,1)}, u32[]{:S(2)}, u32[]{:S(2)}) collective-permute-start(bf16[512,2048]{1,0:T(8,128)(2,1)} %get-tuple-element.246), channel_id=1, source_target_pairs={{0,4},{4,0},{1,5},{5,1},{2,6},{6,2},{3,7},{7,3},{8,12},{12,8},{9,1... | collective-permute-start | bytes 6291464 | tf_op jit(solution)/shard_map/ppermute | solution.py:29
  739.2 60.4 %collective-permute-start.61 = (bf16[128,2048]{1,0:T(8,128)(2,1)}, bf16[128,2048]{1,0:T(8,128)(2,1)}, u32[]{:S(2)}, u32[]{:S(2)}) collective-permute-start(bf16[128,2048]{1,0:T(8,128)(2,1)} %get-tuple-element.478), channel_id=1, source_target_pairs={{0,2},{1,3},{2,0},{3,1},{4,6},{5,7},{6,4},{7,5},{8,10},{9,11},{10,... | collective-permute-start | bytes 1572872 | tf_op jit(solution)/shard_map/ppermute | solution.py:29
  746.3 89.8 %all-to-all-start.5 = ((bf16[8,4,64,176]{3,2,1,0:T(8,128)(2,1)}), bf16[8,4,64,176]{3,2,1,0:T(8,128)(2,1)}, u32[]{:S(2)}, u32[]{:S(2)}) async-start(bf16[8,4,64,176]{3,2,1,0:T(8,128)(2,1)} %copy.268), calls=%async_computation.5 | async-start | bytes 2097152 | tf_op jit(solution)/shard_map/all_to_all | solution.py:833
  752.5 60.5 %collective-permute-start.79 = (bf16[8,80,512]{2,1,0:T(8,128)(2,1)S(1)}, bf16[8,80,512]{2,1,0:T(8,128)(2,1)S(1)}, u32[]{:S(2)}, u32[]{:S(2)}) collective-permute-start(bf16[8,80,512]{2,1,0:T(8,128)(2,1)S(1)} %get-tuple-element.486), channel_id=1, source_target_pairs={{0,24},{8,16},{16,8},{24,0},{1,25},{9,17},{17,9},{25,1},{2,26},{10... | collective-permute-start | bytes 1966088 | tf_op jit(solution)/shard_map/ppermute | solution.py:29
  763.1 50.7 %collective-permute-start.78 = (bf16[8,80,512]{2,1,0:T(8,128)(2,1)S(1)}, bf16[8,80,512]{2,1,0:T(8,128)(2,1)S(1)}, u32[]{:S(2)}, u32[]{:S(2)}) collective-permute-start(bf16[8,80,512]{2,1,0:T(8,128)(2,1)S(1)} %get-tuple-element.487), channel_id=1, source_target_pairs={{0,16},{8,24},{16,0},{24,8},{1,17},{9,25},{17,1},{25,9},{2,18},{10... | collective-permute-start | bytes 1966088 | tf_op jit(solution)/shard_map/ppermute | solution.py:29
  763.7 52.7 %collective-permute-start.77 = (bf16[8,80,512]{2,1,0:T(8,128)(2,1)S(1)}, bf16[8,80,512]{2,1,0:T(8,128)(2,1)S(1)}, u32[]{:S(2)}, u32[]{:S(2)}) collective-permute-start(bf16[8,80,512]{2,1,0:T(8,128)(2,1)S(1)} %get-tuple-element.488), channel_id=1, source_target_pairs={{0,8},{8,0},{16,24},{24,16},{1,9},{9,1},{17,25},{25,17},{2,10},{10... | collective-permute-start | bytes 1966088 | tf_op jit(solution)/shard_map/ppermute | solution.py:29
  845.2 67.4 %all-to-all-start.4 = ((bf16[8,80,512]{2,1,0:T(8,128)(2,1)}), bf16[8,80,512]{2,1,0:T(8,128)(2,1)S(1)}, u32[]{:S(2)}, u32[]{:S(2)}) async-start(bf16[8,80,512]{2,1,0:T(8,128)(2,1)} %fusion.8), calls=%async_computation.4 | async-start | bytes 1310720 | tf_op jit(solution)/shard_map/all_to_all | solution.py:912
  848.9 55.1 %collective-permute-start.85 = (bf16[8,64,176]{2,1,0:T(8,128)(2,1)}, bf16[8,64,176]{2,1,0:T(8,128)(2,1)}, u32[]{:S(2)}, u32[]{:S(2)}) collective-permute-start(bf16[8,64,176]{2,1,0:T(8,128)(2,1)} %get-tuple-element.502), channel_id=1, source_target_pairs={{0,24},{8,16},{16,8},{24,0},{1,25},{9,17},{17,9},{25,1},{2,26},{10... | collective-permute-start | bytes 540680 | tf_op jit(solution)/shard_map/ppermute | solution.py:29
  850.6 53.5 %collective-permute-start.84 = (bf16[8,64,176]{2,1,0:T(8,128)(2,1)}, bf16[8,64,176]{2,1,0:T(8,128)(2,1)}, u32[]{:S(2)}, u32[]{:S(2)}) collective-permute-start(bf16[8,64,176]{2,1,0:T(8,128)(2,1)} %get-tuple-element.503), channel_id=1, source_target_pairs={{0,16},{8,24},{16,0},{24,8},{1,17},{9,25},{17,1},{25,9},{2,18},{10... | collective-permute-start | bytes 540680 | tf_op jit(solution)/shard_map/ppermute | solution.py:29
  (143 other events, 2280.2 us)

commit v4 on v3

--- a/solution.py
+++ b/solution.py
@@ -773,7 +773,7 @@
             second_groups[-1] = after(second_groups[-1], marks[d - 1])
             where = after(where, second_groups[-1])
         if d > 1:
-            where = after(where, out_sums[d - 2], sums[d - 1])
+            where = after(where, sums[d - 1])
         results = list(
             expert_group(
                 where, pair(group), cot_groups[d], weights, kept, capacity, rows, experts, c_size

time: 923 us -> 922 us (level)
  transfers between devices with their start and end apart: 92 -> 92, of which waited for: 35 -> 34; matrix products, arithmetic and copies ran while one was open for 29% -> 29% of each run, Pallas kernels for 18% -> 15%
where the time goes in v4:
time: 922 us; the launch traced here: 916 us
  waiting for transfers between devices  312 us (34%)
  Pallas kernels  169 us (18%)
  local copies, waits for them, and re-layouts  149 us (16%)
  starting transfers between devices  133 us (14%)
  other arithmetic  88.9 us (10%)
  matrix products  62.4 us (7%)
    ppermute x86, waiting for transfers between devices, swap(): return lax.ppermute(block, axis, [(i, i ^ distance) for i in range(n)])  305 us
    pallas_call x4, Pallas kernels, expert_group(): pl.pallas_call(functools.partial(expert_kernel, local_experts, capacity,...  131 us
    ppermute x86, starting transfers between devices, swap(): return lax.ppermute(block, axis, [(i, i ^ distance) for i in range(n)])  106 us
    dynamic_update_slice x32, local copies, waits for them, and re-layouts, put(): return lax.dynamic_update_slice_in_dim(buffer, block[None], index, axis=0)  48.2 us
    dot_general x3, matrix products, on_device(): ein = lambda spec, a, b: jnp.einsum(spec, a, b, preferred_element_type=F32)  38.7 us
    dot_general x7, matrix products, dot(): return lax.dot_general(a, b, (dims, ((), ())), preferred_element_type=F32)  23.7 us
    pallas_call x1, Pallas kernels, attend_back(): pl.pallas_call(functools.partial(attend_back_kernel, heads), out_shape=sh...  20.6 us
  transfers between devices with their start and end apart: 92, of which 34 were waited for; matrix products, arithmetic and copies ran while one was open for 29% of the time, Pallas kernels for 15%

profile of v4, /device:TPU:0, one launch (start us, length us, event | category | flops | bytes accessed | tf_op | source)
XLA Modules:
  0.0 916.3 jit_solution(17956228270462196401)
XLA Ops:
  56.4 9.6 %collective-permute-done.9 = bf16[4,72,640]{2,1,0:T(8,128)(2,1)S(1)} collective-permute-done((bf16[4,72,640]{2,1,0:T(8,128)(2,1)S(1)}, bf16[4,72,640]{2,1,0:T(8,128)(2,1)S(1)}, u32[]{:S(2)}, u32[]{:S(2)}) %collective-permute-start.9) | collective-permute-done | bytes 368672 | tf_op jit(solution)/shard_map/ppermute | solution.py:29
  84.8 19.2 %collective-permute-done.1 = bf16[128,2176]{1,0:T(8,128)(2,1)S(1)} collective-permute-done((bf16[128,2176]{1,0:T(8,128)(2,1)S(1)}, bf16[128,2176]{1,0:T(8,128)(2,1)S(1)}, u32[]{:S(2)}, u32[]{:S(2)}) %collective-permute-start.1) | collective-permute-done | bytes 557088 | tf_op jit(solution)/shard_map/ppermute | solution.py:29
  150.0 17.1 %shard_map.297 = (bf16[1024,256]{1,0:T(8,128)(2,1)}, bf16[1024,2048]{1,0:T(8,128)(2,1)}, bf16[1024,384]{1,0:T(8,128)(2,1)}, bf16[1024,512]{1,0:T(8,128)(2,1)}, b...) custom-call(s32[2]{0:T(128)} %pad_add_fusion.place, bf16[1024,2176]{1,0:T(8,128)(2,1)} %bitcast.20.seq, ...), custom_call_target="tpu_custom_call" | custom-call | flops 1048576 | bytes 65536 | tf_op jit(solution)/shard_map/pallas_call | solution.py:481
  167.7 15.5 %collective-permute-done.15 = bf16[128,2176]{1,0:T(8,128)(2,1)} collective-permute-done((bf16[128,2176]{1,0:T(8,128)(2,1)}, bf16[128,2176]{1,0:T(8,128)(2,1)}, u32[]{:S(2)}, u32[]{:S(2)}) %collective-permute-start.15) | collective-permute-done | bytes 557088 | tf_op jit(solution)/shard_map/ppermute | solution.py:29
  242.2 15.8 %collective-permute-done.26 = bf16[128,2176]{1,0:T(8,128)(2,1)S(1)} collective-permute-done((bf16[128,2176]{1,0:T(8,128)(2,1)S(1)}, bf16[128,2176]{1,0:T(8,128)(2,1)S(1)}, u32[]{:S(2)}, u32[]{:S(2)}) %collective-permute-start.26) | collective-permute-done | bytes 557088 | tf_op jit(solution)/shard_map/ppermute | solution.py:29
  258.0 21.8 %collective-permute-start.24 = (bf16[128,2176]{1,0:T(8,128)(2,1)S(1)}, bf16[128,2176]{1,0:T(8,128)(2,1)S(1)}, u32[]{:S(2)}, u32[]{:S(2)}) collective-permute-start(bf16[128,2176]{1,0:T(8,128)(2,1)S(1)} %pad_maximum_fusion.5), channel_id=1, source_target_pairs={{0,1},{1,0},{2,3},{3,2},{4,5},{5,4},{6,7},{7,6},{8,9},{9,8},{10,11... | collective-permute-start | bytes 1671176 | tf_op jit(solution)/shard_map/ppermute | solution.py:29
  279.8 10.6 %collective-permute-done.25 = bf16[128,2176]{1,0:T(8,128)(2,1)S(1)} collective-permute-done((bf16[128,2176]{1,0:T(8,128)(2,1)S(1)}, bf16[128,2176]{1,0:T(8,128)(2,1)S(1)}, u32[]{:S(2)}, u32[]{:S(2)}) %collective-permute-start.25) | collective-permute-done | bytes 557088 | tf_op jit(solution)/shard_map/ppermute | solution.py:29
  290.4 11.7 %collective-permute-done.24 = bf16[128,2176]{1,0:T(8,128)(2,1)S(1)} collective-permute-done((bf16[128,2176]{1,0:T(8,128)(2,1)S(1)}, bf16[128,2176]{1,0:T(8,128)(2,1)S(1)}, u32[]{:S(2)}, u32[]{:S(2)}) %collective-permute-start.24) | collective-permute-done | bytes 557088 | tf_op jit(solution)/shard_map/ppermute | solution.py:29
  317.0 32.5 %shard_map.298 = (bf16[2,2048,2048]{2,1,0:T(8,128)(2,1)}, bf16[2,2048,2048]{2,1,0:T(8,128)(2,1)}, bf16[2,2048,352]{2,1,0:T(8,128)(2,1)}, bf16[2,2048,352]{2,1,0:...) custom-call(s32[2]{0:T(128)} %copy-done.79, ...), custom_call_target="tpu_custom_call" | custom-call | flops 1048576 | bytes 65536 | tf_op jit(solution)/shard_map/pallas_call | solution.py:375
  349.4 14.0 %collective-permute-done.34.sec_a = bf16[512,2176]{1,0:T(8,128)(2,1)} collective-permute-done((bf16[512,2176]{1,0:T(8,128)(2,1)}, bf16[512,2176]{1,0:T(8,128)(2,1)}, u32[]{:S(2)}, u32[]{:S(2)}) %collective-permute-start.34) | collective-permute-done | bytes 2228256 | tf_op jit(solution)/shard_map/ppermute | solution.py:29
  369.3 32.9 %shard_map.299 = (bf16[2,2048,2048]{2,1,0:T(8,128)(2,1)}, bf16[2,2048,2048]{2,1,0:T(8,128)(2,1)}, bf16[2,2048,352]{2,1,0:T(8,128)(2,1)}, bf16[2,2048,352]{2,1,0:...) custom-call(s32[2]{0:T(128)} %copy-done.74, ...), custom_call_target="tpu_custom_call", output_to_operand_aliasing={{0}: (10, {}), {1}: (11, {}), {2}: (12, {}), {3}: (13, {}),... | custom-call | flops 1048576 | bytes 65536 | tf_op jit(solution)/shard_map/pallas_call | solution.py:375
  402.9 13.8 %collective-permute-done.40.sec_a = bf16[512,2176]{1,0:T(8,128)(2,1)} collective-permute-done((bf16[512,2176]{1,0:T(8,128)(2,1)}, bf16[512,2176]{1,0:T(8,128)(2,1)}, u32[]{:S(2)}, u32[]{:S(2)}) %collective-permute-start.40) | collective-permute-done | bytes 2228256 | tf_op jit(solution)/shard_map/ppermute | solution.py:29
  420.2 32.9 %shard_map.300 = (bf16[2,2048,2048]{2,1,0:T(8,128)(2,1)}, bf16[2,2048,2048]{2,1,0:T(8,128)(2,1)}, bf16[2,2048,352]{2,1,0:T(8,128)(2,1)}, bf16[2,2048,352]{2,1,0:...) custom-call(s32[2]{0:T(128)} %copy-done.73, ...), custom_call_target="tpu_custom_call", output_to_operand_aliasing={{0}: (10, {}), {1}: (11, {}), {2}: (12, {}), {3}: (13, {}),... | custom-call | flops 1048576 | bytes 65536 | tf_op jit(solution)/shard_map/pallas_call | solution.py:375
  464.3 32.6 %shard_map.301 = (bf16[2,2048,2048]{2,1,0:T(8,128)(2,1)}, bf16[2,2048,2048]{2,1,0:T(8,128)(2,1)}, bf16[2,2048,352]{2,1,0:T(8,128)(2,1)}, bf16[2,2048,352]{2,1,0:...) custom-call(s32[2]{0:T(128)} %copy-done.72, ...), custom_call_target="tpu_custom_call", output_to_operand_aliasing={{0}: (10, {}), {1}: (11, {}), {2}: (12, {}), {3}: (13, {}),... | custom-call | flops 1048576 | bytes 65536 | tf_op jit(solution)/shard_map/pallas_call | solution.py:375
  505.0 9.4 %collective-permute-done.44 = bf16[512,2176]{1,0:T(8,128)(2,1)} collective-permute-done((bf16[512,2176]{1,0:T(8,128)(2,1)}, bf16[512,2176]{1,0:T(8,128)(2,1)}, u32[]{:S(2)}, u32[]{:S(2)}) %collective-permute-start.44) | collective-permute-done | bytes 2228256 | tf_op jit(solution)/shard_map/ppermute | solution.py:29
  517.7 13.1 %fusion.93 = f32[2,2048,352]{1,2,0:T(8,128)} fusion(bf16[2,2048,2048]{2,1,0:T(8,128)(2,1)} %get-tuple-element.297, bf16[2,2048,352]{2,1,0:T(8,128)(2,1)S(1)} %copy-done.2), kind=kOutput, calls=%fused_computation.256 | convolution fusion | flops 5905580032 | bytes 25427968 | tf_op jit(solution)/shard_map/esf,esd->efd/dot_general | solution.py:797
  530.8 12.7 %fusion.94 = f32[2,2048,352]{1,2,0:T(8,128)} fusion(bf16[2,2048,2048]{2,1,0:T(8,128)(2,1)} %get-tuple-element.297, bf16[2,2048,352]{2,1,0:T(8,128)(2,1)S(1)} %copy-done.3), kind=kOutput, calls=%fused_computation.257 | convolution fusion | flops 5905580032 | bytes 25427968 | tf_op jit(solution)/shard_map/esf,esd->efd/dot_general | solution.py:797
  543.5 12.9 %fusion.92 = f32[2,352,2048]{2,1,0:T(8,128)} fusion(bf16[2,2048,352]{2,1,0:T(8,128)(2,1)S(1)} %copy-done, bf16[2,2048,2048]{2,1,0:T(8,128)(2,1)} %get-tuple-element.296), kind=kOutput, calls=%fused_computation.255 | convolution fusion | flops 5905580032 | bytes 25427968 | tf_op jit(solution)/shard_map/esf,esd->efd/dot_general | solution.py:797
  556.4 10.8 %collective-permute-done.48 = bf16[512,2176]{1,0:T(8,128)(2,1)} collective-permute-done((bf16[512,2176]{1,0:T(8,128)(2,1)}, bf16[512,2176]{1,0:T(8,128)(2,1)}, u32[]{:S(2)}, u32[]{:S(2)}) %collective-permute-start.48) | collective-permute-done | bytes 2228256 | tf_op jit(solution)/shard_map/ppermute | solution.py:29
  590.6 11.5 %collective-permute-done.57 = bf16[128,2176]{1,0:T(8,128)(2,1)S(1)} collective-permute-done((bf16[128,2176]{1,0:T(8,128)(2,1)S(1)}, bf16[128,2176]{1,0:T(8,128)(2,1)S(1)}, u32[]{:S(2)}, u32[]{:S(2)}) %collective-permute-start.57) | collective-permute-done | bytes 557088 | tf_op jit(solution)/shard_map/ppermute | solution.py:29
  602.1 28.3 %collective-permute-done.56 = bf16[128,2176]{1,0:T(8,128)(2,1)S(1)} collective-permute-done((bf16[128,2176]{1,0:T(8,128)(2,1)S(1)}, bf16[128,2176]{1,0:T(8,128)(2,1)S(1)}, u32[]{:S(2)}, u32[]{:S(2)}) %collective-permute-start.56) | collective-permute-done | bytes 557088 | tf_op jit(solution)/shard_map/ppermute | solution.py:29
  644.7 7.1 convolution_convert_fusion.2
  665.8 7.3 fusion.2
  677.5 20.6 %shard_map.302 = (f32[1,2048]{1,0:T(1,128)}, bf16[512,2048]{1,0:T(8,128)(2,1)}, bf16[512,2048]{1,0:T(8,128)(2,1)}, bf16[512,640]{1,0:T(8,128)(2,1)}, bf16[512,64...) custom-call(s32[2]{0:T(128)} %pad_add_fusion.place, bf16[1024,256]{1,0:T(8,128)(2,1)} %bitcast.73.grad, ...), custom_call_target="tpu_custom_call" | custom-call | flops 1048576 | bytes 65536 | tf_op jit(solution)/shard_map/pallas_call | solution.py:569
  713.6 7.4 collective-permute-done.65
  754.7 7.4 collective-permute-done.60
  764.2 34.4 %collective-permute-done.61 = bf16[128,2048]{1,0:T(8,128)(2,1)} collective-permute-done((bf16[128,2048]{1,0:T(8,128)(2,1)}, bf16[128,2048]{1,0:T(8,128)(2,1)}, u32[]{:S(2)}, u32[]{:S(2)}) %collective-permute-start.61) | collective-permute-done | bytes 524320 | tf_op jit(solution)/shard_map/ppermute | solution.py:29
  804.0 6.6 fusion.86
  817.4 12.3 %collective-permute-done.74 = bf16[256,640]{1,0:T(8,128)(2,1)S(1)} collective-permute-done((bf16[256,640]{1,0:T(8,128)(2,1)S(1)}, bf16[256,640]{1,0:T(8,128)(2,1)S(1)}, u32[]{:S(2)}, u32[]{:S(2)}) %collective-permute-start.74) | collective-permute-done | bytes 327712 | tf_op jit(solution)/shard_map/ppermute | solution.py:29
  855.1 12.4 %collective-permute-done.71 = bf16[128,2048]{1,0:T(8,128)(2,1)} collective-permute-done((bf16[128,2048]{1,0:T(8,128)(2,1)}, bf16[128,2048]{1,0:T(8,128)(2,1)}, u32[]{:S(2)}, u32[]{:S(2)}) %collective-permute-start.71) | collective-permute-done | bytes 524320 | tf_op jit(solution)/shard_map/ppermute | solution.py:29
  872.1 8.2 collective-permute-done.80
  881.6 18.7 %collective-permute-done.81 = bf16[64,2688]{1,0:T(8,128)(2,1)S(1)} collective-permute-done((bf16[64,2688]{1,0:T(8,128)(2,1)S(1)}, bf16[64,2688]{1,0:T(8,128)(2,1)S(1)}, u32[]{:S(2)}, u32[]{:S(2)}) %collective-permute-start.81) | collective-permute-done | bytes 344096 | tf_op jit(solution)/shard_map/ppermute | solution.py:29
  (560 shorter events, 392.7 us)
Async XLA Ops:
  104.9 78.3 %all-to-all-start.1 = ((bf16[32,64,176]{2,1,0:T(8,128)(2,1)}), bf16[32,64,176]{2,1,0:T(8,128)(2,1)}, u32[]{:S(2)}, u32[]{:S(2)}) async-start(bf16[32,64,176]{2,1,0:T(8,128)(2,1)} %maximum_bitcast_fusion), calls=%async_computation.1 | async-start | bytes 2097152 | tf_op jit(solution)/shard_map/all_to_all | solution.py:685
  109.2 57.9 %collective-permute-start.16 = (bf16[128,2176]{1,0:T(8,128)(2,1)}, bf16[128,2176]{1,0:T(8,128)(2,1)}, u32[]{:S(2)}, u32[]{:S(2)}) collective-permute-start(bf16[128,2176]{1,0:T(8,128)(2,1)} %pad_maximum_fusion.4), channel_id=1, source_target_pairs={{0,3},{1,2},{2,1},{3,0},{4,7},{5,6},{6,5},{7,4},{8,11},{9,10},{10,... | collective-permute-start | bytes 1671176 | tf_op jit(solution)/shard_map/ppermute | solution.py:29
  112.9 70.3 %collective-permute-start.15 = (bf16[128,2176]{1,0:T(8,128)(2,1)}, bf16[128,2176]{1,0:T(8,128)(2,1)}, u32[]{:S(2)}, u32[]{:S(2)}) collective-permute-start(bf16[128,2176]{1,0:T(8,128)(2,1)} %pad_maximum_fusion.4), channel_id=1, source_target_pairs={{0,2},{1,3},{2,0},{3,1},{4,6},{5,7},{6,4},{7,5},{8,10},{9,11},{10,... | collective-permute-start | bytes 1671176 | tf_op jit(solution)/shard_map/ppermute | solution.py:29
  112.9 70.3 %collective-permute-start.14 = (bf16[128,2176]{1,0:T(8,128)(2,1)}, bf16[128,2176]{1,0:T(8,128)(2,1)}, u32[]{:S(2)}, u32[]{:S(2)}) collective-permute-start(bf16[128,2176]{1,0:T(8,128)(2,1)} %pad_maximum_fusion.4), channel_id=1, source_target_pairs={{0,1},{1,0},{2,3},{3,2},{4,5},{5,4},{6,7},{7,6},{8,9},{9,8},{10,11... | collective-permute-start | bytes 1671176 | tf_op jit(solution)/shard_map/ppermute | solution.py:29
  129.3 62.0 %collective-permute-start.22 = (bf16[4,64,2048]{2,1,0:T(8,128)(2,1)}, bf16[4,64,2048]{2,1,0:T(8,128)(2,1)}, u32[]{:S(2)}, u32[]{:S(2)}) collective-permute-start(bf16[4,64,2048]{2,1,0:T(8,128)(2,1)} %bitcast_dynamic-update-slice_fusion.24), channel_id=1, source_target_pairs={{0,24},{8,16},{16,8},{24,0},{1,25},{9,17},{17,9},{25,1},{2,26},{10... | collective-permute-start | bytes 3145736 | tf_op jit(solution)/shard_map/ppermute | solution.py:29
  146.2 45.1 %collective-permute-start.21 = (bf16[4,64,2048]{2,1,0:T(8,128)(2,1)}, bf16[4,64,2048]{2,1,0:T(8,128)(2,1)S(1)}, u32[]{:S(2)}, u32[]{:S(2)}) collective-permute-start(bf16[4,64,2048]{2,1,0:T(8,128)(2,1)} %bitcast_dynamic-update-slice_fusion.24), channel_id=1, source_target_pairs={{0,16},{8,24},{16,0},{24,8},{1,17},{9,25},{17,1},{25,9},{2,18},{10... | collective-permute-start | bytes 3145736 | tf_op jit(solution)/shard_map/ppermute | solution.py:29
  212.4 94.1 %collective-permute-start.29 = (bf16[512,2176]{1,0:T(8,128)(2,1)}, bf16[512,2176]{1,0:T(8,128)(2,1)}, u32[]{:S(2)}, u32[]{:S(2)}) collective-permute-start(bf16[512,2176]{1,0:T(8,128)(2,1)} %constant_dynamic-update-slice_fusion.1.cot_a), channel_id=1, source_target_pairs={{0,24},{8,16},{16,8},{24,0},{1,25},{9,17},{17,9},{25,1},{2,26},{10... | collective-permute-start | bytes 6684680 | tf_op jit(solution)/shard_map/ppermute | solution.py:29
  214.6 97.6 %collective-permute-start.28 = (bf16[512,2176]{1,0:T(8,128)(2,1)}, bf16[512,2176]{1,0:T(8,128)(2,1)}, u32[]{:S(2)}, u32[]{:S(2)}) collective-permute-start(bf16[512,2176]{1,0:T(8,128)(2,1)} %constant_dynamic-update-slice_fusion.1.cot_a), channel_id=1, source_target_pairs={{0,16},{8,24},{16,0},{24,8},{1,17},{9,25},{17,1},{25,9},{2,18},{10... | collective-permute-start | bytes 6684680 | tf_op jit(solution)/shard_map/ppermute | solution.py:29
  215.2 97.1 %collective-permute-start.27 = (bf16[512,2176]{1,0:T(8,128)(2,1)}, bf16[512,2176]{1,0:T(8,128)(2,1)}, u32[]{:S(2)}, u32[]{:S(2)}) collective-permute-start(bf16[512,2176]{1,0:T(8,128)(2,1)} %constant_dynamic-update-slice_fusion.1.cot_a), channel_id=1, source_target_pairs={{0,8},{8,0},{16,24},{24,16},{1,9},{9,1},{17,25},{25,17},{2,10},{10... | collective-permute-start | bytes 6684680 | tf_op jit(solution)/shard_map/ppermute | solution.py:29
  242.2 48.1 %collective-permute-start.25 = (bf16[128,2176]{1,0:T(8,128)(2,1)S(1)}, bf16[128,2176]{1,0:T(8,128)(2,1)S(1)}, u32[]{:S(2)}, u32[]{:S(2)}) collective-permute-start(bf16[128,2176]{1,0:T(8,128)(2,1)S(1)} %pad_maximum_fusion.5), channel_id=1, source_target_pairs={{0,2},{1,3},{2,0},{3,1},{4,6},{5,7},{6,4},{7,5},{8,10},{9,11},{10,... | collective-permute-start | bytes 1671176 | tf_op jit(solution)/shard_map/ppermute | solution.py:29
  312.3 51.2 %collective-permute-start.34 = (bf16[512,2176]{1,0:T(8,128)(2,1)}, bf16[512,2176]{1,0:T(8,128)(2,1)}, u32[]{:S(2)}, u32[]{:S(2)}) collective-permute-start(bf16[512,2176]{1,0:T(8,128)(2,1)} %pad_maximum_fusion.1.sec_a), channel_id=1, source_target_pairs={{0,16},{8,24},{16,0},{24,8},{1,17},{9,25},{17,1},{25,9},{2,18},{10... | collective-permute-start | bytes 6684680 | tf_op jit(solution)/shard_map/ppermute | solution.py:29
  313.7 50.8 %collective-permute-start.33 = (bf16[512,2176]{1,0:T(8,128)(2,1)}, bf16[512,2176]{1,0:T(8,128)(2,1)}, u32[]{:S(2)}, u32[]{:S(2)}) collective-permute-start(bf16[512,2176]{1,0:T(8,128)(2,1)} %pad_maximum_fusion.1.sec_a), channel_id=1, source_target_pairs={{0,8},{8,0},{16,24},{24,16},{1,9},{9,1},{17,25},{25,17},{2,10},{10... | collective-permute-start | bytes 6684680 | tf_op jit(solution)/shard_map/ppermute | solution.py:29
  315.5 50.5 %collective-permute-start.36 = (bf16[512,2176]{1,0:T(8,128)(2,1)}, bf16[512,2176]{1,0:T(8,128)(2,1)}, u32[]{:S(2)}, u32[]{:S(2)}) collective-permute-start(bf16[512,2176]{1,0:T(8,128)(2,1)} %collective-permute-done.27.cot_a), channel_id=1, source_target_pairs={{0,4},{4,0},{1,5},{5,1},{2,6},{6,2},{3,7},{7,3},{8,12},{12,8},{9,1... | collective-permute-start | bytes 6684680 | tf_op jit(solution)/shard_map/ppermute | solution.py:29
  364.6 52.1 %collective-permute-start.40 = (bf16[512,2176]{1,0:T(8,128)(2,1)}, bf16[512,2176]{1,0:T(8,128)(2,1)}, u32[]{:S(2)}, u32[]{:S(2)}) collective-permute-start(bf16[512,2176]{1,0:T(8,128)(2,1)} %pad_maximum_fusion.1.sec_a), channel_id=1, source_target_pairs={{0,24},{8,16},{16,8},{24,0},{1,25},{9,17},{17,9},{25,1},{2,26},{10... | collective-permute-start | bytes 6684680 | tf_op jit(solution)/shard_map/ppermute | solution.py:29
  454.3 50.7 %collective-permute-start.39 = (bf16[512,2176]{1,0:T(8,128)(2,1)}, bf16[512,2176]{1,0:T(8,128)(2,1)}, u32[]{:S(2)}, u32[]{:S(2)}) collective-permute-start(bf16[512,2176]{1,0:T(8,128)(2,1)} %add_convert_fusion.2), channel_id=1, source_target_pairs={{0,8},{8,0},{16,24},{24,16},{1,9},{9,1},{17,25},{25,17},{2,10},{10... | collective-permute-start | bytes 6684680 | tf_op jit(solution)/shard_map/ppermute | solution.py:29
  463.7 50.8 %collective-permute-start.44 = (bf16[512,2176]{1,0:T(8,128)(2,1)}, bf16[512,2176]{1,0:T(8,128)(2,1)}, u32[]{:S(2)}, u32[]{:S(2)}) collective-permute-start(bf16[512,2176]{1,0:T(8,128)(2,1)} %add_convert_fusion.1), channel_id=1, source_target_pairs={{0,16},{8,24},{16,0},{24,8},{1,17},{9,25},{17,1},{25,9},{2,18},{10... | collective-permute-start | bytes 6684680 | tf_op jit(solution)/shard_map/ppermute | solution.py:29
  497.1 70.1 %collective-permute-start.54 = (bf16[512,2176]{1,0:T(8,128)(2,1)}, bf16[512,2176]{1,0:T(8,128)(2,1)}, u32[]{:S(2)}, u32[]{:S(2)}) collective-permute-start(bf16[512,2176]{1,0:T(8,128)(2,1)} %get-tuple-element.289), channel_id=1, source_target_pairs={{0,4},{4,0},{1,5},{5,1},{2,6},{6,2},{3,7},{7,3},{8,12},{12,8},{9,1... | collective-permute-start | bytes 6684680 | tf_op jit(solution)/shard_map/ppermute | solution.py:29
  502.1 72.4 %collective-permute-start.50 = (bf16[512,2048]{1,0:T(8,128)(2,1)}, bf16[512,2048]{1,0:T(8,128)(2,1)}, u32[]{:S(2)}, u32[]{:S(2)}) collective-permute-start(bf16[512,2048]{1,0:T(8,128)(2,1)} %get-tuple-element.282), channel_id=1, source_target_pairs={{0,4},{4,0},{1,5},{5,1},{2,6},{6,2},{3,7},{7,3},{8,12},{12,8},{9,1... | collective-permute-start | bytes 6291464 | tf_op jit(solution)/shard_map/ppermute | solution.py:29
  516.3 50.9 %collective-permute-start.48 = (bf16[512,2176]{1,0:T(8,128)(2,1)}, bf16[512,2176]{1,0:T(8,128)(2,1)}, u32[]{:S(2)}, u32[]{:S(2)}) collective-permute-start(bf16[512,2176]{1,0:T(8,128)(2,1)} %add_convert_fusion), channel_id=1, source_target_pairs={{0,24},{8,16},{16,8},{24,0},{1,25},{9,17},{17,9},{25,1},{2,26},{10... | collective-permute-start | bytes 6684680 | tf_op jit(solution)/shard_map/ppermute | solution.py:29
  567.2 63.4 %collective-permute-start.52 = (bf16[512,2048]{1,0:T(8,128)(2,1)S(1)}, bf16[512,2048]{1,0:T(8,128)(2,1)S(1)}, u32[]{:S(2)}, u32[]{:S(2)}) collective-permute-start(bf16[512,2048]{1,0:T(8,128)(2,1)S(1)} %copy-done.80), channel_id=1, source_target_pairs={{0,4},{4,0},{1,5},{5,1},{2,6},{6,2},{3,7},{7,3},{8,12},{12,8},{9,1... | collective-permute-start | bytes 6291464 | tf_op jit(solution)/shard_map/ppermute | solution.py:29
  577.1 55.6 %collective-permute-start.49 = (bf16[512,2048]{1,0:T(8,128)(2,1)S(1)}, bf16[512,2048]{1,0:T(8,128)(2,1)S(1)}, u32[]{:S(2)}, u32[]{:S(2)}) collective-permute-start(bf16[512,2048]{1,0:T(8,128)(2,1)S(1)} %copy-done.25), channel_id=1, source_target_pairs={{0,8},{8,0},{16,24},{24,16},{1,9},{9,1},{17,25},{25,17},{2,10},{10... | collective-permute-start | bytes 6291464 | tf_op jit(solution)/shard_map/ppermute | solution.py:29
  578.0 54.7 %collective-permute-start.51 = (bf16[512,2048]{1,0:T(8,128)(2,1)S(1)}, bf16[512,2048]{1,0:T(8,128)(2,1)S(1)}, u32[]{:S(2)}, u32[]{:S(2)}) collective-permute-start(bf16[512,2048]{1,0:T(8,128)(2,1)S(1)} %add_convert_fusion.4), channel_id=1, source_target_pairs={{0,16},{8,24},{16,0},{24,8},{1,17},{9,25},{17,1},{25,9},{2,18},{10... | collective-permute-start | bytes 6291464 | tf_op jit(solution)/shard_map/ppermute | solution.py:29
  643.1 55.0 %collective-permute-start.53 = (bf16[512,2048]{1,0:T(8,128)(2,1)}, bf16[512,2048]{1,0:T(8,128)(2,1)}, u32[]{:S(2)}, u32[]{:S(2)}) collective-permute-start(bf16[512,2048]{1,0:T(8,128)(2,1)} %add_convert_fusion.3), channel_id=1, source_target_pairs={{0,24},{8,16},{16,8},{24,0},{1,25},{9,17},{17,9},{25,1},{2,26},{10... | collective-permute-start | bytes 6291464 | tf_op jit(solution)/shard_map/ppermute | solution.py:29
  665.3 137.3 %collective-permute-start.32 = (bf16[512,2048]{1,0:T(8,128)(2,1)}, bf16[512,2048]{1,0:T(8,128)(2,1)}, u32[]{:S(2)}, u32[]{:S(2)}) collective-permute-start(bf16[512,2048]{1,0:T(8,128)(2,1)} %get-tuple-element.246), channel_id=1, source_target_pairs={{0,4},{4,0},{1,5},{5,1},{2,6},{6,2},{3,7},{7,3},{8,12},{12,8},{9,1... | collective-permute-start | bytes 6291464 | tf_op jit(solution)/shard_map/ppermute | solution.py:29
  738.2 60.4 %collective-permute-start.61 = (bf16[128,2048]{1,0:T(8,128)(2,1)}, bf16[128,2048]{1,0:T(8,128)(2,1)}, u32[]{:S(2)}, u32[]{:S(2)}) collective-permute-start(bf16[128,2048]{1,0:T(8,128)(2,1)} %get-tuple-element.478), channel_id=1, source_target_pairs={{0,2},{1,3},{2,0},{3,1},{4,6},{5,7},{6,4},{7,5},{8,10},{9,11},{10,... | collective-permute-start | bytes 1572872 | tf_op jit(solution)/shard_map/ppermute | solution.py:29
  745.3 89.8 %all-to-all-start.5 = ((bf16[8,4,64,176]{3,2,1,0:T(8,128)(2,1)}), bf16[8,4,64,176]{3,2,1,0:T(8,128)(2,1)}, u32[]{:S(2)}, u32[]{:S(2)}) async-start(bf16[8,4,64,176]{3,2,1,0:T(8,128)(2,1)} %copy.268), calls=%async_computation.5 | async-start | bytes 2097152 | tf_op jit(solution)/shard_map/all_to_all | solution.py:833
  751.5 60.5 %collective-permute-start.79 = (bf16[8,80,512]{2,1,0:T(8,128)(2,1)S(1)}, bf16[8,80,512]{2,1,0:T(8,128)(2,1)S(1)}, u32[]{:S(2)}, u32[]{:S(2)}) collective-permute-start(bf16[8,80,512]{2,1,0:T(8,128)(2,1)S(1)} %get-tuple-element.486), channel_id=1, source_target_pairs={{0,24},{8,16},{16,8},{24,0},{1,25},{9,17},{17,9},{25,1},{2,26},{10... | collective-permute-start | bytes 1966088 | tf_op jit(solution)/shard_map/ppermute | solution.py:29
  762.1 50.7 %collective-permute-start.78 = (bf16[8,80,512]{2,1,0:T(8,128)(2,1)S(1)}, bf16[8,80,512]{2,1,0:T(8,128)(2,1)S(1)}, u32[]{:S(2)}, u32[]{:S(2)}) collective-permute-start(bf16[8,80,512]{2,1,0:T(8,128)(2,1)S(1)} %get-tuple-element.487), channel_id=1, source_target_pairs={{0,16},{8,24},{16,0},{24,8},{1,17},{9,25},{17,1},{25,9},{2,18},{10... | collective-permute-start | bytes 1966088 | tf_op jit(solution)/shard_map/ppermute | solution.py:29
  762.7 52.7 %collective-permute-start.77 = (bf16[8,80,512]{2,1,0:T(8,128)(2,1)S(1)}, bf16[8,80,512]{2,1,0:T(8,128)(2,1)S(1)}, u32[]{:S(2)}, u32[]{:S(2)}) collective-permute-start(bf16[8,80,512]{2,1,0:T(8,128)(2,1)S(1)} %get-tuple-element.488), channel_id=1, source_target_pairs={{0,8},{8,0},{16,24},{24,16},{1,9},{9,1},{17,25},{25,17},{2,10},{10... | collective-permute-start | bytes 1966088 | tf_op jit(solution)/shard_map/ppermute | solution.py:29
  844.2 67.4 %all-to-all-start.4 = ((bf16[8,80,512]{2,1,0:T(8,128)(2,1)}), bf16[8,80,512]{2,1,0:T(8,128)(2,1)S(1)}, u32[]{:S(2)}, u32[]{:S(2)}) async-start(bf16[8,80,512]{2,1,0:T(8,128)(2,1)} %fusion.8), calls=%async_computation.4 | async-start | bytes 1310720 | tf_op jit(solution)/shard_map/all_to_all | solution.py:912
  848.0 55.2 %collective-permute-start.85 = (bf16[8,64,176]{2,1,0:T(8,128)(2,1)}, bf16[8,64,176]{2,1,0:T(8,128)(2,1)}, u32[]{:S(2)}, u32[]{:S(2)}) collective-permute-start(bf16[8,64,176]{2,1,0:T(8,128)(2,1)} %get-tuple-element.502), channel_id=1, source_target_pairs={{0,24},{8,16},{16,8},{24,0},{1,25},{9,17},{17,9},{25,1},{2,26},{10... | collective-permute-start | bytes 540680 | tf_op jit(solution)/shard_map/ppermute | solution.py:29
  849.6 53.6 %collective-permute-start.84 = (bf16[8,64,176]{2,1,0:T(8,128)(2,1)}, bf16[8,64,176]{2,1,0:T(8,128)(2,1)}, u32[]{:S(2)}, u32[]{:S(2)}) collective-permute-start(bf16[8,64,176]{2,1,0:T(8,128)(2,1)} %get-tuple-element.503), channel_id=1, source_target_pairs={{0,16},{8,24},{16,0},{24,8},{1,17},{9,25},{17,1},{25,9},{2,18},{10... | collective-permute-start | bytes 540680 | tf_op jit(solution)/shard_map/ppermute | solution.py:29
  (143 other events, 2303.7 us)
